TPU v7x, 32 devices: a whole 2x2x4 slice. The times are simulated.
32 devices in a mesh: grp: 2 (over y), space: 4 (over z), snap: 4 (over x, core).
Axes of the slice: x: 2, y: 2, z: 4, core: 2. Of those that a mesh axis runs over, the one named last changes fastest.
Arguments:
- velocity: bfloat16 [32, 3, 8, 96, 128], P(('grp', 'snap'), None, None, 'space'), parts along dimension 0, may hold values from -20 to 20
- row_level: int32 [96], P('space'), may hold values from 0 to 127
- metric_table: float32 [8, 128], replicated, may hold values from 0.5 to 2
Outputs:
- gram: float32 [32, 16], P(('grp', 'snap')), parts along dimension 0
- profile: float32 [32, 96], P(('grp', 'snap'), 'space'), parts along dimension 0
There are 2 independent parts, one for each index of `grp`. A program takes and returns all parts, laid end to end along the dimension named above; an argument that names none is the same for every part. Nothing has to cross between parts.
All inputs are finite; a program needn't handle non-finite values.
Results may differ from a plain program's by a relative error of at most 0.0005.
Values may be sent and summed in bfloat16 or wider, within the bound.
No kernel may reach another device: no remote copies, remote signals or barrier semaphores. Data moves between devices by JAX's collectives and lax.ppermute only.
A program may use at most 128 MiB of HBM per device.

v0:
```python
import jax
import jax.numpy as jnp
from jax import lax
from jax.sharding import PartitionSpec as P


def extended(cells, sides, width):
    for axis, dim in sides:
        count = lax.axis_size(axis)
        ends = count - 1
        head = lax.slice_in_dim(cells, 0, width, axis=dim)
        tail = lax.slice_in_dim(cells, cells.shape[dim] - width, cells.shape[dim], axis=dim)
        cells = jnp.concatenate(
            [
                lax.ppermute(tail, axis, [(i, (i + 1) % count) for i in range(ends)]),
                cells,
                lax.ppermute(head, axis, [((i + 1) % count, i) for i in range(ends)]),
            ],
            axis=dim,
        )
    return cells


def passed_along(array, axis, by):
    length = lax.axis_size(axis)
    return lax.ppermute(array, axis, [(i, (i + by) % length) for i in range(length)])


def derivative(field, axis):
    count = field.shape[axis]
    first = lax.slice_in_dim(field, 1, 2, axis=axis) - lax.slice_in_dim(field, 0, 1, axis=axis)
    inner = (
        lax.slice_in_dim(field, 2, count, axis=axis)
        - lax.slice_in_dim(field, 0, count - 2, axis=axis)
    ) * 0.5
    last = lax.slice_in_dim(field, count - 1, count, axis=axis) - lax.slice_in_dim(
        field, count - 2, count - 1, axis=axis
    )
    return jnp.concatenate([first, inner, last], axis=axis)


def features(padded, metric):
    field = padded.astype(jnp.float32)
    inner = field[:, :, :, 1:-1, :]
    normal_grad = (
        (field[:, :, :, 2:, :] - field[:, :, :, :-2, :]) * 0.5 * metric[None, None, :, :, None]
    )
    stream_grad = derivative(inner, 2)
    span_grad = derivative(inner, 4)
    joined = jnp.concatenate([inner, 0.5 * stream_grad, 0.5 * normal_grad, 0.5 * span_grad], axis=1)
    return joined.astype(jnp.bfloat16)


def weighted_copy(feats, volume):
    return (feats.astype(jnp.float32) * volume[None, None, :, :, None]).astype(jnp.bfloat16)


def block_product(left, right):
    return lax.dot_general(
        left.reshape(left.shape[0], -1),
        right.reshape(right.shape[0], -1),
        (((1,), (1,)), ((), ())),
        preferred_element_type=jnp.float32,
    )


def local(velocity, row_level, metric_table):
    snaps_dev = velocity.shape[0]
    planes = velocity.shape[2]
    rows_dev = velocity.shape[3]
    span_cells = velocity.shape[4]
    space_size = lax.axis_size("space")
    cycle_size = lax.axis_size("snap")
    snap_rank = lax.axis_index("snap")
    rows_all = rows_dev * space_size
    snaps_all = snaps_dev * cycle_size
    row_ids = lax.axis_index("space") * rows_dev + lax.iota(jnp.int32, rows_dev)
    stretch = 0.25 + 2.25 * row_ids.astype(jnp.float32) / (rows_all - 1)
    onehot = (row_level[:, None] == lax.iota(jnp.int32, metric_table.shape[1])[None, :]).astype(
        jnp.float32
    )
    picked = jnp.dot(metric_table, onehot.T, precision=lax.Precision.HIGHEST)
    metric = picked / stretch[None, :]
    volume = stretch[None, :] / picked
    padded = extended(velocity, (("space", 3),), 1)
    own_feats = features(padded, metric)
    own_weighted = weighted_copy(own_feats, volume)
    profile = jnp.sum(
        own_weighted.astype(jnp.float32) * own_feats.astype(jnp.float32), axis=(1, 2, 4)
    ) / (planes * span_cells)
    inverse_count = 1.0 / (planes * rows_all * span_cells)
    zero_index = jnp.int32(0)
    partial_value = jnp.zeros((snaps_dev, snaps_all), jnp.float32)
    partial_value = lax.dynamic_update_slice(
        partial_value, block_product(own_weighted, own_feats), (zero_index, snap_rank * snaps_dev)
    )

    def advance(turn, state):
        piece, partial_value = state
        piece = passed_along(piece, "snap", 1)
        source = (snap_rank - turn) % cycle_size
        partial_value = lax.dynamic_update_slice(
            partial_value, block_product(own_weighted, piece), (zero_index, source * snaps_dev)
        )
        return (piece, partial_value)

    partial_value = lax.fori_loop(1, cycle_size, advance, (own_feats, partial_value))[1]
    gram_rows = lax.psum(partial_value, "space") * inverse_count
    return (gram_rows, profile)


def solution(mesh):
    in_specs = (P(("grp", "snap"), None, None, "space", None), P("space"), P())
    out_specs = (P(("grp", "snap"), None), P(("grp", "snap"), "space"))
    return jax.shard_map(local, mesh=mesh, in_specs=in_specs, out_specs=out_specs, check_vma=False)
```

profile of v0, /device:TPU:0, one launch (start us, length us, event | category | flops | bytes accessed | tf_op | source)
XLA Modules:
  0.0 145.1 jit_solution(383292536808486865)
XLA Ops:
  0.6 0.0 copy-start
  0.6 0.0 copy-start.2
  0.7 1.5 %copy.12 = bf16[4,3,8,24,128]{4,0,3,2,1:T(4,128)(2,1)S(1)} copy(bf16[4,3,8,24,128]{4,3,2,1,0:T(8,128)(2,1)} %param.5) | data formatting | bytes 1179648 | tf_op args[0]
  2.2 4.9 %collective-permute-start.1 = (bf16[4,3,8,1,128]{4,0,3,2,1:T(4,128)(2,1)S(1)}, bf16[4,3,8,1,128]{4,0,3,2,1:T(4,128)(2,1)S(1)}, u32[]{:S(2)}, u32[]{:S(2)}) collective-permute-start(bf16[4,3,8,1,128]{4,0,3,2,1:T(4,128)(2,1)S(1)} %get-tuple-element.154), channel_id=1, source_target_pairs={{0,4},{4,8},{8,12},{1,5},{5,9},{9,13},{2,6},{6,10},{10,14},{3,7},{... | collective-permute-start | bytes 73736 | tf_op jit(solution)/shard_map/ppermute | solution.py:15
  7.2 1.3 collective-permute-start.2
  8.5 0.0 copy-done
  8.5 0.0 copy-done.2
  8.5 0.2 multiply_bitcast_fusion
  8.7 0.0 collective-permute-done.1
  8.7 4.2 %collective-permute-done.2 = bf16[4,3,8,1,128]{4,0,3,2,1:T(4,128)(2,1)S(1)} collective-permute-done((bf16[4,3,8,1,128]{4,0,3,2,1:T(4,128)(2,1)S(1)}, bf16[4,3,8,1,128]{4,0,3,2,1:T(4,128)(2,1)S(1)}, u32[]{:S(2)}, u32[]{:S(2)}) %collective-permute-start.2) | collective-permute-done | bytes 24608 | tf_op jit(solution)/shard_map/ppermute | solution.py:17
  12.9 0.4 maximum_convert_fusion
  13.3 0.1 slice_subtract_fusion.6
  13.4 0.2 fusion.13
  13.6 0.7 fusion.4
  14.3 1.9 %slice_subtract_fusion.2 = (f32[4,3,8,24,1]{4,0,3,2,1:T(4,128)S(1)}, f32[4,3,8,24,1]{4,0,3,2,1:T(4,128)S(1)}) fusion(f32[4,3,8,26,128]{4,0,3,2,1:T(4,128)S(1)} %maximum_convert_fusion), kind=kLoop, calls=%fused_computation.10 | loop fusion | flops 4608 | bytes 55296 | tf_op jit(solution)/shard_map/sub | solution.py:31
  16.2 1.3 fusion.9
  17.5 1.1 fusion.7
  18.6 2.6 %fusion.1 = (f32[4,24]{0,1:T(8,128)S(1)}, bf16[4,12,8,24,128]{4,0,3,2,1:T(4,128)(2,1)S(1)}) fusion(f32[8,24]{1,0:T(8,128)S(1)} %get-tuple-element.157, bf16[4,3,8,24,128]{4,0,3,2,1:T(4,128)(2,1)S(1)} %fusion.9, bf16[4,3,8,24,128]{4,0,3,2,1:T(4,128)(2,1)S(1)} %get-tuple-element.158, bf16[4,3,8,24,128]{4,0,3,2,1:T(4,128)(2,1)S(1)} %get-tuple-element.159, ...), kind=kLoop, calls=%fused_computation.4 | loop fusion | flops 10616736 | bytes 4719744 | tf_op jit(solution)/shard_map/reduce_sum | solution.py:88
  21.2 0.0 copy-start.1
  21.2 3.9 %fusion.10 = f32[4,4]{1,0:T(4,128)S(1)} fusion(bf16[4,12,8,24,128]{4,0,3,2,1:T(4,128)(2,1)S(1)} %get-tuple-element.192, f32[8,24]{1,0:T(8,128)S(1)} %get-tuple-element.157), kind=kOutput, calls=%fused_computation.19 | convolution fusion | flops 12976128 | bytes 2360128 | tf_op jit(solution)/shard_map/dot_general | solution.py:59
  25.1 0.0 copy-done.1
  25.1 2.7 %fusion = bf16[4,12,8,24,128]{4,0,3,2,1:T(4,128)(2,1)} fusion(bf16[4,12,8,24,128]{4,0,3,2,1:T(4,128)(2,1)S(1)} %get-tuple-element.192, f32[8,24]{1,0:T(8,128)S(1)} %get-tuple-element.157), kind=kLoop, calls=%fused_computation.3 | loop fusion | flops 3538944 | bytes 4719360 | tf_op jit(solution)/shard_map/convert_element_type | solution.py:55
  27.8 0.7 copy.13
  28.4 0.1 dynamic_update_slice.13
  28.5 105.9 %while.17 = (s32[]{:T(128)}, bf16[4,12,8,24,128]{4,0,3,2,1:T(4,128)(2,1)}, f32[4,16]{1,0:T(4,128)S(1)}, bf16[4,12,8,24,128]{4,0,3,2,1:T(4,128)(2,1)}, s32[]{:T(1...) while((s32[]{:T(128)}, bf16[4,12,8,24,128]{4,0,3,2,1:T(4,128)(2,1)}, ...), condition=%wide.region_1.2_spmd, body=%wide.region_0.0_spmd.sunk | while | flops 9437202 | bytes 18874864 | solution.py:107
  28.5 0.1 collective-permute-start
  28.6 28.4 %collective-permute-done = bf16[4,12,8,24,128]{4,0,3,2,1:T(4,128)(2,1)S(1)} collective-permute-done((bf16[4,12,8,24,128]{4,0,3,2,1:T(4,128)(2,1)}, bf16[4,12,8,24,128]{4,0,3,2,1:T(4,128)(2,1)S(1)}, u32[]{:S(2)}, u32[]{:S(2)}) %collective-permute-start) | collective-permute-done | bytes 2359328 | tf_op jit(solution)/shard_map/while/body/eval_jaxpr/ppermute | solution.py:26
  57.0 5.2 %convolution_bitcast_fusion.2 = f32[4,4]{1,0:T(4,128)S(1)} fusion(bf16[4,12,8,24,128]{4,0,3,2,1:T(4,128)(2,1)} %get-tuple-element.214, bf16[4,12,8,24,128]{4,0,3,2,1:T(4,128)(2,1)S(1)} %collective-permute-done), kind=kOutput, calls=%fused_computation.clone.1 | convolution fusion | flops 9437184 | bytes 4718656 | tf_op jit(solution)/shard_map/while/body/eval_jaxpr/dot_general | solution.py:59
  62.2 0.2 dynamic_update_slice.15
  62.4 1.4 copy.25
  63.8 0.0 collective-permute-start
  63.8 28.5 %collective-permute-done = bf16[4,12,8,24,128]{4,0,3,2,1:T(4,128)(2,1)S(1)} collective-permute-done((bf16[4,12,8,24,128]{4,0,3,2,1:T(4,128)(2,1)}, bf16[4,12,8,24,128]{4,0,3,2,1:T(4,128)(2,1)S(1)}, u32[]{:S(2)}, u32[]{:S(2)}) %collective-permute-start) | collective-permute-done | bytes 2359328 | tf_op jit(solution)/shard_map/while/body/eval_jaxpr/ppermute | solution.py:26
  92.3 5.2 %convolution_bitcast_fusion.2 = f32[4,4]{1,0:T(4,128)S(1)} fusion(bf16[4,12,8,24,128]{4,0,3,2,1:T(4,128)(2,1)} %get-tuple-element.214, bf16[4,12,8,24,128]{4,0,3,2,1:T(4,128)(2,1)S(1)} %collective-permute-done), kind=kOutput, calls=%fused_computation.clone.1 | convolution fusion | flops 9437184 | bytes 4718656 | tf_op jit(solution)/shard_map/while/body/eval_jaxpr/dot_general | solution.py:59
  97.5 0.2 dynamic_update_slice.15
  97.7 1.4 copy.25
  99.1 0.0 collective-permute-start
  99.1 28.5 %collective-permute-done = bf16[4,12,8,24,128]{4,0,3,2,1:T(4,128)(2,1)S(1)} collective-permute-done((bf16[4,12,8,24,128]{4,0,3,2,1:T(4,128)(2,1)}, bf16[4,12,8,24,128]{4,0,3,2,1:T(4,128)(2,1)S(1)}, u32[]{:S(2)}, u32[]{:S(2)}) %collective-permute-start) | collective-permute-done | bytes 2359328 | tf_op jit(solution)/shard_map/while/body/eval_jaxpr/ppermute | solution.py:26
  127.6 5.2 %convolution_bitcast_fusion.2 = f32[4,4]{1,0:T(4,128)S(1)} fusion(bf16[4,12,8,24,128]{4,0,3,2,1:T(4,128)(2,1)} %get-tuple-element.214, bf16[4,12,8,24,128]{4,0,3,2,1:T(4,128)(2,1)S(1)} %collective-permute-done), kind=kOutput, calls=%fused_computation.clone.1 | convolution fusion | flops 9437184 | bytes 4718656 | tf_op jit(solution)/shard_map/while/body/eval_jaxpr/dot_general | solution.py:59
  132.8 0.2 dynamic_update_slice.15
  133.0 1.4 copy.25
  134.4 10.1 %psum.7 = f32[4,16]{1,0:T(4,128)S(1)} all-reduce(f32[4,16]{1,0:T(4,128)S(1)} %get-tuple-element.135), channel_id=1, replica_groups=mesh['grp'=2,'space'=4,'snap'=4] {'space'}, use_global_device_ids=true, to_apply=%region_2.3 | all-reduce | flops 64 | bytes 512 | tf_op jit(solution)/shard_map/psum | solution.py:108
  144.5 0.6 broadcast_multiply_fusion.1
  (4 shorter events, 0.0 us)
Async XLA Ops:
  0.6 7.8 %copy-start = (f32[8,128]{1,0:T(8,128)S(1)}, f32[8,128]{1,0:T(8,128)}, u32[]{:S(2)}) copy-start(f32[8,128]{1,0:T(8,128)} %param.7) | copy-start | bytes 12292
  0.6 7.8 %copy-start.2 = (s32[24]{0:T(128)S(1)}, s32[24]{0:T(128)}, u32[]{:S(2)}) copy-start(s32[24]{0:T(128)} %param.6) | copy-start | bytes 292
  2.2 6.5 %collective-permute-start.1 = (bf16[4,3,8,1,128]{4,0,3,2,1:T(4,128)(2,1)S(1)}, bf16[4,3,8,1,128]{4,0,3,2,1:T(4,128)(2,1)S(1)}, u32[]{:S(2)}, u32[]{:S(2)}) collective-permute-start(bf16[4,3,8,1,128]{4,0,3,2,1:T(4,128)(2,1)S(1)} %get-tuple-element.154), channel_id=1, source_target_pairs={{0,4},{4,8},{8,12},{1,5},{5,9},{9,13},{2,6},{6,10},{10,14},{3,7},{... | collective-permute-start | bytes 73736 | tf_op jit(solution)/shard_map/ppermute | solution.py:15
  7.2 5.7 %collective-permute-start.2 = (bf16[4,3,8,1,128]{4,0,3,2,1:T(4,128)(2,1)S(1)}, bf16[4,3,8,1,128]{4,0,3,2,1:T(4,128)(2,1)S(1)}, u32[]{:S(2)}, u32[]{:S(2)}) collective-permute-start(bf16[4,3,8,1,128]{4,0,3,2,1:T(4,128)(2,1)S(1)} %get-tuple-element.155), channel_id=1, source_target_pairs={{4,0},{8,4},{12,8},{5,1},{9,5},{13,9},{6,2},{10,6},{14,10},{7,3},{... | collective-permute-start | bytes 73736 | tf_op jit(solution)/shard_map/ppermute | solution.py:17
  21.2 3.9 %copy-start.1 = (bf16[4,12,8,24,128]{4,0,3,2,1:T(4,128)(2,1)}, bf16[4,12,8,24,128]{4,0,3,2,1:T(4,128)(2,1)S(1)}, u32[]{:S(2)}) copy-start(bf16[4,12,8,24,128]{4,0,3,2,1:T(4,128)(2,1)S(1)} %get-tuple-element.192) | copy-start | bytes 7077892
  28.5 28.5 %collective-permute-start = (bf16[4,12,8,24,128]{4,0,3,2,1:T(4,128)(2,1)}, bf16[4,12,8,24,128]{4,0,3,2,1:T(4,128)(2,1)S(1)}, u32[]{:S(2)}, u32[]{:S(2)}) collective-permute-start(bf16[4,12,8,24,128]{4,0,3,2,1:T(4,128)(2,1)} %get-tuple-element.202), channel_id=1, source_target_pairs={{0,1},{1,2},{2,3},{3,0},{4,5},{5,6},{6,7},{7,4},{8,9},{9,10},{10,1... | collective-permute-start | bytes 7077896 | tf_op jit(solution)/shard_map/while/body/eval_jaxpr/ppermute | solution.py:26
  63.8 28.5 %collective-permute-start = (bf16[4,12,8,24,128]{4,0,3,2,1:T(4,128)(2,1)}, bf16[4,12,8,24,128]{4,0,3,2,1:T(4,128)(2,1)S(1)}, u32[]{:S(2)}, u32[]{:S(2)}) collective-permute-start(bf16[4,12,8,24,128]{4,0,3,2,1:T(4,128)(2,1)} %get-tuple-element.202), channel_id=1, source_target_pairs={{0,1},{1,2},{2,3},{3,0},{4,5},{5,6},{6,7},{7,4},{8,9},{9,10},{10,1... | collective-permute-start | bytes 7077896 | tf_op jit(solution)/shard_map/while/body/eval_jaxpr/ppermute | solution.py:26
  99.1 28.5 %collective-permute-start = (bf16[4,12,8,24,128]{4,0,3,2,1:T(4,128)(2,1)}, bf16[4,12,8,24,128]{4,0,3,2,1:T(4,128)(2,1)S(1)}, u32[]{:S(2)}, u32[]{:S(2)}) collective-permute-start(bf16[4,12,8,24,128]{4,0,3,2,1:T(4,128)(2,1)} %get-tuple-element.202), channel_id=1, source_target_pairs={{0,1},{1,2},{2,3},{3,0},{4,5},{5,6},{6,7},{7,4},{8,9},{9,10},{10,1... | collective-permute-start | bytes 7077896 | tf_op jit(solution)/shard_map/while/body/eval_jaxpr/ppermute | solution.py:26
where the time goes:
time: 145 us
  waiting for transfers between devices  89.6 us (62%)
  matrix products  19.6 us (14%)
  other arithmetic  11.5 us (8%)
  blocking collectives  10.1 us (7%)
  local copies, waits for them, and re-layouts  7.16 us (5%)
  starting transfers between devices  6.28 us (4%)
    ppermute x3, waiting for transfers between devices, passed_along(): lax.ppermute(array, axis, [(i, (i + by) % length) for i in range(length)])  85.4 us
    dot_general x4, matrix products, block_product(): lax.dot_general(left.reshape(left.shape[0], -1), right.reshape(right.shap...  19.4 us
    psum x1, blocking collectives, local(): gram_rows = lax.psum(partial_value, 'space') * inverse_count  10.1 us
    ppermute x1, starting transfers between devices, extended(): lax.ppermute(tail, axis, [(i, (i + 1) % count) for i in range(ends)])  4.93 us
    while x3, local copies, waits for them, and re-layouts  4.28 us
    ppermute x1, waiting for transfers between devices, extended(): lax.ppermute(head, axis, [((i + 1) % count, i) for i in range(ends)])  4.18 us
  transfers between devices with their start and end apart: 5, of which 4 were waited for; matrix products, arithmetic and copies ran while one was open for 0% of the time, Pallas kernels for 0%

commit v1 on v0

v1 whole, which is shorter than its diff:
```python
import functools

import jax
import jax.numpy as jnp
import numpy as np
from jax import lax
from jax.experimental import pallas as pl
from jax.experimental.pallas import tpu as pltpu
from jax.sharding import PartitionSpec as P

F32 = jnp.float32
BF16 = jnp.bfloat16
ROWS = 8
VMEM = pl.BlockSpec(memory_space=pltpu.VMEM)
SMEM = pl.BlockSpec(memory_space=pltpu.SMEM)
PARAMS = pltpu.CompilerParams(vmem_limit_bytes=16 * 2**20)


def span_operator(cells):
    diff = np.zeros((cells, cells), np.float32)
    for i in range(cells):
        lo, hi = max(i - 1, 0), min(i + 1, cells - 1)
        scale = 0.5 / (hi - lo)
        diff[i, hi] += scale
        diff[i, lo] -= scale
    return diff.T @ diff


def sublane(shape):
    return lax.broadcasted_iota(jnp.int32, shape, len(shape) - 2)


def lanes(shape):
    return lax.broadcasted_iota(jnp.int32, shape, len(shape) - 1)


def prep_kernel(place_ref, level_ref, table_ref, top_ref, bottom_ref, up_ref, down_ref, metric_ref, volume_ref):
    snaps, comps, planes, _, span = top_ref.shape
    rows = metric_ref.shape[1]
    levels = table_ref.shape[1]
    row = lax.broadcasted_iota(jnp.int32, (rows, levels), 0)
    level = jnp.zeros((rows, levels), jnp.int32)
    for j in range(rows):
        level = jnp.where(row == j, level_ref[j], level)
    chosen = level == lanes((rows, levels))
    row_ids = (place_ref[0] * rows + lax.broadcasted_iota(jnp.int32, (rows, span), 0)).astype(F32)
    stretch = 0.25 + 2.25 * row_ids / (place_ref[1] - 1).astype(F32)
    for p in range(planes):
        picked = jnp.sum(jnp.where(chosen, table_ref[p : p + 1, :], 0.0), axis=1, keepdims=True)
        picked = jnp.broadcast_to(picked, (rows, span))
        metric_ref[p] = picked / stretch
        volume_ref[p] = stretch / picked
    row8 = sublane((ROWS, span))
    for c in range(comps):
        for p in range(planes):
            up = jnp.zeros((ROWS, span), F32)
            down = jnp.zeros((ROWS, span), F32)
            for a in range(snaps):
                mine = row8 // 2 == a
                last = bottom_ref[a, c, p].astype(F32)
                first = top_ref[a, c, p].astype(F32)
                up = jnp.where(mine, pltpu.roll(last, (2 * a + 2) % ROWS, 0), up)
                down = jnp.where(mine, pltpu.roll(first, (2 * a) % ROWS, 0), down)
            up_ref[c * planes + p] = up.astype(BF16)
            down_ref[c * planes + p] = down.astype(BF16)
    count = comps * planes
    for ref, j in ((up_ref, rows - 1), (down_ref, 0)):
        rest = jnp.zeros((ROWS, span), F32)
        for p in range(planes):
            rest = jnp.where(row8 == p, jnp.broadcast_to(metric_ref[p, j : j + 1, :], (ROWS, span)), rest)
        for piece in range(3):
            part = rest.astype(BF16)
            ref[count + piece] = part
            rest = rest - part.astype(F32)


def weigh_kernel(u_ref, metric_ref, volume_ref, below_ref, above_ref, op_ref, w_ref, profile_ref, f_ref, e_ref, prof_ref):
    snaps, comps, planes, rows, span = u_ref.shape
    count = comps * planes
    m_below = sum(below_ref[count + i].astype(F32) for i in range(3)) * 0.0625
    m_above = sum(above_ref[count + i].astype(F32) for i in range(3)) * 0.0625
    first, end = ROWS, ROWS + rows
    for a in range(snaps):
        prof_ref[a] = jnp.zeros((rows, span), F32)

    def field(c, carry):
        for a in range(snaps):
            raw = u_ref[a, c]
            spanned = jnp.dot(raw.reshape(planes * rows, span), op_ref[...], preferred_element_type=F32)
            spanned = spanned.reshape(planes, rows, span)
            u = raw.astype(F32)
            for p in range(planes):
                f_ref[p, first:end, :] = u[p]
                f_ref[p, 0:ROWS, :] = pltpu.roll(below_ref[c * planes + p].astype(F32), (ROWS - 2 - 2 * a) % ROWS, 0)
                f_ref[p, end : end + ROWS, :] = pltpu.roll(above_ref[c * planes + p].astype(F32), (-2 * a) % ROWS, 0)
            stream = [None] * planes
            for i in range(planes):
                lo, hi = max(i - 1, 0), min(i + 1, planes - 1)
                scale = 0.25 / (hi - lo) ** 2
                edge = (volume_ref[i] * scale) * (u[hi] - u[lo])
                stream[hi] = edge if stream[hi] is None else stream[hi] + edge
                stream[lo] = -edge if stream[lo] is None else stream[lo] - edge
            total = prof_ref[a]
            for p in range(planes):
                jump = f_ref[p, first + 1 : end + 1, :] - f_ref[p, first - 1 : end - 1, :]
                edge = (metric_ref[p] * 0.0625) * jump
                e_ref[p, first:end, :] = edge
                e_ref[p, first - 1 : first, :] = m_below[p : p + 1, :] * (
                    f_ref[p, first : first + 1, :] - f_ref[p, first - 2 : first - 1, :]
                )
                e_ref[p, end : end + 1, :] = m_above[p : p + 1, :] * (
                    f_ref[p, end + 1 : end + 2, :] - f_ref[p, end - 1 : end, :]
                )
                partial = volume_ref[p] * (u[p] + spanned[p]) + stream[p]
                total = total + (u[p] * partial + edge * jump)
                normal = e_ref[p, first - 1 : end - 1, :] - e_ref[p, first + 1 : end + 1, :]
                w_ref[a, c, p] = (partial + normal).astype(BF16)
            prof_ref[a] = total
        return carry

    lax.fori_loop(0, comps, field, 0)
    ones = jnp.ones((ROWS, span), F32)
    for a in range(snaps):
        sums = lax.dot_general(
            ones, prof_ref[a], (((1,), (1,)), ((), ())), precision=lax.Precision.HIGHEST, preferred_element_type=F32
        )
        profile_ref[a : a + 1, :] = sums[0:1, :] * (1.0 / (planes * span))


def pair_sums(left_at, right_at, lefts, rights, comps, planes, pairs):
    def step(index, sums):
        c, p = index // planes, index % planes
        left = [left_at(i, c, p).astype(F32) for i in range(lefts)]
        right = [right_at(i, c, p).astype(F32) for i in range(rights)]
        out = list(sums)
        for t in range(0, left[0].shape[0], ROWS):
            for k, (i, j) in enumerate(pairs):
                out[k] = out[k] + left[i][t : t + ROWS] * right[j][t : t + ROWS]
        return tuple(out)

    zero = jnp.zeros((ROWS, 128), F32)
    return lax.fori_loop(0, comps * planes, step, tuple(zero for _ in pairs))


def totals(sums):
    tiles = []
    for start in range(0, len(sums), ROWS):
        tile = jnp.concatenate([jnp.sum(s, axis=0, keepdims=True) for s in sums[start : start + ROWS]], axis=0)
        tiles.append(jnp.broadcast_to(jnp.sum(tile, axis=1, keepdims=True), tile.shape))
    return tiles


def chip_kernel(place_ref, u_ref, w_ref, mate_ref, block_ref):
    snaps, comps, planes, _, span = u_ref.shape
    half = ROWS // snaps
    pairs = [(j, i) for j in range(2 * snaps) for i in range(snaps)]
    pair_list = [(j, i) for j, i in pairs]

    def left(i, c, p):
        return w_ref[i, c, p] if i < snaps else mate_ref[i - snaps, c, p]

    sums = pair_sums(left, lambda i, c, p: u_ref[i, c, p], 2 * snaps, snaps, comps, planes, pair_list)
    tiles = totals(sums)
    lane, row = lanes((ROWS, span)), sublane((ROWS, span))
    block = jnp.zeros((ROWS, span), F32)
    for k, tile in enumerate(tiles):
        j = k * half + row // snaps
        column = jnp.where(j < snaps, place_ref[2] + j, place_ref[3] + j - snaps)
        block = block + jnp.where(lane == column, tile, 0.0)
    fold = block
    for i in range(1, half):
        fold = fold + pltpu.roll(block, i * snaps, 0)
    block_ref[...] = fold


def cross_kernel(chips, place_ref, *refs):
    starts, got = refs[0], refs[1 : chips]
    w_ref, mate_ref, block_ref = refs[chips : chips + 3]
    own_ref, mate_out = refs[chips + 3 : chips + 5]
    back = refs[chips + 5 :]
    snaps, comps, planes, _, span = got[0].shape
    half = ROWS // snaps
    lane, row = lanes((ROWS, span)), sublane((ROWS, span))
    own = block_ref[...]
    mate = jnp.zeros((ROWS, span), F32)
    for k in range(chips - 1):
        start = starts[2 * k]
        column = starts[2 * k + 1]

        def left(i, c, p):
            return w_ref[i, c, start + p] if i < snaps else mate_ref[i - snaps, c, start + p]

        pairs = [(i, j) for i in range(2 * snaps) for j in range(snaps)]
        sums = pair_sums(left, lambda i, c, p: got[k][i, c, p], 2 * snaps, snaps, comps, planes, pairs)
        block = jnp.zeros((ROWS, span), F32)
        for t, tile in enumerate(totals(sums)):
            i = t * half + row // snaps
            to = jnp.where(i < snaps, place_ref[2] + i, place_ref[3] + i - snaps)
            block = block + jnp.where(lane == to, tile, 0.0)
        fold = block
        for i in range(1, half):
            fold = fold + pltpu.roll(block, i * snaps, 0)
        back[k][...] = fold
        flipped = [sums[i * snaps + j] for j in range(snaps) for i in range(2 * snaps)]
        for t, tile in enumerate(totals(flipped)):
            own = own + jnp.where((lane == column + t) & (row < snaps), tile, 0.0)
            mate = mate + jnp.where((lane == column + t) & (row >= snaps), tile, 0.0)
    own_ref[...] = own
    mate_out[...] = pltpu.roll(mate, ROWS - snaps, 0)


def local(velocity, row_level, metric_table):
    snaps, comps, planes, rows, span = velocity.shape
    spaces, cores = lax.axis_size("space"), lax.axis_size("snap")
    chips = cores // 2
    z, s = lax.axis_index("space"), lax.axis_index("snap")
    chip, core = s // 2, s % 2
    mate = s + 1 - 2 * core
    half = planes // 2
    place = jnp.stack([z, jnp.int32(rows * spaces), s * snaps, mate * snaps]).astype(jnp.int32)

    def begin(worker, other):
        return jnp.where(worker < other, 0, half).astype(jnp.int32)

    got = []
    for k in range(1, chips):
        start = begin((chip + k) % chips, chip)
        piece = lax.dynamic_slice_in_dim(velocity, start, half, axis=2)
        got.append(lax.ppermute(piece, "snap", [(i, (i + 2 * k) % cores) for i in range(cores)]))

    up, down, metric, volume = pl.pallas_call(
        prep_kernel,
        name="prep",
        grid=(1,),
        out_shape=[
            jax.ShapeDtypeStruct((comps * planes + 3, ROWS, span), BF16),
            jax.ShapeDtypeStruct((comps * planes + 3, ROWS, span), BF16),
            jax.ShapeDtypeStruct((planes, rows, span), F32),
            jax.ShapeDtypeStruct((planes, rows, span), F32),
        ],
        in_specs=[
            SMEM,
            SMEM,
            VMEM,
            pl.BlockSpec((snaps, comps, planes, ROWS, span), lambda i: (0, 0, 0, 0, 0)),
            pl.BlockSpec((snaps, comps, planes, ROWS, span), lambda i: (0, 0, 0, rows // ROWS - 1, 0)),
        ],
        out_specs=[VMEM] * 4,
        compiler_params=PARAMS,
    )(place, row_level, metric_table, velocity, velocity)
    below = lax.ppermute(up, "space", [(i, i + 1) for i in range(spaces - 1)])
    above = lax.ppermute(down, "space", [(i + 1, i) for i in range(spaces - 1)])

    operator = jnp.asarray(span_operator(span), BF16)
    w, profile = pl.pallas_call(
        weigh_kernel,
        name="weigh",
        out_shape=[
            jax.ShapeDtypeStruct(velocity.shape, BF16),
            jax.ShapeDtypeStruct((snaps, rows), F32),
        ],
        in_specs=[VMEM] * 6,
        out_specs=[VMEM] * 2,
        scratch_shapes=[
            pltpu.VMEM((planes, rows + 2 * ROWS, span), F32),
            pltpu.VMEM((planes, rows + 2 * ROWS, span), F32),
            pltpu.VMEM((snaps, rows, span), F32),
        ],
        compiler_params=PARAMS,
    )(velocity, metric, volume, below, above, operator)
    w_mate = lax.ppermute(w, "snap", [(i, i ^ 1) for i in range(cores)])
    tile = jax.ShapeDtypeStruct((ROWS, span), F32)
    block = pl.pallas_call(
        chip_kernel,
        name="chip",
        out_shape=tile,
        in_specs=[SMEM] + [VMEM] * 3,
        out_specs=VMEM,
        compiler_params=PARAMS,
    )(place, velocity, w, w_mate)

    starts = []
    for k in range(1, chips):
        source = (chip - k) % chips
        starts += [begin(chip, source), (2 * source + core) * snaps]
    own, for_mate, *back = pl.pallas_call(
        functools.partial(cross_kernel, chips),
        name="cross",
        out_shape=[tile] * (chips + 1),
        in_specs=[SMEM, SMEM] + [VMEM] * (chips + 2),
        out_specs=[VMEM] * (chips + 1),
        compiler_params=PARAMS,
    )(place, jnp.stack(starts).astype(jnp.int32), *got, w, w_mate, block)
    total = own
    for k in range(1, chips):
        total = total + lax.ppermute(back[k - 1], "snap", [(i, (i - 2 * k) % cores) for i in range(cores)])
    total = total + lax.ppermute(for_mate, "snap", [(i, i ^ 1) for i in range(cores)])
    gram = total
    for k in range(1, spaces):
        gram = gram + lax.ppermute(total, "space", [(i, (i + k) % spaces) for i in range(spaces)])
    gram = gram[:snaps, : snaps * cores] * (1.0 / (planes * rows * spaces * span))
    return gram, profile


def solution(mesh):
    in_specs = (P(("grp", "snap"), None, None, "space", None), P("space"), P())
    out_specs = (P(("grp", "snap"), None), P(("grp", "snap"), "space"))
    return jax.shard_map(local, mesh=mesh, in_specs=in_specs, out_specs=out_specs, check_vma=False)
```

time: 145 us -> 40 us (0.28)
  waiting for transfers between devices: 89.6 us -> 16.7 us
  matrix products: 19.6 us -> 0 us
  other arithmetic: 11.5 us -> 0.75 us
  blocking collectives: 10.1 us -> 0 us
  starting transfers between devices: 6.28 us -> 14 us
  Pallas kernels: 0 us -> 5.92 us
  local copies, waits for them, and re-layouts: 7.16 us -> 1.7 us
    ppermute x5 -> x9, waiting for transfers between devices: 89.6 us -> 16.7 us  [the longest x1 5.71 us: local(): lax.ppermute(piece, 'snap', [(i, (i + 2 * k) % cores) for i in range(core...]
    dot_general x5 -> x0, matrix products: 19.6 us -> none  [the longest x4 19.4 us: block_product(): lax.dot_general(left.reshape(left.shape[0], -1), right.reshape(right.shap...]
    psum x1 -> x0, blocking collectives: 10.1 us -> none  [local(): gram_rows = lax.psum(partial_value, 'space') * inverse_count]
    ppermute x5 -> x9, starting transfers between devices: 6.28 us -> 14 us  [the longest x1 4.93 us: local(): below = lax.ppermute(up, 'space', [(i, i + 1) for i in range(spaces - 1)])]
    pallas_call x0 -> x4, Pallas kernels: none -> 5.92 us  [the longest x1 2.14 us: local(): pl.pallas_call(weigh_kernel, name='weigh', out_shape=[jax.ShapeDtypeStruc...]
    while x3 -> x0, local copies, waits for them, and re-layouts: 4.28 us -> none
    convert_element_type x2 -> x0, other arithmetic: 3.1 us -> none  [the longest x1 2.68 us: weighted_copy(): (feats.astype(jnp.float32) * volume[None, None, :, :, None]).astype(jnp.b...]
    reduce_sum x1 -> x0, other arithmetic: 2.56 us -> none  [local(): jnp.sum(own_weighted.astype(jnp.float32) * own_feats.astype(jnp.float32),...]
  transfers between devices with their start and end apart: 5 -> 9, of which waited for: 4 -> 7; matrix products, arithmetic and copies ran while one was open for 0% -> 0% of each run, Pallas kernels for 0% -> 5%
where the time goes in v1:
time: 40 us; the launch traced here: 39.8 us
  waiting for transfers between devices  16.7 us (42%)
  starting transfers between devices  14 us (35%)
  Pallas kernels  5.92 us (15%)
  local copies, waits for them, and re-layouts  1.7 us (4%)
  other arithmetic  0.75 us (2%)
  between operations  0.71 us (2%)
    ppermute x1, waiting for transfers between devices, local(): lax.ppermute(piece, 'snap', [(i, (i + 2 * k) % cores) for i in range(core...  5.71 us
    ppermute x1, starting transfers between devices, local(): below = lax.ppermute(up, 'space', [(i, i + 1) for i in range(spaces - 1)])  4.93 us
    ppermute x3, starting transfers between devices, local(): lax.ppermute(total, 'space', [(i, (i + k) % spaces) for i in range(spaces)])  4.62 us
    ppermute x1, waiting for transfers between devices, local(): above = lax.ppermute(down, 'space', [(i + 1, i) for i in range(spaces - 1)])  4.26 us
    ppermute x3, waiting for transfers between devices, local(): lax.ppermute(total, 'space', [(i, (i + k) % spaces) for i in range(spaces)])  3.83 us
    pallas_call x1, Pallas kernels, local(): pl.pallas_call(weigh_kernel, name='weigh', out_shape=[jax.ShapeDtypeStruc...  2.14 us
    ppermute x1, waiting for transfers between devices, local(): lax.ppermute(back[k - 1], 'snap', [(i, (i - 2 * k) % cores) for i in rang...  2.11 us
    pallas_call x1, Pallas kernels, local(): pl.pallas_call(chip_kernel, name='chip', out_shape=tile, in_specs=[SMEM]...  1.81 us
  transfers between devices with their start and end apart: 9, of which 7 were waited for; matrix products, arithmetic and copies ran while one was open for 0% of the time, Pallas kernels for 5%

profile of v1, /device:TPU:0, one launch (start us, length us, event | category | flops | bytes accessed | tf_op | source)
XLA Modules:
  0.0 39.8 jit_solution(17810909809422674808)
XLA Ops:
  0.6 0.0 copy-start.3
  0.7 0.0 copy-start.4
  0.7 0.1 pad_add_fusion.place_ref
  0.7 0.6 %copy-done.3 = f32[8,128]{1,0:T(8,128)S(1)} copy-done((f32[8,128]{1,0:T(8,128)S(1)}, f32[8,128]{1,0:T(8,128)}, u32[]{:S(2)}) %copy-start.3) | copy-done | bytes 4120
  1.3 0.0 copy-done.4
  1.3 0.0 copy-start
  1.3 1.1 %copy-done = bf16[4,3,8,24,128]{4,3,2,1,0:T(8,128)(2,1)S(1)} copy-done((bf16[4,3,8,24,128]{4,3,2,1,0:T(8,128)(2,1)S(1)}, bf16[4,3,8,24,128]{4,3,2,1,0:T(8,128)(2,1)}, u32[]{:S(2)}) %copy-start) | copy-done | bytes 589848
  2.4 0.0 copy-start.1
  2.4 0.0 copy-start.2
  2.4 0.7 %prep.1 = (bf16[27,8,128]{2,1,0:T(8,128)(2,1)S(1)}, bf16[27,8,128]{2,1,0:T(8,128)(2,1)S(1)}, f32[8,24,128]{2,1,0:T(8,128)S(1)}, f32[8,24,128]{2,1,0:T(8,128)S(1)}) custom-call(s32[4]{0:T(128)S(1)} %pad_add_fusion.place_ref, s32[24]{0:T(128)S(1)} %copy-done.4, f32[8,128]{1,0:T(8,128)S(1)} %copy-done.3, bf16[4,3,8,24,128]{4,3,2,1,0:T(8,128)(2,1)S(1)} %copy-done, ...), custom_call_target="tpu_custom_call" | custom-call | tf_op jit(solution)/shard_map/prep/pallas_call | solution.py:231
  3.2 4.9 %collective-permute-start.1 = (bf16[27,8,128]{2,1,0:T(8,128)(2,1)S(1)}, bf16[27,8,128]{2,1,0:T(8,128)(2,1)S(1)}, u32[]{:S(2)}, u32[]{:S(2)}) collective-permute-start(bf16[27,8,128]{2,1,0:T(8,128)(2,1)S(1)} %get-tuple-element.13), channel_id=1, source_target_pairs={{0,4},{4,8},{8,12},{1,5},{5,9},{9,13},{2,6},{6,10},{10,14},{3,7},{... | collective-permute-start | bytes 165896 | tf_op jit(solution)/shard_map/ppermute | solution.py:251
  8.1 1.3 %collective-permute-start.2 = (bf16[27,8,128]{2,1,0:T(8,128)(2,1)S(1)}, bf16[27,8,128]{2,1,0:T(8,128)(2,1)S(1)}, u32[]{:S(2)}, u32[]{:S(2)}) collective-permute-start(bf16[27,8,128]{2,1,0:T(8,128)(2,1)S(1)} %get-tuple-element.14), channel_id=1, source_target_pairs={{4,0},{8,4},{12,8},{5,1},{9,5},{13,9},{6,2},{10,6},{14,10},{7,3},{... | collective-permute-start | bytes 165896 | tf_op jit(solution)/shard_map/ppermute | solution.py:252
  9.4 0.5 %collective-permute-done.1.below_ref = bf16[27,8,128]{2,1,0:T(8,128)(2,1)S(1)} collective-permute-done((bf16[27,8,128]{2,1,0:T(8,128)(2,1)S(1)}, bf16[27,8,128]{2,1,0:T(8,128)(2,1)S(1)}, u32[]{:S(2)}, u32[]{:S(2)}) %collective-permute-start.1) | collective-permute-done | bytes 55328 | tf_op jit(solution)/shard_map/ppermute | solution.py:251
  9.9 4.3 %collective-permute-done.2.above_ref = bf16[27,8,128]{2,1,0:T(8,128)(2,1)S(1)} collective-permute-done((bf16[27,8,128]{2,1,0:T(8,128)(2,1)S(1)}, bf16[27,8,128]{2,1,0:T(8,128)(2,1)S(1)}, u32[]{:S(2)}, u32[]{:S(2)}) %collective-permute-start.2) | collective-permute-done | bytes 55328 | tf_op jit(solution)/shard_map/ppermute | solution.py:252
  14.1 0.0 copy-done.1
  14.1 0.0 copy-done.2
  14.1 2.1 %weigh.1 = (bf16[4,3,8,24,128]{4,3,2,1,0:T(8,128)(2,1)S(1)}, f32[4,24]{1,0:T(4,128)}) custom-call(bf16[4,3,8,24,128]{4,3,2,1,0:T(8,128)(2,1)S(1)} %copy-done.1, f32[8,24,128]{2,1,0:T(8,128)S(1)} %get-tuple-element.11.metric_ref, f32[8,24,128]{2,1,0:T(8,128)S(1)} %get-tuple-element.12.volume_ref, bf16[27,8,128]{2,1,0:T(8,128)(2,1)S(1)} %collective-permute-done.1.below_ref, ...), custom_call_target="tpu_custom_call" | custom-call | tf_op jit(solution)/shard_map/weigh/pallas_call | solution.py:255
  16.3 0.0 collective-permute-start.3
  16.3 1.6 %collective-permute-start = (bf16[4,3,4,24,128]{4,3,2,1,0:T(8,128)(2,1)S(1)}, bf16[4,3,4,24,128]{4,3,2,1,0:T(8,128)(2,1)S(1)}, u32[]{:S(2)}, u32[]{:S(2)}) collective-permute-start(bf16[4,3,4,24,128]{4,3,2,1,0:T(8,128)(2,1)S(1)} %constant_dynamic-slice_fusion), channel_id=1, source_target_pairs={{0,2},{1,3},{2,0},{3,1},{4,6},{5,7},{6,4},{7,5},{8,10},{9,11},{10,... | collective-permute-start | bytes 884744 | tf_op jit(solution)/shard_map/ppermute | solution.py:229
  17.9 0.1 pad_add_fusion.1.refs_0_
  18.0 0.3 collective-permute-done.3.mate_ref.refs_3_
  18.3 1.8 %chip.1.refs_4_ = f32[8,128]{1,0:T(8,128)S(1)} custom-call(s32[4]{0:T(128)S(1)} %pad_add_fusion.place_ref, bf16[4,3,8,24,128]{4,3,2,1,0:T(8,128)(2,1)S(1)} %copy-done.1, bf16[4,3,8,24,128]{4,3,2,1,0:T(8,128)(2,1)S(1)} %get-tuple-element.15.w_ref.refs_2_, bf16[4,3,8,24,128]{4,3,2,1,0:T(8,128)(2,1)S(1)} %collective-permute-done.3.mate_ref.refs_3_), custom_call_target="tpu_custom_call" | custom-call | tf_op jit(solution)/shard_map/chip/pallas_call | solution.py:273
  20.1 5.7 %collective-permute-done.refs_1_ = bf16[4,3,4,24,128]{4,3,2,1,0:T(8,128)(2,1)S(1)} collective-permute-done((bf16[4,3,4,24,128]{4,3,2,1,0:T(8,128)(2,1)S(1)}, bf16[4,3,4,24,128]{4,3,2,1,0:T(8,128)(2,1)S(1)}, u32[]{:S(2)}, u32[]{:S(2)}) %collective-permute-start) | collective-permute-done | bytes 294944 | tf_op jit(solution)/shard_map/ppermute | solution.py:229
  25.8 1.2 %cross.1 = (f32[8,128]{1,0:T(8,128)S(1)}, f32[8,128]{1,0:T(8,128)S(1)}, f32[8,128]{1,0:T(8,128)S(1)}) custom-call(s32[4]{0:T(128)S(1)} %pad_add_fusion.place_ref, s32[2]{0:T(128)S(1)} %pad_add_fusion.1.refs_0_, bf16[4,3,4,24,128]{4,3,2,1,0:T(8,128)(2,1)S(1)} %collective-permute-done.refs_1_, bf16[4,3,8,24,128]{4,3,2,1,0:T(8,128)(2,1)S(1)} %get-tuple-element.15.w_ref.refs_2_, ...), custom_call_target="tpu_custom_call" | custom-call | tf_op jit(solution)/shard_map/cross/pallas_call | solution.py:286
  27.0 1.6 %collective-permute-start.4 = (f32[8,128]{1,0:T(8,128)S(1)}, f32[8,128]{1,0:T(8,128)S(1)}, u32[]{:S(2)}, u32[]{:S(2)}) collective-permute-start(f32[8,128]{1,0:T(8,128)S(1)} %get-tuple-element.17), channel_id=1, source_target_pairs={{0,2},{1,3},{2,0},{3,1},{4,6},{5,7},{6,4},{7,5},{8,10},{9,11},{10,... | collective-permute-start | bytes 12296 | tf_op jit(solution)/shard_map/ppermute | solution.py:296
  28.6 0.0 collective-permute-start.5
  28.6 2.1 %collective-permute-done.4 = f32[8,128]{1,0:T(8,128)S(1)} collective-permute-done((f32[8,128]{1,0:T(8,128)S(1)}, f32[8,128]{1,0:T(8,128)S(1)}, u32[]{:S(2)}, u32[]{:S(2)}) %collective-permute-start.4) | collective-permute-done | bytes 4128 | tf_op jit(solution)/shard_map/ppermute | solution.py:296
  30.7 0.0 collective-permute-done.5
  30.7 1.7 %collective-permute-start.8 = (f32[8,128]{1,0:T(8,128)S(1)}, f32[8,128]{1,0:T(8,128)S(1)}, u32[]{:S(2)}, u32[]{:S(2)}) collective-permute-start(f32[8,128]{1,0:T(8,128)S(1)} %add_add_fusion.1), channel_id=1, source_target_pairs={{0,12},{4,0},{8,4},{12,8},{1,13},{5,1},{9,5},{13,9},{2,14},{6,2},{... | collective-permute-start | bytes 12296 | tf_op jit(solution)/shard_map/ppermute | solution.py:300
  32.4 1.3 %collective-permute-start.7 = (f32[8,128]{1,0:T(8,128)S(1)}, f32[8,128]{1,0:T(8,128)S(1)}, u32[]{:S(2)}, u32[]{:S(2)}) collective-permute-start(f32[8,128]{1,0:T(8,128)S(1)} %add_add_fusion.1), channel_id=1, source_target_pairs={{0,8},{4,12},{8,0},{12,4},{1,9},{5,13},{9,1},{13,5},{2,10},{6,14},... | collective-permute-start | bytes 12296 | tf_op jit(solution)/shard_map/ppermute | solution.py:300
  33.8 1.6 %collective-permute-start.6 = (f32[8,128]{1,0:T(8,128)S(1)}, f32[8,128]{1,0:T(8,128)S(1)}, u32[]{:S(2)}, u32[]{:S(2)}) collective-permute-start(f32[8,128]{1,0:T(8,128)S(1)} %add_add_fusion.1), channel_id=1, source_target_pairs={{0,4},{4,8},{8,12},{12,0},{1,5},{5,9},{9,13},{13,1},{2,6},{6,10},{... | collective-permute-start | bytes 12296 | tf_op jit(solution)/shard_map/ppermute | solution.py:300
  35.3 0.0 collective-permute-done.8
  35.3 1.6 %collective-permute-done.7 = f32[8,128]{1,0:T(8,128)S(1)} collective-permute-done((f32[8,128]{1,0:T(8,128)S(1)}, f32[8,128]{1,0:T(8,128)S(1)}, u32[]{:S(2)}, u32[]{:S(2)}) %collective-permute-start.7) | collective-permute-done | bytes 4128 | tf_op jit(solution)/shard_map/ppermute | solution.py:300
  36.9 2.2 %collective-permute-done.6 = f32[8,128]{1,0:T(8,128)S(1)} collective-permute-done((f32[8,128]{1,0:T(8,128)S(1)}, f32[8,128]{1,0:T(8,128)S(1)}, u32[]{:S(2)}, u32[]{:S(2)}) %collective-permute-start.6) | collective-permute-done | bytes 4128 | tf_op jit(solution)/shard_map/ppermute | solution.py:300
  39.2 0.6 %slice_multiply_fusion = f32[4,16]{1,0:T(4,128)} fusion(f32[8,128]{1,0:T(8,128)S(1)} %add_add_fusion), kind=kLoop, calls=%fused_computation.2 | loop fusion | flops 64 | bytes 512 | tf_op jit(solution)/shard_map/mul | solution.py:301
  (3 shorter events, 0.0 us)
Async XLA Ops:
  0.6 0.7 %copy-start.3 = (f32[8,128]{1,0:T(8,128)S(1)}, f32[8,128]{1,0:T(8,128)}, u32[]{:S(2)}) copy-start(f32[8,128]{1,0:T(8,128)} %table_ref.1) | copy-start | bytes 12292
  0.7 0.7 %copy-start.4 = (s32[24]{0:T(128)S(1)}, s32[24]{0:T(128)}, u32[]{:S(2)}) copy-start(s32[24]{0:T(128)} %level_ref.1) | copy-start | bytes 292
  1.3 1.1 %copy-start = (bf16[4,3,8,24,128]{4,3,2,1,0:T(8,128)(2,1)S(1)}, bf16[4,3,8,24,128]{4,3,2,1,0:T(8,128)(2,1)}, u32[]{:S(2)}) copy-start(bf16[4,3,8,24,128]{4,3,2,1,0:T(8,128)(2,1)} %u_ref.3) | copy-start | bytes 1769476
  2.4 11.7 %copy-start.1 = (bf16[4,3,8,24,128]{4,3,2,1,0:T(8,128)(2,1)S(1)}, bf16[4,3,8,24,128]{4,3,2,1,0:T(8,128)(2,1)}, u32[]{:S(2)}) copy-start(bf16[4,3,8,24,128]{4,3,2,1,0:T(8,128)(2,1)} %u_ref.3) | copy-start | bytes 1769476
  2.4 11.7 %copy-start.2 = (bf16[128,128]{1,0:T(8,128)(2,1)S(1)}, bf16[128,128]{1,0:T(8,128)(2,1)}, u32[]{:S(2)}) copy-start(bf16[128,128]{1,0:T(8,128)(2,1)} %constant.52.clone.op_ref) | copy-start | bytes 98308
  3.2 6.7 %collective-permute-start.1 = (bf16[27,8,128]{2,1,0:T(8,128)(2,1)S(1)}, bf16[27,8,128]{2,1,0:T(8,128)(2,1)S(1)}, u32[]{:S(2)}, u32[]{:S(2)}) collective-permute-start(bf16[27,8,128]{2,1,0:T(8,128)(2,1)S(1)} %get-tuple-element.13), channel_id=1, source_target_pairs={{0,4},{4,8},{8,12},{1,5},{5,9},{9,13},{2,6},{6,10},{10,14},{3,7},{... | collective-permute-start | bytes 165896 | tf_op jit(solution)/shard_map/ppermute | solution.py:251
  8.1 6.0 %collective-permute-start.2 = (bf16[27,8,128]{2,1,0:T(8,128)(2,1)S(1)}, bf16[27,8,128]{2,1,0:T(8,128)(2,1)S(1)}, u32[]{:S(2)}, u32[]{:S(2)}) collective-permute-start(bf16[27,8,128]{2,1,0:T(8,128)(2,1)S(1)} %get-tuple-element.14), channel_id=1, source_target_pairs={{4,0},{8,4},{12,8},{5,1},{9,5},{13,9},{6,2},{10,6},{14,10},{7,3},{... | collective-permute-start | bytes 165896 | tf_op jit(solution)/shard_map/ppermute | solution.py:252
  16.3 2.0 %collective-permute-start.3 = (bf16[4,3,8,24,128]{4,3,2,1,0:T(8,128)(2,1)S(1)}, bf16[4,3,8,24,128]{4,3,2,1,0:T(8,128)(2,1)S(1)}, u32[]{:S(2)}, u32[]{:S(2)}) collective-permute-start(bf16[4,3,8,24,128]{4,3,2,1,0:T(8,128)(2,1)S(1)} %get-tuple-element.15.w_ref.refs_2_), channel_id=1, source_target_pairs={{0,1},{1,0},{2,3},{3,2},{4,5},{5,4},{6,7},{7,6},{8,9},{9,8},{10,11... | collective-permute-start | bytes 1769480 | tf_op jit(solution)/shard_map/ppermute | solution.py:271
  16.3 9.5 %collective-permute-start = (bf16[4,3,4,24,128]{4,3,2,1,0:T(8,128)(2,1)S(1)}, bf16[4,3,4,24,128]{4,3,2,1,0:T(8,128)(2,1)S(1)}, u32[]{:S(2)}, u32[]{:S(2)}) collective-permute-start(bf16[4,3,4,24,128]{4,3,2,1,0:T(8,128)(2,1)S(1)} %constant_dynamic-slice_fusion), channel_id=1, source_target_pairs={{0,2},{1,3},{2,0},{3,1},{4,6},{5,7},{6,4},{7,5},{8,10},{9,11},{10,... | collective-permute-start | bytes 884744 | tf_op jit(solution)/shard_map/ppermute | solution.py:229
  27.0 3.7 %collective-permute-start.4 = (f32[8,128]{1,0:T(8,128)S(1)}, f32[8,128]{1,0:T(8,128)S(1)}, u32[]{:S(2)}, u32[]{:S(2)}) collective-permute-start(f32[8,128]{1,0:T(8,128)S(1)} %get-tuple-element.17), channel_id=1, source_target_pairs={{0,2},{1,3},{2,0},{3,1},{4,6},{5,7},{6,4},{7,5},{8,10},{9,11},{10,... | collective-permute-start | bytes 12296 | tf_op jit(solution)/shard_map/ppermute | solution.py:296
  28.6 2.1 %collective-permute-start.5 = (f32[8,128]{1,0:T(8,128)S(1)}, f32[8,128]{1,0:T(8,128)S(1)}, u32[]{:S(2)}, u32[]{:S(2)}) collective-permute-start(f32[8,128]{1,0:T(8,128)S(1)} %get-tuple-element.18), channel_id=1, source_target_pairs={{0,1},{1,0},{2,3},{3,2},{4,5},{5,4},{6,7},{7,6},{8,9},{9,8},{10,11... | collective-permute-start | bytes 12296 | tf_op jit(solution)/shard_map/ppermute | solution.py:297
  30.7 4.6 %collective-permute-start.8 = (f32[8,128]{1,0:T(8,128)S(1)}, f32[8,128]{1,0:T(8,128)S(1)}, u32[]{:S(2)}, u32[]{:S(2)}) collective-permute-start(f32[8,128]{1,0:T(8,128)S(1)} %add_add_fusion.1), channel_id=1, source_target_pairs={{0,12},{4,0},{8,4},{12,8},{1,13},{5,1},{9,5},{13,9},{2,14},{6,2},{... | collective-permute-start | bytes 12296 | tf_op jit(solution)/shard_map/ppermute | solution.py:300
  32.4 4.5 %collective-permute-start.7 = (f32[8,128]{1,0:T(8,128)S(1)}, f32[8,128]{1,0:T(8,128)S(1)}, u32[]{:S(2)}, u32[]{:S(2)}) collective-permute-start(f32[8,128]{1,0:T(8,128)S(1)} %add_add_fusion.1), channel_id=1, source_target_pairs={{0,8},{4,12},{8,0},{12,4},{1,9},{5,13},{9,1},{13,5},{2,10},{6,14},... | collective-permute-start | bytes 12296 | tf_op jit(solution)/shard_map/ppermute | solution.py:300
  33.8 5.4 %collective-permute-start.6 = (f32[8,128]{1,0:T(8,128)S(1)}, f32[8,128]{1,0:T(8,128)S(1)}, u32[]{:S(2)}, u32[]{:S(2)}) collective-permute-start(f32[8,128]{1,0:T(8,128)S(1)} %add_add_fusion.1), channel_id=1, source_target_pairs={{0,4},{4,8},{8,12},{12,0},{1,5},{5,9},{9,13},{13,1},{2,6},{6,10},{... | collective-permute-start | bytes 12296 | tf_op jit(solution)/shard_map/ppermute | solution.py:300

commit v2 on v0

v2 whole, which is shorter than its diff:
```python
import functools

import jax
import jax.numpy as jnp
import numpy as np
from jax import lax
from jax.experimental import pallas as pl
from jax.experimental.pallas import tpu as pltpu
from jax.sharding import PartitionSpec as P

F32 = jnp.float32
BF16 = jnp.bfloat16
ROWS = 8
VMEM = pl.BlockSpec(memory_space=pltpu.VMEM)
SMEM = pl.BlockSpec(memory_space=pltpu.SMEM)


def call(kernel, name, out_shape, in_specs, scratch_shapes=()):
    single = not isinstance(out_shape, list)
    return pl.pallas_call(
        kernel,
        name=name,
        out_shape=out_shape,
        in_specs=in_specs,
        out_specs=VMEM if single else [VMEM] * len(out_shape),
        scratch_shapes=list(scratch_shapes),
        compiler_params=pltpu.CompilerParams(vmem_limit_bytes=16 * 2**20),
        cost_estimate=pl.CostEstimate(flops=1000, bytes_accessed=1000, transcendentals=0),
    )


def span_operator(cells):
    diff = np.zeros((cells, cells), np.float32)
    for i in range(cells):
        lo, hi = max(i - 1, 0), min(i + 1, cells - 1)
        scale = 0.5 / (hi - lo)
        diff[i, hi] += scale
        diff[i, lo] -= scale
    return diff.T @ diff


def sublane(shape):
    return lax.broadcasted_iota(jnp.int32, shape, len(shape) - 2)


def lanes(shape):
    return lax.broadcasted_iota(jnp.int32, shape, len(shape) - 1)


def pack_kernel(u_ref, metric_ref, up_ref, down_ref):
    snaps, comps, planes, rows, span = u_ref.shape
    count = comps * planes
    row8 = sublane((ROWS, span))
    for ref, j in ((up_ref, rows - 1), (down_ref, 0)):
        rest = jnp.zeros((ROWS, span), F32)
        for p in range(planes):
            rest = jnp.where(row8 == p, jnp.broadcast_to(metric_ref[p, j : j + 1, :], (ROWS, span)), rest)
        for piece in range(3):
            part = rest.astype(BF16)
            ref[count + piece] = part
            rest = rest - part.astype(F32)
    for c in range(comps):
        for p in range(planes):
            up = jnp.zeros((ROWS, span), F32)
            down = jnp.zeros((ROWS, span), F32)
            for a in range(snaps):
                mine = row8 // 2 == a
                first = u_ref[a, c, p, 0:ROWS, :].astype(F32)
                last = u_ref[a, c, p, rows - ROWS : rows, :].astype(F32)
                up = jnp.where(mine, pltpu.roll(last, (2 * a + 2) % ROWS, 0), up)
                down = jnp.where(mine, pltpu.roll(first, (2 * a) % ROWS, 0), down)
            up_ref[c * planes + p] = up.astype(BF16)
            down_ref[c * planes + p] = down.astype(BF16)


def inner_kernel(u_ref, metric_ref, volume_ref, op_ref, part_ref, energy_ref, f_ref, e_ref):
    snaps, comps, planes, rows, span = u_ref.shape
    first, end = ROWS, ROWS + rows
    row = sublane((rows, span))
    within = (row > 0) & (row < rows - 1)
    for a in range(snaps):
        energy_ref[a] = jnp.zeros((rows, span), F32)
    for p in range(planes):
        f_ref[p, 0:first, :] = jnp.zeros((ROWS, span), F32)
        f_ref[p, end : end + ROWS, :] = jnp.zeros((ROWS, span), F32)
        e_ref[p, 0:first, :] = jnp.zeros((ROWS, span), F32)
        e_ref[p, end : end + ROWS, :] = jnp.zeros((ROWS, span), F32)

    def field(c, carry):
        for a in range(snaps):
            raw = u_ref[a, c]
            spanned = jnp.dot(raw.reshape(planes * rows, span), op_ref[...], preferred_element_type=F32)
            spanned = spanned.reshape(planes, rows, span)
            u = raw.astype(F32)
            for p in range(planes):
                f_ref[p, first:end, :] = u[p]
            stream = [None] * planes
            for i in range(planes):
                lo, hi = max(i - 1, 0), min(i + 1, planes - 1)
                scale = 0.25 / (hi - lo) ** 2
                edge = (volume_ref[i] * scale) * (u[hi] - u[lo])
                stream[hi] = edge if stream[hi] is None else stream[hi] + edge
                stream[lo] = -edge if stream[lo] is None else stream[lo] - edge
            total = energy_ref[a]
            for p in range(planes):
                jump = f_ref[p, first + 1 : end + 1, :] - f_ref[p, first - 1 : end - 1, :]
                edge = jnp.where(within, (metric_ref[p] * 0.0625) * jump, 0.0)
                e_ref[p, first:end, :] = edge
                partial = volume_ref[p] * (u[p] + spanned[p]) + stream[p]
                total = total + (u[p] * partial + edge * jump)
                normal = e_ref[p, first - 1 : end - 1, :] - e_ref[p, first + 1 : end + 1, :]
                part_ref[a, c, p] = partial + normal
            energy_ref[a] = total
        return carry

    lax.fori_loop(0, comps, field, 0)


def edge_kernel(place_ref, u_ref, part_ref, metric_ref, low_ref, high_ref, here_ref, other_ref, gain_ref, below_ref, above_ref):
    snaps, comps, planes, rows, span = u_ref.shape
    count = comps * planes
    half = planes // 2
    row8 = sublane((ROWS, span))
    below_ref[...] = sum(low_ref[count + i].astype(F32) for i in range(3)) * 0.0625
    above_ref[...] = sum(high_ref[count + i].astype(F32) for i in range(3)) * 0.0625
    zero = jnp.zeros((ROWS, span), F32)
    sums = [[zero, zero] for _ in range(snaps)]
    for i in range(planes):
        p = (place_ref[2] + i) % planes
        metric_low = metric_ref[p, 0:ROWS, :] * 0.0625
        metric_high = metric_ref[p, rows - ROWS : rows, :] * 0.0625
        scale_low = jnp.where(row8 == 0, jnp.broadcast_to(below_ref[pl.ds(p, 1), :], (ROWS, span)), 0.0)
        scale_low = jnp.where(row8 == 1, pltpu.roll(metric_low, 1, 0), scale_low)
        scale_high = jnp.where(row8 == ROWS - 1, jnp.broadcast_to(above_ref[pl.ds(p, 1), :], (ROWS, span)), 0.0)
        scale_high = jnp.where(row8 == ROWS - 2, pltpu.roll(metric_high, ROWS - 1, 0), scale_high)
        for c in range(comps):
            low = low_ref[c * planes + p].astype(F32)
            high = high_ref[c * planes + p].astype(F32)
            for a in range(snaps):
                jump_low = u_ref[a, c, p, 0:ROWS, :].astype(F32) - pltpu.roll(low, (-2 * a) % ROWS, 0)
                jump_high = u_ref[a, c, p, rows - ROWS : rows, :].astype(F32) - pltpu.roll(
                    high, (ROWS - 2 - 2 * a) % ROWS, 0
                )
                edge_low = scale_low * jump_low
                edge_high = scale_high * jump_high
                sums[a][0] = sums[a][0] + edge_low * jump_low
                sums[a][1] = sums[a][1] + edge_high * jump_high
                out = jnp.concatenate(
                    [
                        part_ref[a, c, p, 0:ROWS, :] + edge_low,
                        part_ref[a, c, p, ROWS : rows - ROWS, :],
                        part_ref[a, c, p, rows - ROWS : rows, :] + edge_high,
                    ],
                    axis=0,
                ).astype(BF16)
                if i < half:
                    here_ref[a, c, i] = out
                else:
                    other_ref[a, c, i - half] = out
    for a in range(snaps):
        gain_ref[a, 0] = sums[a][0]
        gain_ref[a, 1] = sums[a][1]


def profile_kernel(planes, energy_ref, gain_ref, profile_ref):
    snaps, rows, span = energy_ref.shape
    row8 = sublane((ROWS, span))
    ones = jnp.ones((ROWS, span), F32)
    for a in range(snaps):
        first = jnp.where(row8 == 0, pltpu.roll(gain_ref[a, 0], ROWS - 1, 0), 0.0)
        last = jnp.where(row8 == ROWS - 1, pltpu.roll(gain_ref[a, 1], 1, 0), 0.0)
        energy = jnp.concatenate(
            [
                energy_ref[a, 0:ROWS, :] + first,
                energy_ref[a, ROWS : rows - ROWS, :],
                energy_ref[a, rows - ROWS : rows, :] + last,
            ],
            axis=0,
        )
        line = lax.dot_general(
            ones, energy, (((1,), (1,)), ((), ())), precision=lax.Precision.HIGHEST, preferred_element_type=F32
        )
        profile_ref[a : a + 1, :] = line[0:1, :] * (1.0 / (planes * span))


def pair_sums(sums, pairs, lefts, rights):
    lefts = [x.astype(F32) for x in lefts]
    rights = [x.astype(F32) for x in rights]
    out = list(sums)
    for t in range(0, lefts[0].shape[0], ROWS):
        for k, (a, b) in enumerate(pairs):
            out[k] = out[k] + lefts[a][t : t + ROWS] * rights[b][t : t + ROWS]
    return out


def totals(sums):
    tiles = []
    for start in range(0, len(sums), ROWS):
        tile = jnp.concatenate([jnp.sum(s, axis=0, keepdims=True) for s in sums[start : start + ROWS]], axis=0)
        tiles.append(jnp.broadcast_to(jnp.sum(tile, axis=1, keepdims=True), tile.shape))
    return tiles


def square_kernel(by_mate, place_ref, u_ref, here_ref, other_ref, block_ref):
    snaps, comps, planes, _, span = u_ref.shape
    half = planes // 2
    row, lane = sublane((ROWS, span)), lanes((ROWS, span))
    pairs = [(b, a) for b in range(snaps) for a in range(snaps) if by_mate or a <= b]
    sums = [jnp.zeros((ROWS, span), F32) for _ in pairs]
    for c in range(comps):
        for i in range(planes):
            p = (place_ref[2] + i) % planes
            ref = here_ref if i < half else other_ref
            sums = pair_sums(
                sums, pairs, [ref[b, c, i % half] for b in range(snaps)], [u_ref[a, c, p] for a in range(snaps)]
            )
    column = place_ref[1] if by_mate else place_ref[0]
    block = jnp.zeros((ROWS, span), F32)
    stacked = []
    for b in range(snaps):
        stacked += [sums[pairs.index((b, a) if (b, a) in pairs else (a, b))] for a in range(snaps)]
        stacked += [sums[0]] * (ROWS - snaps)
    for b, tile in enumerate(totals(stacked)):
        block = jnp.where((lane == column + b) & (row < snaps), tile, block)
    block_ref[...] = block


def cross_kernel(place_ref, got_ref, w_ref, forward_ref, back_ref):
    snaps, comps, planes, _, span = got_ref.shape
    group = ROWS // snaps
    lane, row = lanes((ROWS, span)), sublane((ROWS, span))
    pairs = [(i, j) for i in range(snaps) for j in range(snaps)]
    sums = [jnp.zeros((ROWS, span), F32) for _ in pairs]
    for c in range(comps):
        for i in range(planes):
            sums = pair_sums(
                sums, pairs, [w_ref[a, c, i] for a in range(snaps)], [got_ref[a, c, i] for a in range(snaps)]
            )
    order = [sums[i * snaps + j] for j in range(snaps) for i in range(snaps)]
    forward = jnp.zeros((ROWS, span), F32)
    for t, tile in enumerate(totals(order)):
        forward = forward + jnp.where(lane == place_ref[1] + t * group + row // snaps, tile, 0.0)
    back = jnp.zeros((ROWS, span), F32)
    for t, tile in enumerate(totals(sums)):
        back = back + jnp.where(lane == place_ref[0] + t * group + row // snaps, tile, 0.0)
    for ref, block in ((forward_ref, forward), (back_ref, back)):
        fold = block
        for i in range(1, group):
            fold = fold + pltpu.roll(block, i * snaps, 0)
        ref[...] = fold


def local(velocity, row_level, metric_table):
    snaps, comps, planes, rows, span = velocity.shape
    spaces, cores = lax.axis_size("space"), lax.axis_size("snap")
    chips = cores // 2
    z, s = lax.axis_index("space"), lax.axis_index("snap")
    chip, core = s // 2, s % 2
    mate = s + 1 - 2 * core
    half = planes // 2

    def begin(worker, other):
        return jnp.where(worker < other, 0, half)

    def ints(*values):
        return jnp.stack([jnp.asarray(x, jnp.int32) for x in values])

    def shape(*dims, dtype=BF16):
        return jax.ShapeDtypeStruct(dims, dtype)

    shifts = range(1, chips)
    starts = [begin(chip, (chip - k) % chips) for k in shifts]
    got = []
    for k in shifts:
        piece = lax.dynamic_slice_in_dim(velocity, begin((chip + k) % chips, chip), half, axis=2)
        got.append(lax.ppermute(piece, "snap", [(i, (i + 2 * k) % cores) for i in range(cores)]))

    row_ids = (z * rows + lax.iota(jnp.int32, rows)).astype(F32)
    stretch = 0.25 + 2.25 * row_ids / (rows * spaces - 1)
    chosen = row_level[:, None] == lax.iota(jnp.int32, metric_table.shape[1])[None, :]
    picked = jnp.sum(jnp.where(chosen[None], metric_table[:, None, :], 0.0), axis=2)
    metric = jnp.broadcast_to((picked / stretch)[:, :, None], (planes, rows, span))
    volume = jnp.broadcast_to((stretch / picked)[:, :, None], (planes, rows, span))
    packed = shape(comps * planes + 3, ROWS, span)
    up, down = call(pack_kernel, "pack", [packed, packed], [VMEM] * 2)(velocity, metric)

    def swap(array, first):
        pairs = []
        for i in range(spaces):
            j = ((i - first) ^ 1) + first
            alone = not 0 <= j < spaces
            pairs += [(i * cores + t, i * cores + (t ^ 1) if alone else j * cores + t) for t in range(cores)]
        return lax.ppermute(array, ("space", "snap"), pairs)

    odd = z % 2 == 1
    first = swap(jnp.where(odd, down, up), 0)
    second = swap(jnp.where(odd, up, down), 1)
    first, second, *got = lax.optimization_barrier((first, second, *got))
    low = jnp.where(z > 0, jnp.where(odd, first, second), 0)
    high = jnp.where(z < spaces - 1, jnp.where(odd, second, first), 0)

    operator = jnp.asarray(span_operator(span), BF16)
    part, energy = call(
        inner_kernel,
        "inner",
        [shape(*velocity.shape, dtype=F32), shape(snaps, rows, span, dtype=F32)],
        [VMEM] * 4,
        [pltpu.VMEM((planes, rows + 2 * ROWS, span), F32)] * 2,
    )(velocity, metric, volume, operator)
    own_at, mate_at = s * snaps, mate * snaps
    place = ints(own_at, mate_at, starts[0])
    halves = shape(snaps, comps, half, rows, span)
    here, other, gain = call(
        edge_kernel,
        "edges",
        [halves, halves, shape(snaps, 2, ROWS, span, dtype=F32)],
        [SMEM] + [VMEM] * 5,
        [pltpu.VMEM((ROWS, span), F32)] * 2,
    )(place, velocity, part, metric, low, high)

    def to_mate(array):
        return lax.ppermute(array, "snap", [(i, i ^ 1) for i in range(cores)])

    mate_here, mate_other = to_mate(here), to_mate(other)
    tile = shape(ROWS, span, dtype=F32)
    total = call(functools.partial(square_kernel, False), "square", tile, [SMEM] + [VMEM] * 3)(
        place, velocity, here, other
    )
    for_mate = 0
    back = []
    for k in shifts:
        source = 2 * ((chip - k) % chips) + core
        answer = []
        for at, set_here, set_other in ((own_at, here, other), (mate_at, mate_here, mate_other)):
            w = set_here if k == 1 else jnp.where(starts[k - 1] == starts[0], set_here, set_other)
            answer.append(
                call(cross_kernel, "cross", [tile, tile], [SMEM] + [VMEM] * 2)(
                    ints(at, source * snaps), got[k - 1], w
                )
            )
        total = total + answer[0][0]
        for_mate = for_mate + answer[1][0]
        back.append(answer[0][1] + answer[1][1])
    mates = call(functools.partial(square_kernel, True), "mates", tile, [SMEM] + [VMEM] * 3)(
        place, velocity, mate_here, mate_other
    )
    profile = call(
        functools.partial(profile_kernel, planes), "profile", shape(snaps, rows, dtype=F32), [VMEM] * 2
    )(energy, gain)
    for k in shifts:
        total = total + lax.ppermute(back[k - 1], "snap", [(i, (i - 2 * k) % cores) for i in range(cores)])
    total = total + to_mate(for_mate) + mates
    if spaces & (spaces - 1):
        gram = lax.psum(total, "space")
    else:
        gram = total
        step = 1
        while step < spaces:
            gram = gram + lax.ppermute(gram, "space", [(i, i ^ step) for i in range(spaces)])
            step *= 2
    gram = gram[:snaps, : snaps * cores] * (1.0 / (planes * rows * spaces * span))
    return gram, profile


def solution(mesh):
    in_specs = (P(("grp", "snap"), None, None, "space", None), P("space"), P())
    out_specs = (P(("grp", "snap"), None), P(("grp", "snap"), "space"))
    return jax.shard_map(local, mesh=mesh, in_specs=in_specs, out_specs=out_specs, check_vma=False)
```

time: 145 us -> 27.8 us (0.19)
  waiting for transfers between devices: 89.6 us -> 3.45 us
  matrix products: 19.6 us -> 0 us
  blocking collectives: 10.1 us -> 0 us
  other arithmetic: 11.5 us -> 2.41 us
  starting transfers between devices: 6.28 us -> 13.2 us
  Pallas kernels: 0 us -> 6.46 us
  local copies, waits for them, and re-layouts: 7.16 us -> 1.23 us
    ppermute x5 -> x9, waiting for transfers between devices: 89.6 us -> 3.45 us  [the longest x2 2.59 us: local(): lax.ppermute(gram, 'space', [(i, i ^ step) for i in range(spaces)])]
    dot_general x5 -> x0, matrix products: 19.6 us -> none  [the longest x4 19.4 us: block_product(): lax.dot_general(left.reshape(left.shape[0], -1), right.reshape(right.shap...]
    psum x1 -> x0, blocking collectives: 10.1 us -> none  [local(): gram_rows = lax.psum(partial_value, 'space') * inverse_count]
    ppermute x5 -> x9, starting transfers between devices: 6.28 us -> 13.2 us  [the longest x2 4.81 us: local(): lax.ppermute(gram, 'space', [(i, i ^ step) for i in range(spaces)])]
    pallas_call x0 -> x8, Pallas kernels: none -> 6.46 us  [the longest x2 1.67 us: local(): call(cross_kernel, 'cross', [tile, tile], [SMEM] + [VMEM] * 2)]
    while x3 -> x0, local copies, waits for them, and re-layouts: 4.28 us -> none
    convert_element_type x2 -> x0, other arithmetic: 3.1 us -> none  [the longest x1 2.68 us: weighted_copy(): (feats.astype(jnp.float32) * volume[None, None, :, :, None]).astype(jnp.b...]
    unnamed x8 -> x4, local copies, waits for them, and re-layouts: 2.21 us -> 0.01 us
  transfers between devices with their start and end apart: 5 -> 9, of which waited for: 4 -> 4; matrix products, arithmetic and copies ran while one was open for 0% -> 7% of each run, Pallas kernels for 0% -> 21%
where the time goes in v2:
time: 27.8 us; the launch traced here: 27.6 us
  starting transfers between devices  13.2 us (47%)
  Pallas kernels  6.46 us (23%)
  waiting for transfers between devices  3.45 us (12%)
  other arithmetic  2.41 us (9%)
  local copies, waits for them, and re-layouts  1.23 us (4%)
  between operations  0.81 us (3%)
    ppermute x2, starting transfers between devices, local(): lax.ppermute(gram, 'space', [(i, i ^ step) for i in range(spaces)])  4.81 us
    ppermute x2, starting transfers between devices, swap(): return lax.ppermute(array, ('space', 'snap'), pairs)  3.21 us
    ppermute x1, starting transfers between devices, local(): lax.ppermute(piece, 'snap', [(i, (i + 2 * k) % cores) for i in range(core...  3 us
    ppermute x2, waiting for transfers between devices, local(): lax.ppermute(gram, 'space', [(i, i ^ step) for i in range(spaces)])  2.59 us
    pallas_call x2, Pallas kernels, local(): call(cross_kernel, 'cross', [tile, tile], [SMEM] + [VMEM] * 2)  1.67 us
    ppermute x1, starting transfers between devices, local(): lax.ppermute(back[k - 1], 'snap', [(i, (i - 2 * k) % cores) for i in rang...  1.63 us
    pallas_call x1, Pallas kernels, local(): call(inner_kernel, 'inner', [shape(*velocity.shape, dtype=F32), shape(sna...  1.17 us
    dynamic_slice x1, local copies, waits for them, and re-layouts, local(): lax.dynamic_slice_in_dim(velocity, begin((chip + k) % chips, chip), half,...  1.05 us
  transfers between devices with their start and end apart: 9, of which 4 were waited for; matrix products, arithmetic and copies ran while one was open for 7% of the time, Pallas kernels for 21%

profile of v2, /device:TPU:0, one launch (start us, length us, event | category | flops | bytes accessed | tf_op | source)
XLA Modules:
  0.0 27.6 jit_solution(14461941269528683661)
XLA Ops:
  0.6 0.0 copy-start.1
  0.6 0.0 copy-start
  0.7 1.1 %constant_dynamic-slice_fusion = bf16[4,3,4,24,128]{4,3,2,1,0:T(8,128)(2,1)S(1)} fusion(bf16[4,3,8,24,128]{4,3,2,1,0:T(8,128)(2,1)} %u_ref.9, s32[]{:T(128)S(6)} %select_n.82), kind=kLoop, calls=%fused_computation.14 | loop fusion | bytes 589828 | tf_op jit(solution)/shard_map/dynamic_slice | solution.py:275
  1.7 3.0 %collective-permute-start.2 = (bf16[4,3,4,24,128]{4,3,2,1,0:T(8,128)(2,1)S(1)}, bf16[4,3,4,24,128]{4,3,2,1,0:T(8,128)(2,1)S(1)}, u32[]{:S(2)}, u32[]{:S(2)}) collective-permute-start(bf16[4,3,4,24,128]{4,3,2,1,0:T(8,128)(2,1)S(1)} %constant_dynamic-slice_fusion), channel_id=1, source_target_pairs={{0,2},{1,3},{2,0},{3,1},{4,6},{5,7},{6,4},{7,5},{8,10},{9,11},{10,... | collective-permute-start | bytes 884744 | tf_op jit(solution)/shard_map/ppermute | solution.py:276
  4.8 0.7 %iota_compare_fusion = pred[24,128]{1,0:T(8,128)(4,1)S(1)} fusion(s32[24]{0:T(128)} %param.5), kind=kLoop, calls=%fused_computation.5 | loop fusion | flops 3072 | bytes 3168 | tf_op jit(solution)/shard_map/eq | solution.py:280
  5.5 0.8 %select_reduce_fusion = f32[8,24]{1,0:T(8,128)S(1)} fusion(f32[8,128]{1,0:T(8,128)} %param.6, pred[24,128]{1,0:T(8,128)(4,1)S(1)} %iota_compare_fusion), kind=kLoop, calls=%fused_computation | loop fusion | flops 48960 | bytes 7936 | tf_op jit(solution)/shard_map/reduce_sum | solution.py:281
  6.3 0.1 broadcast_in_dim.46.metric_ref
  6.4 0.0 copy-done
  6.4 0.1 pack.1
  6.5 0.1 collective-permute-start.1
  6.6 3.1 %collective-permute-start = (bf16[27,8,128]{2,1,0:T(8,128)(2,1)S(1)}, bf16[27,8,128]{2,1,0:T(8,128)(2,1)S(1)}, u32[]{:S(2)}, u32[]{:S(2)}) collective-permute-start(bf16[27,8,128]{2,1,0:T(8,128)(2,1)S(1)} %get-tuple-element.33), channel_id=1, source_target_pairs={{0,4},{1,5},{2,6},{3,7},{4,0},{5,1},{6,2},{7,3},{8,12},{9,13},{10,... | collective-permute-start | bytes 165896 | tf_op jit(solution)/shard_map/ppermute | solution.py:293
  9.7 0.1 pad_add_fusion.place_ref
  9.8 0.1 broadcast_in_dim.47.volume_ref
  9.9 0.0 copy-done.1
  9.9 1.2 %inner.1 = (f32[4,3,8,24,128]{4,3,2,1,0:T(8,128)S(1)}, f32[4,24,128]{2,1,0:T(8,128)S(1)}) custom-call(bf16[4,3,8,24,128]{4,3,2,1,0:T(8,128)(2,1)S(1)} %copy-done, f32[8,24,128]{2,1,0:T(8,128)S(1)} %broadcast_in_dim.46.metric_ref, f32[8,24,128]{2,1,0:T(8,128)S(1)} %broadcast_in_dim.47.volume_ref, bf16[128,128]{1,0:T(8,128)(2,1)S(1)} %copy-done.1), custom_call_target="tpu_custom_call" | custom-call | flops 1000 | bytes 1000 | tf_op jit(solution)/shard_map/inner/pallas_call | solution.py:303
  11.1 0.0 collective-permute-done.1
  11.1 0.8 %collective-permute-done = bf16[27,8,128]{2,1,0:T(8,128)(2,1)S(1)} collective-permute-done((bf16[27,8,128]{2,1,0:T(8,128)(2,1)S(1)}, bf16[27,8,128]{2,1,0:T(8,128)(2,1)S(1)}, u32[]{:S(2)}, u32[]{:S(2)}) %collective-permute-start) | collective-permute-done | bytes 55328 | tf_op jit(solution)/shard_map/ppermute | solution.py:293
  11.9 0.0 collective-permute-done.2.got_ref
  11.9 0.8 %edges.1 = (bf16[4,3,4,24,128]{4,3,2,1,0:T(8,128)(2,1)S(1)}, bf16[4,3,4,24,128]{4,3,2,1,0:T(8,128)(2,1)S(1)}, f32[4,2,8,128]{3,2,1,0:T(8,128)S(1)}) custom-call(s32[3]{0:T(128)S(1)} %pad_add_fusion.place_ref, bf16[4,3,8,24,128]{4,3,2,1,0:T(8,128)(2,1)S(1)} %copy-done, f32[4,3,8,24,128]{4,3,2,1,0:T(8,128)S(1)} %get-tuple-element.16.part_ref, ...), custom_call_target="tpu_custom_call" | custom-call | flops 1000 | bytes 1000 | tf_op jit(solution)/shard_map/edges/pallas_call | solution.py:313
  12.7 0.1 collective-permute-start.3
  12.8 0.5 %collective-permute-start.6 = (bf16[4,3,4,24,128]{4,3,2,1,0:T(8,128)(2,1)S(1)}, bf16[4,3,4,24,128]{4,3,2,1,0:T(8,128)(2,1)S(1)}, u32[]{:S(2)}, u32[]{:S(2)}) collective-permute-start(bf16[4,3,4,24,128]{4,3,2,1,0:T(8,128)(2,1)S(1)} %get-tuple-element.22.other_ref), channel_id=1, source_target_pairs={{0,1},{1,0},{2,3},{3,2},{4,5},{5,4},{6,7},{7,6},{8,9},{9,8},{10,11... | collective-permute-start | bytes 884744 | tf_op jit(solution)/shard_map/ppermute | solution.py:322
  13.3 0.1 pad_add_fusion.1.place_ref
  13.3 0.1 pad_add_fusion.2.place_ref
  13.4 0.8 %cross.2 = (f32[8,128]{1,0:T(8,128)S(1)}, f32[8,128]{1,0:T(8,128)S(1)}) custom-call(s32[2]{0:T(128)S(1)} %pad_add_fusion.1.place_ref, bf16[4,3,4,24,128]{4,3,2,1,0:T(8,128)(2,1)S(1)} %collective-permute-done.2.got_ref, bf16[4,3,4,24,128]{4,3,2,1,0:T(8,128)(2,1)S(1)} %get-tuple-element.21.here_ref.w_ref), custom_call_target="tpu_custom_call" | custom-call | flops 1000 | bytes 1000 | tf_op jit(solution)/shard_map/cross/pallas_call | solution.py:337
  14.2 0.1 collective-permute-done.3.w_ref.here_ref
  14.3 0.8 %cross.3 = (f32[8,128]{1,0:T(8,128)S(1)}, f32[8,128]{1,0:T(8,128)S(1)}) custom-call(s32[2]{0:T(128)S(1)} %pad_add_fusion.2.place_ref, bf16[4,3,4,24,128]{4,3,2,1,0:T(8,128)(2,1)S(1)} %collective-permute-done.2.got_ref, bf16[4,3,4,24,128]{4,3,2,1,0:T(8,128)(2,1)S(1)} %collective-permute-done.3.w_ref.here_ref), custom_call_target="tpu_custom_call" | custom-call | flops 1000 | bytes 1000 | tf_op jit(solution)/shard_map/cross/pallas_call | solution.py:337
  15.2 1.6 %collective-permute-start.4 = (f32[8,128]{1,0:T(8,128)S(1)}, f32[8,128]{1,0:T(8,128)S(1)}, u32[]{:S(2)}, u32[]{:S(2)}) collective-permute-start(f32[8,128]{1,0:T(8,128)S(1)} %add.75), channel_id=1, source_target_pairs={{0,2},{1,3},{2,0},{3,1},{4,6},{5,7},{6,4},{7,5},{8,10},{9,11},{10,... | collective-permute-start | bytes 12296 | tf_op jit(solution)/shard_map/ppermute | solution.py:351
  16.8 0.0 collective-permute-start.5
  16.8 1.0 %square.1 = f32[8,128]{1,0:T(8,128)S(1)} custom-call(s32[3]{0:T(128)S(1)} %pad_add_fusion.place_ref, bf16[4,3,8,24,128]{4,3,2,1,0:T(8,128)(2,1)S(1)} %copy-done, bf16[4,3,4,24,128]{4,3,2,1,0:T(8,128)(2,1)S(1)} %get-tuple-element.21.here_ref.w_ref, bf16[4,3,4,24,128]{4,3,2,1,0:T(8,128)(2,1)S(1)} %get-tuple-element.22.other_ref), custom_call_target="tpu_custom_call" | custom-call | flops 1000 | bytes 1000 | tf_op jit(solution)/shard_map/square/pallas_call | solution.py:326
  17.8 0.0 collective-permute-done.6.other_ref
  17.8 1.0 %mates.1 = f32[8,128]{1,0:T(8,128)S(1)} custom-call(s32[3]{0:T(128)S(1)} %pad_add_fusion.place_ref, bf16[4,3,8,24,128]{4,3,2,1,0:T(8,128)(2,1)S(1)} %copy-done, bf16[4,3,4,24,128]{4,3,2,1,0:T(8,128)(2,1)S(1)} %collective-permute-done.3.w_ref.here_ref, bf16[4,3,4,24,128]{4,3,2,1,0:T(8,128)(2,1)S(1)} %collective-permute-done.6.other_ref), custom_call_target="tpu_custom_call" | custom-call | flops 1000 | bytes 1000 | tf_op jit(solution)/shard_map/mates/pallas_call | solution.py:344
  18.8 0.0 collective-permute-done.4
  18.8 0.0 collective-permute-done.5
  18.8 2.1 %collective-permute-start.7 = (f32[8,128]{1,0:T(8,128)S(1)}, f32[8,128]{1,0:T(8,128)S(1)}, u32[]{:S(2)}, u32[]{:S(2)}) collective-permute-start(f32[8,128]{1,0:T(8,128)S(1)} %add_add_fusion), channel_id=1, source_target_pairs={{0,4},{4,0},{8,12},{12,8},{1,5},{5,1},{9,13},{13,9},{2,6},{6,2},{1... | collective-permute-start | bytes 12296 | tf_op jit(solution)/shard_map/ppermute | solution.py:359
  20.9 1.6 %collective-permute-done.7 = f32[8,128]{1,0:T(8,128)S(1)} collective-permute-done((f32[8,128]{1,0:T(8,128)S(1)}, f32[8,128]{1,0:T(8,128)S(1)}, u32[]{:S(2)}, u32[]{:S(2)}) %collective-permute-start.7) | collective-permute-done | bytes 4128 | tf_op jit(solution)/shard_map/ppermute | solution.py:359
  22.5 2.7 %collective-permute-start.8 = (f32[8,128]{1,0:T(8,128)S(1)}, f32[8,128]{1,0:T(8,128)S(1)}, u32[]{:S(2)}, u32[]{:S(2)}) collective-permute-start(f32[8,128]{1,0:T(8,128)S(1)} %add.79), channel_id=1, source_target_pairs={{0,8},{4,12},{8,0},{12,4},{1,9},{5,13},{9,1},{13,5},{2,10},{6,14},... | collective-permute-start | bytes 12296 | tf_op jit(solution)/shard_map/ppermute | solution.py:359
  25.2 0.8 %profile.1 = f32[4,24]{1,0:T(4,128)} custom-call(f32[4,24,128]{2,1,0:T(8,128)S(1)} %get-tuple-element.28.energy_ref, f32[4,2,8,128]{3,2,1,0:T(8,128)S(1)} %get-tuple-element.29.gain_ref), custom_call_target="tpu_custom_call" | custom-call | flops 1000 | bytes 1000 | tf_op jit(solution)/shard_map/profile/pallas_call | solution.py:347
  26.0 1.0 %collective-permute-done.8 = f32[8,128]{1,0:T(8,128)S(1)} collective-permute-done((f32[8,128]{1,0:T(8,128)S(1)}, f32[8,128]{1,0:T(8,128)S(1)}, u32[]{:S(2)}, u32[]{:S(2)}) %collective-permute-start.8) | collective-permute-done | bytes 4128 | tf_op jit(solution)/shard_map/ppermute | solution.py:359
  27.0 0.6 %slice_multiply_fusion = f32[4,16]{1,0:T(4,128)} fusion(f32[8,128]{1,0:T(8,128)S(1)} %add.80), kind=kLoop, calls=%fused_computation.7 | loop fusion | flops 64 | bytes 512 | tf_op jit(solution)/shard_map/mul | solution.py:361
  (8 shorter events, 0.1 us)
Async XLA Ops:
  0.6 9.3 %copy-start.1 = (bf16[128,128]{1,0:T(8,128)(2,1)S(1)}, bf16[128,128]{1,0:T(8,128)(2,1)}, u32[]{:S(2)}) copy-start(bf16[128,128]{1,0:T(8,128)(2,1)} %constant.71.clone.op_ref) | copy-start | bytes 98308
  0.6 5.7 %copy-start = (bf16[4,3,8,24,128]{4,3,2,1,0:T(8,128)(2,1)S(1)}, bf16[4,3,8,24,128]{4,3,2,1,0:T(8,128)(2,1)}, u32[]{:S(2)}) copy-start(bf16[4,3,8,24,128]{4,3,2,1,0:T(8,128)(2,1)} %u_ref.9) | copy-start | bytes 1769476
  1.7 10.1 %collective-permute-start.2 = (bf16[4,3,4,24,128]{4,3,2,1,0:T(8,128)(2,1)S(1)}, bf16[4,3,4,24,128]{4,3,2,1,0:T(8,128)(2,1)S(1)}, u32[]{:S(2)}, u32[]{:S(2)}) collective-permute-start(bf16[4,3,4,24,128]{4,3,2,1,0:T(8,128)(2,1)S(1)} %constant_dynamic-slice_fusion), channel_id=1, source_target_pairs={{0,2},{1,3},{2,0},{3,1},{4,6},{5,7},{6,4},{7,5},{8,10},{9,11},{10,... | collective-permute-start | bytes 884744 | tf_op jit(solution)/shard_map/ppermute | solution.py:276
  6.5 4.6 %collective-permute-start.1 = (bf16[27,8,128]{2,1,0:T(8,128)(2,1)S(1)}, bf16[27,8,128]{2,1,0:T(8,128)(2,1)S(1)}, u32[]{:S(2)}, u32[]{:S(2)}) collective-permute-start(bf16[27,8,128]{2,1,0:T(8,128)(2,1)S(1)} %get-tuple-element.32), channel_id=1, source_target_pairs={{0,1},{1,0},{2,3},{3,2},{4,8},{5,9},{6,10},{7,11},{8,4},{9,5},{10,... | collective-permute-start | bytes 165896 | tf_op jit(solution)/shard_map/ppermute | solution.py:293
  6.6 5.3 %collective-permute-start = (bf16[27,8,128]{2,1,0:T(8,128)(2,1)S(1)}, bf16[27,8,128]{2,1,0:T(8,128)(2,1)S(1)}, u32[]{:S(2)}, u32[]{:S(2)}) collective-permute-start(bf16[27,8,128]{2,1,0:T(8,128)(2,1)S(1)} %get-tuple-element.33), channel_id=1, source_target_pairs={{0,4},{1,5},{2,6},{3,7},{4,0},{5,1},{6,2},{7,3},{8,12},{9,13},{10,... | collective-permute-start | bytes 165896 | tf_op jit(solution)/shard_map/ppermute | solution.py:293
  12.7 1.6 %collective-permute-start.3 = (bf16[4,3,4,24,128]{4,3,2,1,0:T(8,128)(2,1)S(1)}, bf16[4,3,4,24,128]{4,3,2,1,0:T(8,128)(2,1)S(1)}, u32[]{:S(2)}, u32[]{:S(2)}) collective-permute-start(bf16[4,3,4,24,128]{4,3,2,1,0:T(8,128)(2,1)S(1)} %get-tuple-element.21.here_ref.w_ref), channel_id=1, source_target_pairs={{0,1},{1,0},{2,3},{3,2},{4,5},{5,4},{6,7},{7,6},{8,9},{9,8},{10,11... | collective-permute-start | bytes 884744 | tf_op jit(solution)/shard_map/ppermute | solution.py:322
  12.8 5.0 %collective-permute-start.6 = (bf16[4,3,4,24,128]{4,3,2,1,0:T(8,128)(2,1)S(1)}, bf16[4,3,4,24,128]{4,3,2,1,0:T(8,128)(2,1)S(1)}, u32[]{:S(2)}, u32[]{:S(2)}) collective-permute-start(bf16[4,3,4,24,128]{4,3,2,1,0:T(8,128)(2,1)S(1)} %get-tuple-element.22.other_ref), channel_id=1, source_target_pairs={{0,1},{1,0},{2,3},{3,2},{4,5},{5,4},{6,7},{7,6},{8,9},{9,8},{10,11... | collective-permute-start | bytes 884744 | tf_op jit(solution)/shard_map/ppermute | solution.py:322
  15.2 3.6 %collective-permute-start.4 = (f32[8,128]{1,0:T(8,128)S(1)}, f32[8,128]{1,0:T(8,128)S(1)}, u32[]{:S(2)}, u32[]{:S(2)}) collective-permute-start(f32[8,128]{1,0:T(8,128)S(1)} %add.75), channel_id=1, source_target_pairs={{0,2},{1,3},{2,0},{3,1},{4,6},{5,7},{6,4},{7,5},{8,10},{9,11},{10,... | collective-permute-start | bytes 12296 | tf_op jit(solution)/shard_map/ppermute | solution.py:351
  16.8 2.0 %collective-permute-start.5 = (f32[8,128]{1,0:T(8,128)S(1)}, f32[8,128]{1,0:T(8,128)S(1)}, u32[]{:S(2)}, u32[]{:S(2)}) collective-permute-start(f32[8,128]{1,0:T(8,128)S(1)} %get-tuple-element.27), channel_id=1, source_target_pairs={{0,1},{1,0},{2,3},{3,2},{4,5},{5,4},{6,7},{7,6},{8,9},{9,8},{10,11... | collective-permute-start | bytes 12296 | tf_op jit(solution)/shard_map/ppermute | solution.py:322
  18.8 3.7 %collective-permute-start.7 = (f32[8,128]{1,0:T(8,128)S(1)}, f32[8,128]{1,0:T(8,128)S(1)}, u32[]{:S(2)}, u32[]{:S(2)}) collective-permute-start(f32[8,128]{1,0:T(8,128)S(1)} %add_add_fusion), channel_id=1, source_target_pairs={{0,4},{4,0},{8,12},{12,8},{1,5},{5,1},{9,13},{13,9},{2,6},{6,2},{1... | collective-permute-start | bytes 12296 | tf_op jit(solution)/shard_map/ppermute | solution.py:359
  22.5 4.5 %collective-permute-start.8 = (f32[8,128]{1,0:T(8,128)S(1)}, f32[8,128]{1,0:T(8,128)S(1)}, u32[]{:S(2)}, u32[]{:S(2)}) collective-permute-start(f32[8,128]{1,0:T(8,128)S(1)} %add.79), channel_id=1, source_target_pairs={{0,8},{4,12},{8,0},{12,4},{1,9},{5,13},{9,1},{13,5},{2,10},{6,14},... | collective-permute-start | bytes 12296 | tf_op jit(solution)/shard_map/ppermute | solution.py:359

commit v3 on v2

v3 whole, which is shorter than its diff:
```python
import functools

import jax
import jax.numpy as jnp
import numpy as np
from jax import lax
from jax.experimental import pallas as pl
from jax.experimental.pallas import tpu as pltpu
from jax.sharding import PartitionSpec as P

F32 = jnp.float32
BF16 = jnp.bfloat16
ROWS = 8
VMEM = pl.BlockSpec(memory_space=pltpu.VMEM)
OWN, MATE, FIRST, BASE, LAST, SEND = range(6)


def call(kernel, name, out_shape, scratch_shapes=()):
    single = not isinstance(out_shape, list)

    def run(*args):
        return pl.pallas_call(
            kernel,
            name=name,
            out_shape=out_shape,
            in_specs=[VMEM] * len(args),
            out_specs=VMEM if single else [VMEM] * len(out_shape),
            scratch_shapes=list(scratch_shapes),
            compiler_params=pltpu.CompilerParams(vmem_limit_bytes=16 * 2**20),
            cost_estimate=pl.CostEstimate(flops=0, bytes_accessed=0, transcendentals=0),
        )(*args)

    return run


def span_operator(cells):
    diff = np.zeros((cells, cells), np.float32)
    for i in range(cells):
        lo, hi = max(i - 1, 0), min(i + 1, cells - 1)
        scale = 0.5 / (hi - lo)
        diff[i, hi] += scale
        diff[i, lo] -= scale
    return diff.T @ diff


def sublane(shape):
    return lax.broadcasted_iota(jnp.int32, shape, len(shape) - 2)


def lanes(shape):
    return lax.broadcasted_iota(jnp.int32, shape, len(shape) - 1)


def tall(tile, rows):
    return jnp.concatenate([tile] * (rows // ROWS), axis=0)


def stretch_of(row_ids, last):
    return 0.25 + 2.25 * row_ids.astype(F32) / last.astype(F32)


def pack_kernel(place_ref, u_ref, up_ref, down_ref, *pieces):
    snaps, comps, planes, rows, span = u_ref.shape
    half = planes // 2
    row8 = sublane((ROWS, span))
    for k, piece in enumerate(pieces):
        to_first = tall(place_ref[SEND + k], rows) > 0
        for a in range(snaps):
            for c in range(comps):
                for i in range(half):
                    both = u_ref[a, c, i].astype(F32), u_ref[a, c, i + half].astype(F32)
                    piece[a, c, i] = jnp.where(to_first, *both).astype(BF16)
    for c in range(comps):
        for p in range(planes):
            up = jnp.zeros((ROWS, span), F32)
            down = jnp.zeros((ROWS, span), F32)
            for a in range(snaps):
                mine = row8 // 2 == a
                first = u_ref[a, c, p, 0:ROWS, :].astype(F32)
                last = u_ref[a, c, p, rows - ROWS : rows, :].astype(F32)
                up = jnp.where(mine, pltpu.roll(last, (2 * a + 2) % ROWS, 0), up)
                down = jnp.where(mine, pltpu.roll(first, (2 * a) % ROWS, 0), down)
            up_ref[c * planes + p] = up.astype(BF16)
            down_ref[c * planes + p] = down.astype(BF16)


def metric_kernel(place_ref, level_ref, table_ref, metric_ref, volume_ref):
    planes, rows, span = metric_ref.shape
    levels = table_ref.shape[1]
    level = jnp.broadcast_to(level_ref[0:1, 0:rows], (rows, rows))
    level = jnp.where(sublane((rows, rows)) == lanes((rows, rows)), level, 0).astype(F32)
    level = jnp.sum(level, axis=1, keepdims=True).astype(jnp.int32)
    chosen = jnp.broadcast_to(level, (rows, levels)) == lanes((rows, levels))
    stretch = stretch_of(tall(place_ref[BASE], rows) + sublane((rows, span)), tall(place_ref[LAST], rows))
    for p in range(planes):
        picked = jnp.sum(jnp.where(chosen, table_ref[p : p + 1, :], 0.0), axis=1, keepdims=True)
        picked = jnp.broadcast_to(picked, (rows, span))
        metric_ref[p] = picked / stretch
        volume_ref[p] = stretch / picked


def entry_kernel(rows, level_ref, entry_ref):
    row8, lane = sublane(level_ref.shape), lanes(level_ref.shape)
    for i, j in enumerate((rows - 1, 0)):
        level = jnp.sum(jnp.where(lane == j, level_ref[...], 0).astype(F32), axis=1, keepdims=True)
        level = jnp.broadcast_to(level, level_ref.shape)
        high = jnp.floor(level * (1.0 / 128.0))
        entry = jnp.where(row8 == 0, high, jnp.where(row8 == 1, level - 128.0 * high, 1.0))
        entry_ref[i, 0] = entry.astype(BF16)


def inner_kernel(u_ref, mate_ref, metric_ref, volume_ref, op_ref, part_ref, mate_part_ref, energy_ref, f_ref, e_ref):
    snaps, comps, planes, rows, span = u_ref.shape
    first, end = ROWS, ROWS + rows
    row = sublane((rows, span))
    within = (row > 0) & (row < rows - 1)
    for a in range(snaps):
        energy_ref[a] = jnp.zeros((rows, span), F32)
    for p in range(planes):
        f_ref[p, 0:first, :] = jnp.zeros((ROWS, span), F32)
        f_ref[p, end : end + ROWS, :] = jnp.zeros((ROWS, span), F32)
        e_ref[p, 0:first, :] = jnp.zeros((ROWS, span), F32)
        e_ref[p, end : end + ROWS, :] = jnp.zeros((ROWS, span), F32)

    def operate(source, target, a, c, energy):
        raw = source[a, c]
        spanned = jnp.dot(raw.reshape(planes * rows, span), op_ref[...], preferred_element_type=F32)
        spanned = spanned.reshape(planes, rows, span)
        u = raw.astype(F32)
        for p in range(planes):
            f_ref[p, first:end, :] = u[p]
        stream = [None] * planes
        for i in range(planes):
            lo, hi = max(i - 1, 0), min(i + 1, planes - 1)
            scale = 0.25 / (hi - lo) ** 2
            edge = (volume_ref[i] * scale) * (u[hi] - u[lo])
            stream[hi] = edge if stream[hi] is None else stream[hi] + edge
            stream[lo] = -edge if stream[lo] is None else stream[lo] - edge
        total = energy[a] if energy is not None else None
        for p in range(planes):
            jump = f_ref[p, first + 1 : end + 1, :] - f_ref[p, first - 1 : end - 1, :]
            edge = jnp.where(within, (metric_ref[p] * 0.0625) * jump, 0.0)
            e_ref[p, first:end, :] = edge
            partial = volume_ref[p] * (u[p] + spanned[p]) + stream[p]
            if energy is not None:
                total = total + (u[p] * partial + edge * jump)
            normal = e_ref[p, first - 1 : end - 1, :] - e_ref[p, first + 1 : end + 1, :]
            target[a, c, p] = partial + normal
        if energy is not None:
            energy[a] = total

    def field(c, carry):
        for a in range(snaps):
            operate(u_ref, part_ref, a, c, energy_ref)
        return carry

    def mate_field(c, carry):
        for a in range(snaps):
            operate(mate_ref, mate_part_ref, a, c, None)
        return carry

    lax.fori_loop(0, comps, field, 0)
    lax.fori_loop(0, comps, mate_field, 0)


def edge_kernel(
    place_ref, table_ref, u_ref, mate_ref, part_ref, mate_part_ref, metric_ref, low_ref, high_ref, gain_ref, *refs
):
    snaps, comps, planes, rows, span = u_ref.shape
    count = comps * planes
    levels = table_ref.shape[1]
    half = planes // 2
    row8 = sublane((ROWS, span))
    is_first = tall(place_ref[FIRST], rows) > 0
    factors = []
    for ref, offset in ((low_ref, -1), (high_ref, rows)):
        sent = ref[2 * count].astype(F32)
        level = (128.0 * sent[0:1, :] + sent[1:2, :]).astype(jnp.int32)
        chosen = lanes((planes, levels)) == jnp.broadcast_to(level[:, 0:1], (planes, levels))
        picked = jnp.sum(jnp.where(chosen, table_ref[...], 0.0), axis=1, keepdims=True)
        stretch = stretch_of(place_ref[BASE][0:1, :] + offset, place_ref[LAST][0:1, :])
        exists = sent[2:3, :] > 0.0
        factors.append(jnp.where(exists, jnp.broadcast_to(picked, (planes, span)) / stretch * 0.0625, 0.0))
    below, above = factors
    scales = []
    for p in range(planes):
        metric_low = metric_ref[p, 0:ROWS, :] * 0.0625
        metric_high = metric_ref[p, rows - ROWS : rows, :] * 0.0625
        scale_low = jnp.where(row8 == 0, jnp.broadcast_to(below[p : p + 1, :], (ROWS, span)), 0.0)
        scale_low = jnp.where(row8 == 1, pltpu.roll(metric_low, 1, 0), scale_low)
        scale_high = jnp.where(row8 == ROWS - 1, jnp.broadcast_to(above[p : p + 1, :], (ROWS, span)), 0.0)
        scale_high = jnp.where(row8 == ROWS - 2, pltpu.roll(metric_high, ROWS - 1, 0), scale_high)
        scales.append((scale_low, scale_high))
    zero = jnp.zeros((ROWS, span), F32)
    sums = [[zero, zero] for _ in range(snaps)]
    work = [(u_ref, part_ref, 0, refs[0], refs[1]), (mate_ref, mate_part_ref, count, refs[2], (refs[3:] or [None])[0])]
    for source, part, offset, here, other in work:
        for i in range(half):
            for c in range(comps):
                at = offset + c * planes + i
                halos = [(low_ref[p].astype(F32), high_ref[p].astype(F32)) for p in (at, at + half)]
                for a in range(snaps):
                    outs = []
                    for p, (low, high) in zip((i, i + half), halos):
                        jump_low = source[a, c, p, 0:ROWS, :].astype(F32) - pltpu.roll(low, (-2 * a) % ROWS, 0)
                        jump_high = source[a, c, p, rows - ROWS : rows, :].astype(F32) - pltpu.roll(
                            high, (ROWS - 2 - 2 * a) % ROWS, 0
                        )
                        edge_low = scales[p][0] * jump_low
                        edge_high = scales[p][1] * jump_high
                        if source is u_ref:
                            sums[a][0] = sums[a][0] + edge_low * jump_low
                            sums[a][1] = sums[a][1] + edge_high * jump_high
                        outs.append(
                            jnp.concatenate(
                                [
                                    part[a, c, p, 0:ROWS, :] + edge_low,
                                    part[a, c, p, ROWS : rows - ROWS, :],
                                    part[a, c, p, rows - ROWS : rows, :] + edge_high,
                                ],
                                axis=0,
                            )
                        )
                    here[a, c, i] = jnp.where(is_first, outs[0], outs[1]).astype(BF16)
                    if other is not None:
                        other[a, c, i] = jnp.where(is_first, outs[1], outs[0]).astype(BF16)
    for a in range(snaps):
        gain_ref[a, 0] = sums[a][0]
        gain_ref[a, 1] = sums[a][1]


def profile_kernel(planes, energy_ref, gain_ref, profile_ref):
    snaps, rows, span = energy_ref.shape
    row8 = sublane((ROWS, span))
    ones = jnp.ones((ROWS, span), F32)
    for a in range(snaps):
        first = jnp.where(row8 == 0, pltpu.roll(gain_ref[a, 0], ROWS - 1, 0), 0.0)
        last = jnp.where(row8 == ROWS - 1, pltpu.roll(gain_ref[a, 1], 1, 0), 0.0)
        energy = jnp.concatenate(
            [
                energy_ref[a, 0:ROWS, :] + first,
                energy_ref[a, ROWS : rows - ROWS, :],
                energy_ref[a, rows - ROWS : rows, :] + last,
            ],
            axis=0,
        )
        line = lax.dot_general(
            ones, energy, (((1,), (1,)), ((), ())), precision=lax.Precision.HIGHEST, preferred_element_type=F32
        )
        profile_ref[a : a + 1, :] = line[0:1, :] * (1.0 / (planes * span))


def pair_sums(sums, pairs, lefts, rights):
    lefts = [x.astype(F32) for x in lefts]
    rights = [x.astype(F32) for x in rights]
    out = list(sums)
    for t in range(0, lefts[0].shape[0], ROWS):
        for k, (a, b) in enumerate(pairs):
            out[k] = out[k] + lefts[a][t : t + ROWS] * rights[b][t : t + ROWS]
    return out


def totals(sums):
    tiles = []
    for start in range(0, len(sums), ROWS):
        tile = jnp.concatenate([jnp.sum(s, axis=0, keepdims=True) for s in sums[start : start + ROWS]], axis=0)
        tiles.append(jnp.broadcast_to(jnp.sum(tile, axis=1, keepdims=True), tile.shape))
    return tiles


def square_kernel(by_mate, place_ref, u_ref, here_ref, other_ref, block_ref):
    snaps, comps, planes, rows, span = u_ref.shape
    half = planes // 2
    row, lane = sublane((ROWS, span)), lanes((ROWS, span))
    is_first = tall(place_ref[FIRST], rows) > 0
    pairs = [(b, a) for b in range(snaps) for a in range(snaps) if by_mate or a <= b]
    sums = [jnp.zeros((ROWS, span), F32) for _ in pairs]
    for c in range(comps):
        for i in range(half):
            both = [(u_ref[a, c, i].astype(F32), u_ref[a, c, i + half].astype(F32)) for a in range(snaps)]
            u_here = [jnp.where(is_first, x, y) for x, y in both]
            u_other = [jnp.where(is_first, y, x) for x, y in both]
            sums = pair_sums(sums, pairs, u_here, [here_ref[b, c, i] for b in range(snaps)])
            sums = pair_sums(sums, pairs, u_other, [other_ref[b, c, i] for b in range(snaps)])
    column = place_ref[MATE] if by_mate else place_ref[OWN]
    block = jnp.zeros((ROWS, span), F32)
    stacked = []
    for b in range(snaps):
        stacked += [sums[pairs.index((b, a) if (b, a) in pairs else (a, b))] for a in range(snaps)]
        stacked += [sums[0]] * (ROWS - snaps)
    for b, tile in enumerate(totals(stacked)):
        block = jnp.where((lane == column + b) & (row < snaps), tile, block)
    block_ref[...] = block


def cross_kernel(place_ref, source_ref, got_ref, w_ref, mate_ref, own_ref, for_mate_ref, back_ref):
    snaps, comps, half, _, span = got_ref.shape
    group = ROWS // snaps
    lane, row = lanes((ROWS, span)), sublane((ROWS, span))
    pairs = [(i, j) for i in range(2 * snaps) for j in range(snaps)]
    sums = [jnp.zeros((ROWS, span), F32) for _ in pairs]
    for c in range(comps):
        for i in range(half):
            left = [ref[a, c, i] for ref in (w_ref, mate_ref) for a in range(snaps)]
            sums = pair_sums(sums, pairs, left, [got_ref[a, c, i] for a in range(snaps)])
    ahead = jnp.zeros((ROWS, span), F32)
    flipped = [sums[i * snaps + j] for j in range(snaps) for i in range(2 * snaps)]
    for t, tile in enumerate(totals(flipped)):
        ahead = ahead + jnp.where(lane == source_ref[...] + t, tile, 0.0)
    own_ref[...] = jnp.where(row < snaps, ahead, 0.0)
    for_mate_ref[...] = jnp.where(row < snaps, pltpu.roll(ahead, ROWS - snaps, 0), 0.0)
    back = jnp.zeros((ROWS, span), F32)
    for t, tile in enumerate(totals(sums)):
        i = t * group + row // snaps
        column = jnp.where(i < snaps, place_ref[OWN] + i, place_ref[MATE] + i - snaps)
        back = back + jnp.where(lane == column, tile, 0.0)
    fold = back
    for i in range(1, group):
        fold = fold + pltpu.roll(back, i * snaps, 0)
    back_ref[...] = fold


def local(velocity, row_level, metric_table):
    snaps, comps, planes, rows, span = velocity.shape
    spaces, cores = lax.axis_size("space"), lax.axis_size("snap")
    chips = cores // 2
    z, s = lax.axis_index("space"), lax.axis_index("snap")
    chip, core = s // 2, s % 2
    mate = s + 1 - 2 * core
    half = planes // 2
    shifts = range(1, chips)

    def shape(*dims, dtype=BF16):
        return jax.ShapeDtypeStruct(dims, dtype)

    def tiles(*values):
        values = jnp.stack([jnp.asarray(x, jnp.int32) for x in values])
        return jnp.broadcast_to(values[:, None, None], (values.shape[0], ROWS, span))

    def to_mate(array):
        return lax.ppermute(array, "snap", [(i, i ^ 1) for i in range(cores)])

    def begins(worker, other):
        return worker < other

    starts = [begins(chip, (chip - k) % chips) for k in shifts]
    place = tiles(
        s * snaps,
        mate * snaps,
        starts[0],
        z * rows,
        rows * spaces - 1,
        *[begins((chip + k) % chips, chip) for k in shifts],
    )
    packed = shape(comps * planes, ROWS, span)
    piece = shape(snaps, comps, half, rows, span)
    up, down, *pieces = call(pack_kernel, "pack", [packed, packed] + [piece] * (chips - 1))(place, velocity)
    got = [
        lax.ppermute(piece, "snap", [(i, (i + 2 * k) % cores) for i in range(cores)])
        for k, piece in zip(shifts, pieces)
    ]
    u_mate = to_mate(velocity)

    odd = z % 2 == 1
    edge_rows = jnp.stack([up, down])
    edge_rows = jnp.concatenate([edge_rows, to_mate(edge_rows)], axis=1)
    levels = jnp.broadcast_to(jnp.pad(row_level, (0, span - rows)), (ROWS, span))
    entry = call(functools.partial(entry_kernel, rows), "entry", shape(2, 1, ROWS, span))(levels)
    sent = jnp.concatenate([edge_rows, entry], axis=1)

    def swap(array, first):
        pairs = []
        for i in range(spaces):
            j = ((i - first) ^ 1) + first
            alone = not 0 <= j < spaces
            pairs += [(i * cores + t, i * cores + (t ^ 1) if alone else j * cores + t) for t in range(cores)]
        return lax.ppermute(array, ("space", "snap"), pairs)

    first = swap(jnp.where(odd, sent[1], sent[0]), 0)
    second = swap(jnp.where(odd, sent[0], sent[1]), 1)
    factor = shape(planes, rows, span, dtype=F32)
    metric, volume = call(metric_kernel, "metric", [factor, factor])(place, levels, metric_table)
    operator = jnp.asarray(span_operator(span), BF16)
    scratch = [pltpu.VMEM((planes, rows + 2 * ROWS, span), F32)] * 2
    full = shape(*velocity.shape, dtype=F32)
    part, part_mate, energy = call(inner_kernel, "inner", [full, full, shape(snaps, rows, span, dtype=F32)], scratch)(
        velocity, u_mate, metric, volume, operator
    )
    first, second, part, *got = lax.optimization_barrier((first, second, part, *got))
    low = jnp.where(z > 0, jnp.where(odd, first, second), 0)
    high = jnp.where(z < spaces - 1, jnp.where(odd, second, first), 0)

    gain, here, other, *mates = call(
        edge_kernel, "edges", [shape(snaps, 2, ROWS, span, dtype=F32)] + [piece] * (2 + min(2, chips - 1))
    )(place, metric_table, velocity, u_mate, part, part_mate, metric, low, high)

    tile = shape(ROWS, span, dtype=F32)
    total, for_mate, back = 0, 0, []
    for k in shifts:
        source = tiles((2 * ((chip - k) % chips) + core) * snaps)[0]
        w, w_mate = here, mates[0]
        if k > 1:
            same = starts[k - 1] == starts[0]
            w, w_mate = jnp.where(same, here, other), jnp.where(same, mates[0], mates[1])
        answer = call(cross_kernel, "cross", [tile] * 3)(place, source, got[k - 1], w, w_mate)
        total = total + answer[0]
        for_mate = for_mate + answer[1]
        back.append(answer[2])
    total = total + call(functools.partial(square_kernel, False), "square", tile)(place, velocity, here, other)
    total = total + call(functools.partial(square_kernel, True), "mates", tile)(place, u_mate, here, other)
    profile = call(functools.partial(profile_kernel, planes), "profile", shape(snaps, rows, dtype=F32))(energy, gain)
    for k in shifts:
        total = total + lax.ppermute(back[k - 1], "snap", [(i, (i - 2 * k) % cores) for i in range(cores)])
    total = total + to_mate(for_mate)
    if spaces & (spaces - 1):
        gram = lax.psum(total, "space")
    else:
        gram = total
        step = 1
        while step < spaces:
            gram = gram + lax.ppermute(gram, "space", [(i, i ^ step) for i in range(spaces)])
            step *= 2
    gram = gram[:snaps, : snaps * cores] * (1.0 / (planes * rows * spaces * span))
    return gram, profile


def solution(mesh):
    in_specs = (P(("grp", "snap"), None, None, "space", None), P("space"), P())
    out_specs = (P(("grp", "snap"), None), P(("grp", "snap"), "space"))
    return jax.shard_map(local, mesh=mesh, in_specs=in_specs, out_specs=out_specs, check_vma=False)
```

time: 27.8 us -> 26.5 us (0.953)
  waiting for transfers between devices: 3.45 us -> 5.76 us
  other arithmetic: 2.41 us -> 0.74 us
  starting transfers between devices: 13.2 us -> 11.7 us
  Pallas kernels: 6.46 us -> 5.51 us
  local copies, waits for them, and re-layouts: 1.23 us -> 1.91 us
    ppermute x1, waiting for transfers between devices: 0.01 us -> 1.7 us  [local(): lax.ppermute(piece, 'snap', [(i, (i + 2 * k) % cores) for i in range(core...]
    ppermute x2, starting transfers between devices: 3.21 us -> 1.64 us  [swap(): return lax.ppermute(array, ('space', 'snap'), pairs)]
    unnamed x4 -> x8, local copies, waits for them, and re-layouts: 0.01 us -> 1.08 us
    dynamic_slice x1 -> x0, local copies, waits for them, and re-layouts: 1.05 us -> none  [local(): lax.dynamic_slice_in_dim(velocity, begin((chip + k) % chips, chip), half,...]
    pallas_call x8 -> x9, Pallas kernels: 6.46 us -> 5.51 us  [run(): pl.pallas_call(kernel, name=name, out_shape=out_shape, in_specs=[VMEM] *...]
    ppermute x1, waiting for transfers between devices: 0.01 us -> 0.88 us  [local(): lax.ppermute(back[k - 1], 'snap', [(i, (i - 2 * k) % cores) for i in rang...]
    reduce_sum x1 -> x0, other arithmetic: 0.78 us -> none  [local(): jnp.sum(jnp.where(chosen[None], metric_table[:, None, :], 0.0), axis=2)]
    eq x1 -> x0, other arithmetic: 0.73 us -> none  [local(): row_level[:, None] == lax.iota(jnp.int32, metric_table.shape[1])[None, :]]
  transfers between devices with their start and end apart: 9 -> 9, of which waited for: 4 -> 5; matrix products, arithmetic and copies ran while one was open for 7% -> 3% of each run, Pallas kernels for 21% -> 17%
where the time goes in v3:
time: 26.5 us; the launch traced here: 26.4 us
  starting transfers between devices  11.7 us (44%)
  waiting for transfers between devices  5.76 us (22%)
  Pallas kernels  5.51 us (21%)
  local copies, waits for them, and re-layouts  1.91 us (7%)
  between operations  0.75 us (3%)
  other arithmetic  0.74 us (3%)
    pallas_call x9, Pallas kernels, run(): pl.pallas_call(kernel, name=name, out_shape=out_shape, in_specs=[VMEM] *...  5.51 us
    ppermute x2, starting transfers between devices, local(): lax.ppermute(gram, 'space', [(i, i ^ step) for i in range(spaces)])  4.73 us
    ppermute x1, starting transfers between devices, local(): lax.ppermute(piece, 'snap', [(i, (i + 2 * k) % cores) for i in range(core...  2.92 us
    ppermute x2, waiting for transfers between devices, local(): lax.ppermute(gram, 'space', [(i, i ^ step) for i in range(spaces)])  2.68 us
    ppermute x1, starting transfers between devices, local(): lax.ppermute(back[k - 1], 'snap', [(i, (i - 2 * k) % cores) for i in rang...  1.75 us
    ppermute x1, waiting for transfers between devices, local(): lax.ppermute(piece, 'snap', [(i, (i + 2 * k) % cores) for i in range(core...  1.7 us
    ppermute x2, starting transfers between devices, swap(): return lax.ppermute(array, ('space', 'snap'), pairs)  1.64 us
    unnamed x8, local copies, waits for them, and re-layouts  1.08 us
  transfers between devices with their start and end apart: 9, of which 5 were waited for; matrix products, arithmetic and copies ran while one was open for 3% of the time, Pallas kernels for 17%

profile of v3, /device:TPU:0, one launch (start us, length us, event | category | flops | bytes accessed | tf_op | source)
XLA Modules:
  0.0 26.4 jit_solution(10687958768969096331)
XLA Ops:
  0.6 0.0 copy-start.2
  0.6 0.0 copy-start.3
  0.7 0.5 %collective-permute-start.3 = (bf16[4,3,8,24,128]{4,3,2,1,0:T(8,128)(2,1)}, bf16[4,3,8,24,128]{4,3,2,1,0:T(8,128)(2,1)S(1)}, u32[]{:S(2)}, u32[]{:S(2)}) collective-permute-start(bf16[4,3,8,24,128]{4,3,2,1,0:T(8,128)(2,1)} %u_ref.7), channel_id=1, source_target_pairs={{0,1},{1,0},{2,3},{3,2},{4,5},{5,4},{6,7},{7,6},{8,9},{9,8},{10,11... | collective-permute-start | bytes 1769480 | tf_op jit(solution)/shard_map/ppermute | solution.py:341
  1.2 0.1 stack.40
  1.3 0.1 broadcast_in_dim.9.place_ref
  1.3 0.0 copy-start
  1.3 1.1 %copy-done = bf16[4,3,8,24,128]{4,3,2,1,0:T(8,128)(2,1)S(1)} copy-done((bf16[4,3,8,24,128]{4,3,2,1,0:T(8,128)(2,1)S(1)}, bf16[4,3,8,24,128]{4,3,2,1,0:T(8,128)(2,1)}, u32[]{:S(2)}) %copy-start) | copy-done | bytes 589848
  2.4 0.0 copy-start.1
  2.4 0.1 pack.1
  2.6 0.1 collective-permute-start
  2.7 2.9 %collective-permute-start.4 = (bf16[4,3,4,24,128]{4,3,2,1,0:T(8,128)(2,1)S(1)}, bf16[4,3,4,24,128]{4,3,2,1,0:T(8,128)(2,1)S(1)}, u32[]{:S(2)}, u32[]{:S(2)}) collective-permute-start(bf16[4,3,4,24,128]{4,3,2,1,0:T(8,128)(2,1)S(1)} %get-tuple-element.26), channel_id=1, source_target_pairs={{0,2},{1,3},{2,0},{3,1},{4,6},{5,7},{6,4},{7,5},{8,10},{9,11},{10,... | collective-permute-start | bytes 884744 | tf_op jit(solution)/shard_map/ppermute | solution.py:359
  5.6 0.7 %pad.4 = s32[128]{0:T(128)S(1)} pad(s32[24]{0:T(128)} %param.5, s32[]{:T(128)} %constant.53.clone.1), padding=0_104 | pad | bytes 612 | tf_op jit(solution)/shard_map/jit(_pad)/pad | solution.py:367
  6.3 0.1 entry.1
  6.4 0.0 collective-permute-done
  6.5 1.6 %collective-permute-start.1 = (bf16[49,8,128]{2,1,0:T(8,128)(2,1)S(1)}, bf16[49,8,128]{2,1,0:T(8,128)(2,1)S(1)}, u32[]{:S(2)}, u32[]{:S(2)}) collective-permute-start(bf16[49,8,128]{2,1,0:T(8,128)(2,1)S(1)} %get-tuple-element.43), channel_id=1, source_target_pairs={{0,4},{1,5},{2,6},{3,7},{4,0},{5,1},{6,2},{7,3},{8,12},{9,13},{10,... | collective-permute-start | bytes 301064 | tf_op jit(solution)/shard_map/ppermute | solution.py:377
  8.1 0.0 collective-permute-start.2
  8.1 0.0 copy-done.3
  8.1 0.2 metric.1
  8.3 0.0 collective-permute-done.3.mate_ref.u_ref
  8.3 0.0 copy-done.2
  8.4 0.0 copy-done.1
  8.4 2.3 %inner.1 = (f32[4,3,8,24,128]{4,3,2,1,0:T(8,128)S(1)}, f32[4,3,8,24,128]{4,3,2,1,0:T(8,128)S(1)}, f32[4,24,128]{2,1,0:T(8,128)S(1)}) custom-call(bf16[4,3,8,24,128]{4,3,2,1,0:T(8,128)(2,1)S(1)} %copy-done.1, bf16[4,3,8,24,128]{4,3,2,1,0:T(8,128)(2,1)S(1)} %collective-permute-done.3.mate_ref.u_ref, f32[8,24,128]{2,1,0:T(8,128)S(1)} %get-tuple-element.23.metric_ref, ...), custom_call_target="tpu_custom_call" | custom-call | tf_op jit(solution)/shard_map/inner/pallas_call | solution.py:22
  10.7 0.5 %collective-permute-done.1 = bf16[49,8,128]{2,1,0:T(8,128)(2,1)S(1)} collective-permute-done((bf16[49,8,128]{2,1,0:T(8,128)(2,1)S(1)}, bf16[49,8,128]{2,1,0:T(8,128)(2,1)S(1)}, u32[]{:S(2)}, u32[]{:S(2)}) %collective-permute-start.1) | collective-permute-done | bytes 100384 | tf_op jit(solution)/shard_map/ppermute | solution.py:377
  11.2 0.0 collective-permute-done.2
  11.2 1.7 %collective-permute-done.4.got_ref = bf16[4,3,4,24,128]{4,3,2,1,0:T(8,128)(2,1)S(1)} collective-permute-done((bf16[4,3,4,24,128]{4,3,2,1,0:T(8,128)(2,1)S(1)}, bf16[4,3,4,24,128]{4,3,2,1,0:T(8,128)(2,1)S(1)}, u32[]{:S(2)}, u32[]{:S(2)}) %collective-permute-start.4) | collective-permute-done | bytes 294944 | tf_op jit(solution)/shard_map/ppermute | solution.py:359
  12.9 0.1 select_select_fusion
  12.9 0.5 %edges.1 = (f32[4,2,8,128]{3,2,1,0:T(8,128)S(1)}, bf16[4,3,4,24,128]{4,3,2,1,0:T(8,128)(2,1)S(1)}, bf16[4,3,4,24,128]{4,3,2,1,0:T(8,128)(2,1)S(1)}, bf16[4,3,4,24,128]{4,3,2,1,0:T(8,128)(2,1)S(1)}) custom-call(s32[6,8,128]{2,1,0:T(8,128)S(1)} %broadcast_in_dim.9.place_ref, f32[8,128]{1,0:T(8,128)S(1)} %copy-done.3, ...), custom_call_target="tpu_custom_call" | custom-call | tf_op jit(solution)/shard_map/edges/pallas_call | solution.py:22
  13.5 0.5 %cross.1 = (f32[8,128]{1,0:T(8,128)S(1)}, f32[8,128]{1,0:T(8,128)S(1)}, f32[8,128]{1,0:T(8,128)S(1)}) custom-call(s32[6,8,128]{2,1,0:T(8,128)S(1)} %broadcast_in_dim.9.place_ref, s32[8,128]{1,0:T(8,128)S(1)} %squeeze.2.source_ref, bf16[4,3,4,24,128]{4,3,2,1,0:T(8,128)(2,1)S(1)} %collective-permute-done.4.got_ref, ...), custom_call_target="tpu_custom_call" | custom-call | tf_op jit(solution)/shard_map/cross/pallas_call | solution.py:22
  14.0 1.7 %collective-permute-start.5 = (f32[8,128]{1,0:T(8,128)S(1)}, f32[8,128]{1,0:T(8,128)S(1)}, u32[]{:S(2)}, u32[]{:S(2)}) collective-permute-start(f32[8,128]{1,0:T(8,128)S(1)} %get-tuple-element.36), channel_id=1, source_target_pairs={{0,2},{1,3},{2,0},{3,1},{4,6},{5,7},{6,4},{7,5},{8,10},{9,11},{10,... | collective-permute-start | bytes 12296 | tf_op jit(solution)/shard_map/ppermute | solution.py:413
  15.7 0.0 collective-permute-start.6
  15.7 0.5 %square.1 = f32[8,128]{1,0:T(8,128)S(1)} custom-call(s32[6,8,128]{2,1,0:T(8,128)S(1)} %broadcast_in_dim.9.place_ref, bf16[4,3,8,24,128]{4,3,2,1,0:T(8,128)(2,1)S(1)} %copy-done.1, bf16[4,3,4,24,128]{4,3,2,1,0:T(8,128)(2,1)S(1)} %get-tuple-element.32.w_ref.here_ref, bf16[4,3,4,24,128]{4,3,2,1,0:T(8,128)(2,1)S(1)} %get-tuple-element.35.other_ref), custom_call_target="tpu_custom_call" | custom-call | tf_op jit(solution)/shard_map/square/pallas_call | solution.py:22
  16.2 0.5 %mates.1 = f32[8,128]{1,0:T(8,128)S(1)} custom-call(s32[6,8,128]{2,1,0:T(8,128)S(1)} %broadcast_in_dim.9.place_ref, bf16[4,3,8,24,128]{4,3,2,1,0:T(8,128)(2,1)S(1)} %collective-permute-done.3.mate_ref.u_ref, bf16[4,3,4,24,128]{4,3,2,1,0:T(8,128)(2,1)S(1)} %get-tuple-element.32.w_ref.here_ref, bf16[4,3,4,24,128]{4,3,2,1,0:T(8,128)(2,1)S(1)} %get-tuple-element.35.other_ref), custom_call_target="tpu_custom_call" | custom-call | tf_op jit(solution)/shard_map/mates/pallas_call | solution.py:22
  16.7 0.9 %collective-permute-done.5 = f32[8,128]{1,0:T(8,128)S(1)} collective-permute-done((f32[8,128]{1,0:T(8,128)S(1)}, f32[8,128]{1,0:T(8,128)S(1)}, u32[]{:S(2)}, u32[]{:S(2)}) %collective-permute-start.5) | collective-permute-done | bytes 4128 | tf_op jit(solution)/shard_map/ppermute | solution.py:413
  17.6 0.0 collective-permute-done.6
  17.6 1.9 %collective-permute-start.7 = (f32[8,128]{1,0:T(8,128)S(1)}, f32[8,128]{1,0:T(8,128)S(1)}, u32[]{:S(2)}, u32[]{:S(2)}) collective-permute-start(f32[8,128]{1,0:T(8,128)S(1)} %add_add_fusion), channel_id=1, source_target_pairs={{0,4},{4,0},{8,12},{12,8},{1,5},{5,1},{9,13},{13,9},{2,6},{6,2},{1... | collective-permute-start | bytes 12296 | tf_op jit(solution)/shard_map/ppermute | solution.py:421
  19.5 1.8 %collective-permute-done.7 = f32[8,128]{1,0:T(8,128)S(1)} collective-permute-done((f32[8,128]{1,0:T(8,128)S(1)}, f32[8,128]{1,0:T(8,128)S(1)}, u32[]{:S(2)}, u32[]{:S(2)}) %collective-permute-start.7) | collective-permute-done | bytes 4128 | tf_op jit(solution)/shard_map/ppermute | solution.py:421
  21.3 2.8 %collective-permute-start.8 = (f32[8,128]{1,0:T(8,128)S(1)}, f32[8,128]{1,0:T(8,128)S(1)}, u32[]{:S(2)}, u32[]{:S(2)}) collective-permute-start(f32[8,128]{1,0:T(8,128)S(1)} %add.56), channel_id=1, source_target_pairs={{0,8},{4,12},{8,0},{12,4},{1,9},{5,13},{9,1},{13,5},{2,10},{6,14},... | collective-permute-start | bytes 12296 | tf_op jit(solution)/shard_map/ppermute | solution.py:421
  24.1 0.8 %profile.1 = f32[4,24]{1,0:T(4,128)} custom-call(f32[4,24,128]{2,1,0:T(8,128)S(1)} %get-tuple-element.38.energy_ref, f32[4,2,8,128]{3,2,1,0:T(8,128)S(1)} %get-tuple-element.39.gain_ref), custom_call_target="tpu_custom_call" | custom-call | tf_op jit(solution)/shard_map/profile/pallas_call | solution.py:22
  24.9 0.9 %collective-permute-done.8 = f32[8,128]{1,0:T(8,128)S(1)} collective-permute-done((f32[8,128]{1,0:T(8,128)S(1)}, f32[8,128]{1,0:T(8,128)S(1)}, u32[]{:S(2)}, u32[]{:S(2)}) %collective-permute-start.8) | collective-permute-done | bytes 4128 | tf_op jit(solution)/shard_map/ppermute | solution.py:421
  25.8 0.6 %slice_multiply_fusion = f32[4,16]{1,0:T(4,128)} fusion(f32[8,128]{1,0:T(8,128)S(1)} %add.57), kind=kLoop, calls=%fused_computation.7 | loop fusion | flops 64 | bytes 512 | tf_op jit(solution)/shard_map/mul | solution.py:423
  (8 shorter events, 0.1 us)
Async XLA Ops:
  0.6 7.7 %copy-start.2 = (bf16[128,128]{1,0:T(8,128)(2,1)S(1)}, bf16[128,128]{1,0:T(8,128)(2,1)}, u32[]{:S(2)}) copy-start(bf16[128,128]{1,0:T(8,128)(2,1)} %constant.62.clone.op_ref) | copy-start | bytes 98308
  0.6 7.5 %copy-start.3 = (f32[8,128]{1,0:T(8,128)S(1)}, f32[8,128]{1,0:T(8,128)}, u32[]{:S(2)}) copy-start(f32[8,128]{1,0:T(8,128)} %table_ref.3) | copy-start | bytes 12292
  0.7 7.7 %collective-permute-start.3 = (bf16[4,3,8,24,128]{4,3,2,1,0:T(8,128)(2,1)}, bf16[4,3,8,24,128]{4,3,2,1,0:T(8,128)(2,1)S(1)}, u32[]{:S(2)}, u32[]{:S(2)}) collective-permute-start(bf16[4,3,8,24,128]{4,3,2,1,0:T(8,128)(2,1)} %u_ref.7), channel_id=1, source_target_pairs={{0,1},{1,0},{2,3},{3,2},{4,5},{5,4},{6,7},{7,6},{8,9},{9,8},{10,11... | collective-permute-start | bytes 1769480 | tf_op jit(solution)/shard_map/ppermute | solution.py:341
  1.3 1.1 %copy-start = (bf16[4,3,8,24,128]{4,3,2,1,0:T(8,128)(2,1)S(1)}, bf16[4,3,8,24,128]{4,3,2,1,0:T(8,128)(2,1)}, u32[]{:S(2)}) copy-start(bf16[4,3,8,24,128]{4,3,2,1,0:T(8,128)(2,1)} %u_ref.7) | copy-start | bytes 1769476
  2.4 6.0 %copy-start.1 = (bf16[4,3,8,24,128]{4,3,2,1,0:T(8,128)(2,1)S(1)}, bf16[4,3,8,24,128]{4,3,2,1,0:T(8,128)(2,1)}, u32[]{:S(2)}) copy-start(bf16[4,3,8,24,128]{4,3,2,1,0:T(8,128)(2,1)} %u_ref.7) | copy-start | bytes 1769476
  2.6 3.8 %collective-permute-start = (bf16[2,24,8,128]{3,2,1,0:T(8,128)(2,1)S(1)}, bf16[2,24,8,128]{3,2,1,0:T(8,128)(2,1)S(1)}, u32[]{:S(2)}, u32[]{:S(2)}) collective-permute-start(bf16[2,24,8,128]{3,2,1,0:T(8,128)(2,1)S(1)} %pad_maximum_fusion.1), channel_id=1, source_target_pairs={{0,1},{1,0},{2,3},{3,2},{4,5},{5,4},{6,7},{7,6},{8,9},{9,8},{10,11... | collective-permute-start | bytes 294920 | tf_op jit(solution)/shard_map/ppermute | solution.py:341
  2.7 10.2 %collective-permute-start.4 = (bf16[4,3,4,24,128]{4,3,2,1,0:T(8,128)(2,1)S(1)}, bf16[4,3,4,24,128]{4,3,2,1,0:T(8,128)(2,1)S(1)}, u32[]{:S(2)}, u32[]{:S(2)}) collective-permute-start(bf16[4,3,4,24,128]{4,3,2,1,0:T(8,128)(2,1)S(1)} %get-tuple-element.26), channel_id=1, source_target_pairs={{0,2},{1,3},{2,0},{3,1},{4,6},{5,7},{6,4},{7,5},{8,10},{9,11},{10,... | collective-permute-start | bytes 884744 | tf_op jit(solution)/shard_map/ppermute | solution.py:359
  6.5 4.7 %collective-permute-start.1 = (bf16[49,8,128]{2,1,0:T(8,128)(2,1)S(1)}, bf16[49,8,128]{2,1,0:T(8,128)(2,1)S(1)}, u32[]{:S(2)}, u32[]{:S(2)}) collective-permute-start(bf16[49,8,128]{2,1,0:T(8,128)(2,1)S(1)} %get-tuple-element.43), channel_id=1, source_target_pairs={{0,4},{1,5},{2,6},{3,7},{4,0},{5,1},{6,2},{7,3},{8,12},{9,13},{10,... | collective-permute-start | bytes 301064 | tf_op jit(solution)/shard_map/ppermute | solution.py:377
  8.1 3.1 %collective-permute-start.2 = (bf16[49,8,128]{2,1,0:T(8,128)(2,1)S(1)}, bf16[49,8,128]{2,1,0:T(8,128)(2,1)S(1)}, u32[]{:S(2)}, u32[]{:S(2)}) collective-permute-start(bf16[49,8,128]{2,1,0:T(8,128)(2,1)S(1)} %get-tuple-element.42), channel_id=1, source_target_pairs={{0,1},{1,0},{2,3},{3,2},{4,8},{5,9},{6,10},{7,11},{8,4},{9,5},{10,... | collective-permute-start | bytes 301064 | tf_op jit(solution)/shard_map/ppermute | solution.py:377
  14.0 3.6 %collective-permute-start.5 = (f32[8,128]{1,0:T(8,128)S(1)}, f32[8,128]{1,0:T(8,128)S(1)}, u32[]{:S(2)}, u32[]{:S(2)}) collective-permute-start(f32[8,128]{1,0:T(8,128)S(1)} %get-tuple-element.36), channel_id=1, source_target_pairs={{0,2},{1,3},{2,0},{3,1},{4,6},{5,7},{6,4},{7,5},{8,10},{9,11},{10,... | collective-permute-start | bytes 12296 | tf_op jit(solution)/shard_map/ppermute | solution.py:413
  15.7 1.9 %collective-permute-start.6 = (f32[8,128]{1,0:T(8,128)S(1)}, f32[8,128]{1,0:T(8,128)S(1)}, u32[]{:S(2)}, u32[]{:S(2)}) collective-permute-start(f32[8,128]{1,0:T(8,128)S(1)} %get-tuple-element.37), channel_id=1, source_target_pairs={{0,1},{1,0},{2,3},{3,2},{4,5},{5,4},{6,7},{7,6},{8,9},{9,8},{10,11... | collective-permute-start | bytes 12296 | tf_op jit(solution)/shard_map/ppermute | solution.py:341
  17.6 3.7 %collective-permute-start.7 = (f32[8,128]{1,0:T(8,128)S(1)}, f32[8,128]{1,0:T(8,128)S(1)}, u32[]{:S(2)}, u32[]{:S(2)}) collective-permute-start(f32[8,128]{1,0:T(8,128)S(1)} %add_add_fusion), channel_id=1, source_target_pairs={{0,4},{4,0},{8,12},{12,8},{1,5},{5,1},{9,13},{13,9},{2,6},{6,2},{1... | collective-permute-start | bytes 12296 | tf_op jit(solution)/shard_map/ppermute | solution.py:421
  21.3 4.5 %collective-permute-start.8 = (f32[8,128]{1,0:T(8,128)S(1)}, f32[8,128]{1,0:T(8,128)S(1)}, u32[]{:S(2)}, u32[]{:S(2)}) collective-permute-start(f32[8,128]{1,0:T(8,128)S(1)} %add.56), channel_id=1, source_target_pairs={{0,8},{4,12},{8,0},{12,4},{1,9},{5,13},{9,1},{13,5},{2,10},{6,14},... | collective-permute-start | bytes 12296 | tf_op jit(solution)/shard_map/ppermute | solution.py:421

commit v4 on v3

v4 whole, which is shorter than its diff:
```python
import functools

import jax
import jax.numpy as jnp
import numpy as np
from jax import lax
from jax.experimental import pallas as pl
from jax.experimental.pallas import tpu as pltpu
from jax.sharding import PartitionSpec as P

F32 = jnp.float32
BF16 = jnp.bfloat16
ROWS = 8
VMEM = pl.BlockSpec(memory_space=pltpu.VMEM)


def call(kernel, name, out_shape, scratch_shapes=()):
    single = not isinstance(out_shape, list)

    def run(*args):
        return pl.pallas_call(
            kernel,
            name=name,
            out_shape=out_shape,
            in_specs=[VMEM] * len(args),
            out_specs=VMEM if single else [VMEM] * len(out_shape),
            scratch_shapes=list(scratch_shapes),
            compiler_params=pltpu.CompilerParams(vmem_limit_bytes=16 * 2**20),
            cost_estimate=pl.CostEstimate(flops=0, bytes_accessed=0, transcendentals=0),
        )(*args)

    return run


def span_operator(cells):
    diff = np.zeros((cells, cells), np.float32)
    for i in range(cells):
        lo, hi = max(i - 1, 0), min(i + 1, cells - 1)
        scale = 0.5 / (hi - lo)
        diff[i, hi] += scale
        diff[i, lo] -= scale
    return diff.T @ diff


def sublane(shape):
    return lax.broadcasted_iota(jnp.int32, shape, len(shape) - 2)


def lanes(shape):
    return lax.broadcasted_iota(jnp.int32, shape, len(shape) - 1)


def stretch_of(row_ids, rows):
    z, spaces = lax.axis_index("space"), lax.axis_size("space")
    return 0.25 + 2.25 * (row_ids + z * rows).astype(F32) / (rows * spaces - 1)


def half_here(k, planes):
    chips = lax.axis_size("snap") // 2
    chip = lax.axis_index("snap") // 2
    return jnp.where(chip < (chip + chips - k) % chips, 0, planes // 2)


def piece_kernel(u_ref, *pieces):
    snaps, comps, planes, _, _ = u_ref.shape
    half = planes // 2
    chips = len(pieces) + 1
    chip = lax.axis_index("snap") // 2
    for k, piece in enumerate(pieces):
        start = jnp.where((chip + k + 1) % chips < chip, 0, half)
        for a in range(snaps):
            for c in range(comps):
                for i in range(half):
                    piece[a, c, i] = u_ref[a, c, start + i]


def pack_kernel(mate_planes, level_ref, u_ref, mate_ref, first_ref, second_ref):
    snaps, comps, planes, rows, span = u_ref.shape
    count = comps * planes
    row8, lane = sublane((ROWS, span)), lanes((ROWS, span))
    odd = lax.axis_index("space") % 2 == 1

    def put(at, up, down):
        first_ref[at] = jnp.where(odd, down, up).astype(BF16)
        second_ref[at] = jnp.where(odd, up, down).astype(BF16)

    entries = []
    for j in (rows - 1, 0):
        level = jnp.sum(jnp.where(lane == j, level_ref[...], 0).astype(F32), axis=1, keepdims=True)
        level = jnp.broadcast_to(level, (ROWS, span))
        high = jnp.floor(level * (1.0 / 128.0))
        entries.append(jnp.where(row8 == 0, high, jnp.where(row8 == 1, level - 128.0 * high, 1.0)))
    put(first_ref.shape[0] - 1, *entries)
    for offset, ref, size in ((0, u_ref, planes), (count, mate_ref, mate_planes)):
        for c in range(comps):
            for i in range(size):
                p = i if size == planes else half_here(1, planes) + i
                up = jnp.zeros((ROWS, span), F32)
                down = jnp.zeros((ROWS, span), F32)
                for a in range(snaps):
                    mine = row8 // 2 == a
                    first = ref[a, c, p, 0:ROWS, :].astype(F32)
                    last = ref[a, c, p, rows - ROWS : rows, :].astype(F32)
                    up = jnp.where(mine, pltpu.roll(last, (2 * a + 2) % ROWS, 0), up)
                    down = jnp.where(mine, pltpu.roll(first, (2 * a) % ROWS, 0), down)
                put(offset + c * size + i, up, down)


def metric_kernel(level_ref, table_ref, metric_ref, volume_ref):
    planes, rows, span = metric_ref.shape
    levels = table_ref.shape[1]
    level = jnp.broadcast_to(level_ref[0:1, 0:rows], (rows, rows))
    level = jnp.where(sublane((rows, rows)) == lanes((rows, rows)), level, 0).astype(F32)
    level = jnp.sum(level, axis=1, keepdims=True).astype(jnp.int32)
    chosen = jnp.broadcast_to(level, (rows, levels)) == lanes((rows, levels))
    stretch = stretch_of(sublane((rows, span)), rows)
    for p in range(planes):
        picked = jnp.sum(jnp.where(chosen, table_ref[p : p + 1, :], 0.0), axis=1, keepdims=True)
        picked = jnp.broadcast_to(picked, (rows, span))
        metric_ref[p] = picked / stretch
        volume_ref[p] = stretch / picked


def inner_kernel(u_ref, mate_ref, metric_ref, volume_ref, op_ref, part_ref, mate_part_ref, energy_ref, f_ref, e_ref):
    snaps, comps, planes, rows, span = u_ref.shape
    first, end = ROWS, ROWS + rows
    row = sublane((rows, span))
    within = (row > 0) & (row < rows - 1)
    for a in range(snaps):
        energy_ref[a] = jnp.zeros((rows, span), F32)
    for p in range(planes):
        f_ref[p, 0:first, :] = jnp.zeros((ROWS, span), F32)
        f_ref[p, end : end + ROWS, :] = jnp.zeros((ROWS, span), F32)
        e_ref[p, 0:first, :] = jnp.zeros((ROWS, span), F32)
        e_ref[p, end : end + ROWS, :] = jnp.zeros((ROWS, span), F32)

    def operate(source, target, a, c, energy):
        raw = source[a, c]
        spanned = jnp.dot(raw.reshape(planes * rows, span), op_ref[...], preferred_element_type=F32)
        spanned = spanned.reshape(planes, rows, span)
        u = raw.astype(F32)
        for p in range(planes):
            f_ref[p, first:end, :] = u[p]
        stream = [None] * planes
        for i in range(planes):
            lo, hi = max(i - 1, 0), min(i + 1, planes - 1)
            scale = 0.25 / (hi - lo) ** 2
            edge = (volume_ref[i] * scale) * (u[hi] - u[lo])
            stream[hi] = edge if stream[hi] is None else stream[hi] + edge
            stream[lo] = -edge if stream[lo] is None else stream[lo] - edge
        total = energy[a] if energy is not None else None
        for p in range(planes):
            jump = f_ref[p, first + 1 : end + 1, :] - f_ref[p, first - 1 : end - 1, :]
            edge = jnp.where(within, (metric_ref[p] * 0.0625) * jump, 0.0)
            e_ref[p, first:end, :] = edge
            partial = volume_ref[p] * (u[p] + spanned[p]) + stream[p]
            if energy is not None:
                total = total + (u[p] * partial + edge * jump)
            normal = e_ref[p, first - 1 : end - 1, :] - e_ref[p, first + 1 : end + 1, :]
            target[a, c, p] = partial + normal
        if energy is not None:
            energy[a] = total

    def field(c, carry):
        for a in range(snaps):
            operate(u_ref, part_ref, a, c, energy_ref)
        return carry

    def mate_field(c, carry):
        for a in range(snaps):
            operate(mate_ref, mate_part_ref, a, c, None)
        return carry

    lax.fori_loop(0, comps, field, 0)
    lax.fori_loop(0, comps, mate_field, 0)


def edge_scales(table_ref, metric_ref, low_ref, high_ref):
    planes, rows, span = metric_ref.shape
    levels = table_ref.shape[1]
    row8 = sublane((ROWS, span))
    factors = []
    for ref, offset in ((low_ref, -1), (high_ref, rows)):
        sent = ref[ref.shape[0] - 1].astype(F32)
        level = (128.0 * sent[0:1, :] + sent[1:2, :]).astype(jnp.int32)
        chosen = lanes((planes, levels)) == jnp.broadcast_to(level[:, 0:1], (planes, levels))
        picked = jnp.sum(jnp.where(chosen, table_ref[...], 0.0), axis=1, keepdims=True)
        stretch = stretch_of(jnp.full((1, span), offset, jnp.int32), rows)
        exists = sent[2:3, :] > 0.0
        factors.append(jnp.where(exists, jnp.broadcast_to(picked, (planes, span)) / stretch * 0.0625, 0.0))
    below, above = factors
    scales = []
    for p in range(planes):
        metric_low = metric_ref[p, 0:ROWS, :] * 0.0625
        metric_high = metric_ref[p, rows - ROWS : rows, :] * 0.0625
        scale_low = jnp.where(row8 == 0, jnp.broadcast_to(below[p : p + 1, :], (ROWS, span)), 0.0)
        scale_low = jnp.where(row8 == 1, pltpu.roll(metric_low, 1, 0), scale_low)
        scale_high = jnp.where(row8 == ROWS - 1, jnp.broadcast_to(above[p : p + 1, :], (ROWS, span)), 0.0)
        scale_high = jnp.where(row8 == ROWS - 2, pltpu.roll(metric_high, ROWS - 1, 0), scale_high)
        scales.append((scale_low, scale_high))
    return scales


def edges_at(scale, u, low, high, a):
    jump_low = u[0:ROWS] - pltpu.roll(low, (-2 * a) % ROWS, 0)
    jump_high = u[-ROWS:] - pltpu.roll(high, (ROWS - 2 - 2 * a) % ROWS, 0)
    edge_low, edge_high = scale[0] * jump_low, scale[1] * jump_high
    return edge_low, edge_high, edge_low * jump_low, edge_high * jump_high


def edge_kernel(table_ref, u_ref, part_ref, metric_ref, low_ref, high_ref, w_ref, gain_ref):
    snaps, comps, planes, rows, span = u_ref.shape
    scales = edge_scales(table_ref, metric_ref, low_ref, high_ref)
    zero = jnp.zeros((ROWS, span), F32)
    sums = [[zero, zero] for _ in range(snaps)]
    for c in range(comps):
        for p in range(planes):
            low, high = low_ref[c * planes + p].astype(F32), high_ref[c * planes + p].astype(F32)
            for a in range(snaps):
                edges = edges_at(scales[p], u_ref[a, c, p].astype(F32), low, high, a)
                sums[a] = [x + y for x, y in zip(sums[a], edges[2:])]
                part = part_ref[a, c, p]
                w_ref[a, c, p] = jnp.concatenate(
                    [part[0:ROWS] + edges[0], part[ROWS : rows - ROWS], part[rows - ROWS :] + edges[1]], axis=0
                ).astype(BF16)
    for a in range(snaps):
        gain_ref[a, 0] = sums[a][0]
        gain_ref[a, 1] = sums[a][1]


def profile_kernel(planes, energy_ref, gain_ref, profile_ref):
    snaps, rows, span = energy_ref.shape
    row8 = sublane((ROWS, span))
    ones = jnp.ones((ROWS, span), F32)
    for a in range(snaps):
        first = jnp.where(row8 == 0, pltpu.roll(gain_ref[a, 0], ROWS - 1, 0), 0.0)
        last = jnp.where(row8 == ROWS - 1, pltpu.roll(gain_ref[a, 1], 1, 0), 0.0)
        energy = jnp.concatenate(
            [
                energy_ref[a, 0:ROWS, :] + first,
                energy_ref[a, ROWS : rows - ROWS, :],
                energy_ref[a, rows - ROWS : rows, :] + last,
            ],
            axis=0,
        )
        line = lax.dot_general(
            ones, energy, (((1,), (1,)), ((), ())), precision=lax.Precision.HIGHEST, preferred_element_type=F32
        )
        profile_ref[a : a + 1, :] = line[0:1, :] * (1.0 / (planes * span))


def pair_sums(sums, pairs, lefts, rights):
    lefts = [x.astype(F32) for x in lefts]
    rights = [x.astype(F32) for x in rights]
    out = list(sums)
    for t in range(0, lefts[0].shape[0], ROWS):
        for k, (a, b) in enumerate(pairs):
            out[k] = out[k] + lefts[a][t : t + ROWS] * rights[b][t : t + ROWS]
    return out


def totals(sums):
    tiles = []
    for start in range(0, len(sums), ROWS):
        tile = jnp.concatenate([jnp.sum(s, axis=0, keepdims=True) for s in sums[start : start + ROWS]], axis=0)
        tiles.append(jnp.broadcast_to(jnp.sum(tile, axis=1, keepdims=True), tile.shape))
    return tiles


def square_kernel(by_mate, u_ref, w_ref, block_ref):
    snaps, comps, planes, rows, span = u_ref.shape
    row, lane = sublane((ROWS, span)), lanes((ROWS, span))
    pairs = [(b, a) for b in range(snaps) for a in range(snaps) if by_mate or a <= b]
    sums = [jnp.zeros((ROWS, span), F32) for _ in pairs]
    for c in range(comps):
        for p in range(planes):
            sums = pair_sums(
                sums, pairs, [u_ref[b, c, p] for b in range(snaps)], [w_ref[a, c, p] for a in range(snaps)]
            )
    core = lax.axis_index("snap")
    column = snaps * (core + 1 - 2 * (core % 2) if by_mate else core)
    block = jnp.zeros((ROWS, span), F32)
    stacked = []
    for b in range(snaps):
        stacked += [sums[pairs.index((b, a) if (b, a) in pairs else (a, b))] for a in range(snaps)]
        stacked += [sums[0]] * (ROWS - snaps)
    for b, tile in enumerate(totals(stacked)):
        block = jnp.where((lane == column + b) & (row < snaps), tile, block)
    block_ref[...] = block


def cross_kernel(
    k, table_ref, u_ref, mate_ref, part_ref, mate_part_ref, metric_ref, low_ref, high_ref, got_ref,
    own_ref, for_mate_ref, back_ref, scale_ref,
):
    snaps, comps, half, rows, span = got_ref.shape
    planes = 2 * half
    count = comps * planes
    group = ROWS // snaps
    mate_planes = (low_ref.shape[0] - 1 - count) // comps
    start = half_here(k, planes)
    for p, (low, high) in enumerate(edge_scales(table_ref, metric_ref, low_ref, high_ref)):
        scale_ref[p, 0] = low
        scale_ref[p, 1] = high
    lane, row = lanes((ROWS, span)), sublane((ROWS, span))
    pairs = [(i, j) for i in range(2 * snaps) for j in range(snaps)]
    sums = [jnp.zeros((ROWS, span), F32) for _ in pairs]
    for c in range(comps):
        for i in range(half):
            p = start + i
            scale = scale_ref[p, 0], scale_ref[p, 1]
            at_mate = count + c * mate_planes + (p if mate_planes == planes else i)
            left = []
            for u, part, at in ((u_ref, part_ref, c * planes + p), (mate_ref, mate_part_ref, at_mate)):
                low, high = low_ref[at].astype(F32), high_ref[at].astype(F32)
                for a in range(snaps):
                    edges = edges_at(scale, u[a, c, p].astype(F32), low, high, a)
                    w = part[a, c, p]
                    left.append(
                        jnp.concatenate(
                            [w[0:ROWS] + edges[0], w[ROWS : rows - ROWS], w[rows - ROWS :] + edges[1]], axis=0
                        )
                    )
            sums = pair_sums(sums, pairs, left, [got_ref[a, c, i] for a in range(snaps)])
    cores = lax.axis_size("snap")
    core = lax.axis_index("snap")
    own, mate = core * snaps, (core + 1 - 2 * (core % 2)) * snaps
    source = (core + cores - 2 * k) % cores * snaps
    ahead = jnp.zeros((ROWS, span), F32)
    flipped = [sums[i * snaps + j] for j in range(snaps) for i in range(2 * snaps)]
    for t, tile in enumerate(totals(flipped)):
        ahead = ahead + jnp.where(lane == source + t, tile, 0.0)
    own_ref[...] = jnp.where(row < snaps, ahead, 0.0)
    for_mate_ref[...] = jnp.where(row < snaps, pltpu.roll(ahead, ROWS - snaps, 0), 0.0)
    back = jnp.zeros((ROWS, span), F32)
    for t, tile in enumerate(totals(sums)):
        i = t * group + row // snaps
        back = back + jnp.where(lane == jnp.where(i < snaps, own + i, mate + i - snaps), tile, 0.0)
    fold = back
    for i in range(1, group):
        fold = fold + pltpu.roll(back, i * snaps, 0)
    back_ref[...] = fold


def local(velocity, row_level, metric_table):
    snaps, comps, planes, rows, span = velocity.shape
    spaces, cores = lax.axis_size("space"), lax.axis_size("snap")
    chips = cores // 2
    z = lax.axis_index("space")
    half = planes // 2
    shifts = range(1, chips)

    def shape(*dims, dtype=BF16):
        return jax.ShapeDtypeStruct(dims, dtype)

    def to_mate(array):
        return lax.ppermute(array, "snap", [(i, i ^ 1) for i in range(cores)])

    u_mate = to_mate(velocity)
    piece = shape(snaps, comps, half, rows, span)
    pieces = call(piece_kernel, "piece", [piece] * (chips - 1))(velocity)
    got = [
        lax.ppermute(piece, "snap", [(i, (i + 2 * k) % cores) for i in range(cores)])
        for k, piece in zip(shifts, pieces)
    ]

    odd = z % 2 == 1
    levels = jnp.broadcast_to(jnp.pad(row_level, (0, span - rows)), (ROWS, span))
    mate_planes = half if chips == 2 else planes
    packed = shape(comps * (planes + mate_planes) + 1, ROWS, span)
    first, second = call(functools.partial(pack_kernel, mate_planes), "pack", [packed, packed])(
        levels, velocity, u_mate
    )

    def swap(array, first):
        pairs = []
        for i in range(spaces):
            j = ((i - first) ^ 1) + first
            alone = not 0 <= j < spaces
            pairs += [(i * cores + t, i * cores + (t ^ 1) if alone else j * cores + t) for t in range(cores)]
        return lax.ppermute(array, ("space", "snap"), pairs)

    first, second = swap(first, 0), swap(second, 1)
    factor = shape(planes, rows, span, dtype=F32)
    metric, volume = call(metric_kernel, "metric", [factor, factor])(levels, metric_table)
    operator = jnp.asarray(span_operator(span), BF16)
    scratch = [pltpu.VMEM((planes, rows + 2 * ROWS, span), F32)] * 2
    full = shape(*velocity.shape, dtype=F32)
    part, part_mate, energy = call(inner_kernel, "inner", [full, full, shape(snaps, rows, span, dtype=F32)], scratch)(
        velocity, u_mate, metric, volume, operator
    )
    first, second, part, *got = lax.optimization_barrier((first, second, part, *got))
    low = jnp.where(z > 0, jnp.where(odd, first, second), 0)
    high = jnp.where(z < spaces - 1, jnp.where(odd, second, first), 0)

    tile = shape(ROWS, span, dtype=F32)
    total, for_mate, back = 0, 0, []
    for k in shifts:
        answer = call(
            functools.partial(cross_kernel, k), "cross", [tile] * 3, [pltpu.VMEM((planes, 2, ROWS, span), F32)]
        )(metric_table, velocity, u_mate, part, part_mate, metric, low, high, got[k - 1])
        total = total + answer[0]
        for_mate = for_mate + answer[1]
        back.append(answer[2])
    w, gain = call(edge_kernel, "edges", [shape(*velocity.shape), shape(snaps, 2, ROWS, span, dtype=F32)])(
        metric_table, velocity, part, metric, low, high
    )
    total = total + call(functools.partial(square_kernel, False), "square", tile)(velocity, w)
    total = total + call(functools.partial(square_kernel, True), "mates", tile)(u_mate, w)
    profile = call(functools.partial(profile_kernel, planes), "profile", shape(snaps, rows, dtype=F32))(energy, gain)
    for k in shifts:
        total = total + lax.ppermute(back[k - 1], "snap", [(i, (i - 2 * k) % cores) for i in range(cores)])
    total = total + to_mate(for_mate)
    if spaces & (spaces - 1):
        gram = lax.psum(total, "space")
    else:
        gram = total
        step = 1
        while step < spaces:
            gram = gram + lax.ppermute(gram, "space", [(i, i ^ step) for i in range(spaces)])
            step *= 2
    gram = gram[:snaps, : snaps * cores] * (1.0 / (planes * rows * spaces * span))
    return gram, profile


def solution(mesh):
    in_specs = (P(("grp", "snap"), None, None, "space", None), P("space"), P())
    out_specs = (P(("grp", "snap"), None), P(("grp", "snap"), "space"))
    return jax.shard_map(local, mesh=mesh, in_specs=in_specs, out_specs=out_specs, check_vma=False)
```

time: 26.5 us -> 25.8 us (0.974)
  starting transfers between devices: 11.7 us -> 11.2 us
  waiting for transfers between devices: 5.76 us -> 6.1 us
  Pallas kernels: 5.51 us -> 5.24 us
    ppermute x1, waiting for transfers between devices: 1.7 us -> 2.75 us  [local(): lax.ppermute(piece, 'snap', [(i, (i + 2 * k) % cores) for i in range(core...]
    ppermute x2, waiting for transfers between devices: 0.5 us -> 0.01 us  [swap(): return lax.ppermute(array, ('space', 'snap'), pairs)]
    ppermute x1, starting transfers between devices: 2.92 us -> 2.56 us  [local(): lax.ppermute(piece, 'snap', [(i, (i + 2 * k) % cores) for i in range(core...]
    pallas_call x9, Pallas kernels: 5.51 us -> 5.24 us  [run(): pl.pallas_call(kernel, name=name, out_shape=out_shape, in_specs=[VMEM] *...]
    ppermute x3 -> x2, starting transfers between devices: 0.66 us -> 0.52 us  [to_mate(): return lax.ppermute(array, 'snap', [(i, i ^ 1) for i in range(cores)])]
  transfers between devices with their start and end apart: 9 -> 8, of which waited for: 5 -> 4; matrix products, arithmetic and copies ran while one was open for 3% -> 3% of each run, Pallas kernels for 17% -> 18%
where the time goes in v4:
time: 25.8 us; the launch traced here: 25.6 us
  starting transfers between devices  11.2 us (43%)
  waiting for transfers between devices  6.1 us (24%)
  Pallas kernels  5.24 us (20%)
  local copies, waits for them, and re-layouts  1.73 us (7%)
  between operations  0.69 us (3%)
  other arithmetic  0.64 us (2%)
    pallas_call x9, Pallas kernels, run(): pl.pallas_call(kernel, name=name, out_shape=out_shape, in_specs=[VMEM] *...  5.24 us
    ppermute x2, starting transfers between devices, local(): lax.ppermute(gram, 'space', [(i, i ^ step) for i in range(spaces)])  4.73 us
    ppermute x1, waiting for transfers between devices, local(): lax.ppermute(piece, 'snap', [(i, (i + 2 * k) % cores) for i in range(core...  2.75 us
    ppermute x2, waiting for transfers between devices, local(): lax.ppermute(gram, 'space', [(i, i ^ step) for i in range(spaces)])  2.68 us
    ppermute x1, starting transfers between devices, local(): lax.ppermute(piece, 'snap', [(i, (i + 2 * k) % cores) for i in range(core...  2.56 us
    ppermute x1, starting transfers between devices, local(): lax.ppermute(back[k - 1], 'snap', [(i, (i - 2 * k) % cores) for i in rang...  1.76 us
    ppermute x2, starting transfers between devices, swap(): return lax.ppermute(array, ('space', 'snap'), pairs)  1.64 us
    unnamed x8, local copies, waits for them, and re-layouts  1.07 us
  transfers between devices with their start and end apart: 8, of which 4 were waited for; matrix products, arithmetic and copies ran while one was open for 3% of the time, Pallas kernels for 18%

profile of v4, /device:TPU:0, one launch (start us, length us, event | category | flops | bytes accessed | tf_op | source)
XLA Modules:
  0.0 25.6 jit_solution(9532477438982720335)
XLA Ops:
  0.6 0.5 %collective-permute-start = (bf16[4,3,8,24,128]{4,3,2,1,0:T(8,128)(2,1)}, bf16[4,3,8,24,128]{4,3,2,1,0:T(8,128)(2,1)S(1)}, u32[]{:S(2)}, u32[]{:S(2)}) collective-permute-start(bf16[4,3,8,24,128]{4,3,2,1,0:T(8,128)(2,1)} %u_ref.11), channel_id=1, source_target_pairs={{0,1},{1,0},{2,3},{3,2},{4,5},{5,4},{6,7},{7,6},{8,9},{9,8},{10,11... | collective-permute-start | bytes 1769480 | tf_op jit(solution)/shard_map/ppermute | solution.py:357
  1.1 0.0 copy-start
  1.1 1.1 %copy-done = bf16[4,3,8,24,128]{4,3,2,1,0:T(8,128)(2,1)S(1)} copy-done((bf16[4,3,8,24,128]{4,3,2,1,0:T(8,128)(2,1)S(1)}, bf16[4,3,8,24,128]{4,3,2,1,0:T(8,128)(2,1)}, u32[]{:S(2)}) %copy-start) | copy-done | bytes 589848
  2.2 0.0 copy-start.1
  2.2 0.0 copy-start.2
  2.2 0.0 copy-start.3
  2.2 2.6 %collective-permute-start.3 = (bf16[4,3,4,24,128]{4,3,2,1,0:T(8,128)(2,1)S(1)}, bf16[4,3,4,24,128]{4,3,2,1,0:T(8,128)(2,1)S(1)}, u32[]{:S(2)}, u32[]{:S(2)}) collective-permute-start(bf16[4,3,4,24,128]{4,3,2,1,0:T(8,128)(2,1)S(1)} %piece.1), channel_id=1, source_target_pairs={{0,2},{1,3},{2,0},{3,1},{4,6},{5,7},{6,4},{7,5},{8,10},{9,11},{10,... | collective-permute-start | bytes 884744 | tf_op jit(solution)/shard_map/ppermute | solution.py:363
  4.8 0.7 %pad.4 = s32[128]{0:T(128)S(1)} pad(s32[24]{0:T(128)} %param.5, s32[]{:T(128)} %constant.20.clone.1), padding=0_104 | pad | bytes 612 | tf_op jit(solution)/shard_map/jit(_pad)/pad | solution.py:368
  5.5 0.0 collective-permute-done.mate_ref.u_ref
  5.5 0.0 copy-done.1
  5.5 0.1 pack.1
  5.6 1.6 %collective-permute-start.1 = (bf16[37,8,128]{2,1,0:T(8,128)(2,1)S(1)}, bf16[37,8,128]{2,1,0:T(8,128)(2,1)S(1)}, u32[]{:S(2)}, u32[]{:S(2)}) collective-permute-start(bf16[37,8,128]{2,1,0:T(8,128)(2,1)S(1)} %get-tuple-element.18), channel_id=1, source_target_pairs={{0,4},{1,5},{2,6},{3,7},{4,0},{5,1},{6,2},{7,3},{8,12},{9,13},{10,... | collective-permute-start | bytes 227336 | tf_op jit(solution)/shard_map/ppermute | solution.py:381
  7.3 0.0 collective-permute-start.2
  7.3 0.0 copy-done.2
  7.3 0.2 metric.1
  7.5 0.0 copy-done.3
  7.5 2.2 %inner.1 = (f32[4,3,8,24,128]{4,3,2,1,0:T(8,128)S(1)}, f32[4,3,8,24,128]{4,3,2,1,0:T(8,128)S(1)}, f32[4,24,128]{2,1,0:T(8,128)S(1)}) custom-call(bf16[4,3,8,24,128]{4,3,2,1,0:T(8,128)(2,1)S(1)} %copy-done.1, bf16[4,3,8,24,128]{4,3,2,1,0:T(8,128)(2,1)S(1)} %collective-permute-done.mate_ref.u_ref, f32[8,24,128]{2,1,0:T(8,128)S(1)} %get-tuple-element.20.metric_ref, ...), custom_call_target="tpu_custom_call" | custom-call | tf_op jit(solution)/shard_map/inner/pallas_call | solution.py:21
  9.7 2.8 %collective-permute-done.3.got_ref = bf16[4,3,4,24,128]{4,3,2,1,0:T(8,128)(2,1)S(1)} collective-permute-done((bf16[4,3,4,24,128]{4,3,2,1,0:T(8,128)(2,1)S(1)}, bf16[4,3,4,24,128]{4,3,2,1,0:T(8,128)(2,1)S(1)}, u32[]{:S(2)}, u32[]{:S(2)}) %collective-permute-start.3) | collective-permute-done | bytes 294944 | tf_op jit(solution)/shard_map/ppermute | solution.py:363
  12.5 0.0 collective-permute-done.1
  12.5 0.0 collective-permute-done.2
  12.5 0.7 %cross.1 = (f32[8,128]{1,0:T(8,128)S(1)}, f32[8,128]{1,0:T(8,128)S(1)}, f32[8,128]{1,0:T(8,128)S(1)}) custom-call(f32[8,128]{1,0:T(8,128)S(1)} %copy-done.2, bf16[4,3,8,24,128]{4,3,2,1,0:T(8,128)(2,1)S(1)} %copy-done.1, bf16[4,3,8,24,128]{4,3,2,1,0:T(8,128)(2,1)S(1)} %collective-permute-done.mate_ref.u_ref, ...), custom_call_target="tpu_custom_call" | custom-call | tf_op jit(solution)/shard_map/cross/pallas_call | solution.py:21
  13.2 1.8 %collective-permute-start.4 = (f32[8,128]{1,0:T(8,128)S(1)}, f32[8,128]{1,0:T(8,128)S(1)}, u32[]{:S(2)}, u32[]{:S(2)}) collective-permute-start(f32[8,128]{1,0:T(8,128)S(1)} %get-tuple-element.30), channel_id=1, source_target_pairs={{0,2},{1,3},{2,0},{3,1},{4,6},{5,7},{6,4},{7,5},{8,10},{9,11},{10,... | collective-permute-start | bytes 12296 | tf_op jit(solution)/shard_map/ppermute | solution.py:412
  15.0 0.0 collective-permute-start.5
  15.0 0.3 %edges.1 = (bf16[4,3,8,24,128]{4,3,2,1,0:T(8,128)(2,1)S(1)}, f32[4,2,8,128]{3,2,1,0:T(8,128)S(1)}) custom-call(f32[8,128]{1,0:T(8,128)S(1)} %copy-done.2, bf16[4,3,8,24,128]{4,3,2,1,0:T(8,128)(2,1)S(1)} %copy-done.1, f32[4,3,8,24,128]{4,3,2,1,0:T(8,128)S(1)} %get-tuple-element.23.part_ref, f32[8,24,128]{2,1,0:T(8,128)S(1)} %get-tuple-element.20.metric_ref, ...), custom_call_target="tpu_custom_call" | custom-call | tf_op jit(solution)/shard_map/edges/pallas_call | solution.py:21
  15.3 0.4 %square.1 = f32[8,128]{1,0:T(8,128)S(1)} custom-call(bf16[4,3,8,24,128]{4,3,2,1,0:T(8,128)(2,1)S(1)} %copy-done.1, bf16[4,3,8,24,128]{4,3,2,1,0:T(8,128)(2,1)S(1)} %get-tuple-element.29.w_ref), custom_call_target="tpu_custom_call" | custom-call | tf_op jit(solution)/shard_map/square/pallas_call | solution.py:21
  15.7 0.5 %mates.1 = f32[8,128]{1,0:T(8,128)S(1)} custom-call(bf16[4,3,8,24,128]{4,3,2,1,0:T(8,128)(2,1)S(1)} %collective-permute-done.mate_ref.u_ref, bf16[4,3,8,24,128]{4,3,2,1,0:T(8,128)(2,1)S(1)} %get-tuple-element.29.w_ref), custom_call_target="tpu_custom_call" | custom-call | tf_op jit(solution)/shard_map/mates/pallas_call | solution.py:21
  16.2 0.7 %collective-permute-done.4 = f32[8,128]{1,0:T(8,128)S(1)} collective-permute-done((f32[8,128]{1,0:T(8,128)S(1)}, f32[8,128]{1,0:T(8,128)S(1)}, u32[]{:S(2)}, u32[]{:S(2)}) %collective-permute-start.4) | collective-permute-done | bytes 4128 | tf_op jit(solution)/shard_map/ppermute | solution.py:412
  16.8 0.0 collective-permute-done.5
  16.8 1.9 %collective-permute-start.6 = (f32[8,128]{1,0:T(8,128)S(1)}, f32[8,128]{1,0:T(8,128)S(1)}, u32[]{:S(2)}, u32[]{:S(2)}) collective-permute-start(f32[8,128]{1,0:T(8,128)S(1)} %add_add_fusion), channel_id=1, source_target_pairs={{0,4},{4,0},{8,12},{12,8},{1,5},{5,1},{9,13},{13,9},{2,6},{6,2},{1... | collective-permute-start | bytes 12296 | tf_op jit(solution)/shard_map/ppermute | solution.py:420
  18.7 1.8 %collective-permute-done.6 = f32[8,128]{1,0:T(8,128)S(1)} collective-permute-done((f32[8,128]{1,0:T(8,128)S(1)}, f32[8,128]{1,0:T(8,128)S(1)}, u32[]{:S(2)}, u32[]{:S(2)}) %collective-permute-start.6) | collective-permute-done | bytes 4128 | tf_op jit(solution)/shard_map/ppermute | solution.py:420
  20.5 2.8 %collective-permute-start.7 = (f32[8,128]{1,0:T(8,128)S(1)}, f32[8,128]{1,0:T(8,128)S(1)}, u32[]{:S(2)}, u32[]{:S(2)}) collective-permute-start(f32[8,128]{1,0:T(8,128)S(1)} %add.29), channel_id=1, source_target_pairs={{0,8},{4,12},{8,0},{12,4},{1,9},{5,13},{9,1},{13,5},{2,10},{6,14},... | collective-permute-start | bytes 12296 | tf_op jit(solution)/shard_map/ppermute | solution.py:420
  23.4 0.8 %profile.1 = f32[4,24]{1,0:T(4,128)} custom-call(f32[4,24,128]{2,1,0:T(8,128)S(1)} %get-tuple-element.32.energy_ref, f32[4,2,8,128]{3,2,1,0:T(8,128)S(1)} %get-tuple-element.33.gain_ref), custom_call_target="tpu_custom_call" | custom-call | tf_op jit(solution)/shard_map/profile/pallas_call | solution.py:21
  24.1 0.9 %collective-permute-done.7 = f32[8,128]{1,0:T(8,128)S(1)} collective-permute-done((f32[8,128]{1,0:T(8,128)S(1)}, f32[8,128]{1,0:T(8,128)S(1)}, u32[]{:S(2)}, u32[]{:S(2)}) %collective-permute-start.7) | collective-permute-done | bytes 4128 | tf_op jit(solution)/shard_map/ppermute | solution.py:420
  25.0 0.6 %slice_multiply_fusion = f32[4,16]{1,0:T(4,128)} fusion(f32[8,128]{1,0:T(8,128)S(1)} %add.30), kind=kLoop, calls=%fused_computation.3 | loop fusion | flops 64 | bytes 512 | tf_op jit(solution)/shard_map/mul | solution.py:422
  (6 shorter events, 0.1 us)
Async XLA Ops:
  0.6 4.8 %collective-permute-start = (bf16[4,3,8,24,128]{4,3,2,1,0:T(8,128)(2,1)}, bf16[4,3,8,24,128]{4,3,2,1,0:T(8,128)(2,1)S(1)}, u32[]{:S(2)}, u32[]{:S(2)}) collective-permute-start(bf16[4,3,8,24,128]{4,3,2,1,0:T(8,128)(2,1)} %u_ref.11), channel_id=1, source_target_pairs={{0,1},{1,0},{2,3},{3,2},{4,5},{5,4},{6,7},{7,6},{8,9},{9,8},{10,11... | collective-permute-start | bytes 1769480 | tf_op jit(solution)/shard_map/ppermute | solution.py:357
  1.1 1.1 %copy-start = (bf16[4,3,8,24,128]{4,3,2,1,0:T(8,128)(2,1)S(1)}, bf16[4,3,8,24,128]{4,3,2,1,0:T(8,128)(2,1)}, u32[]{:S(2)}) copy-start(bf16[4,3,8,24,128]{4,3,2,1,0:T(8,128)(2,1)} %u_ref.11) | copy-start | bytes 1769476
  2.2 3.3 %copy-start.1 = (bf16[4,3,8,24,128]{4,3,2,1,0:T(8,128)(2,1)S(1)}, bf16[4,3,8,24,128]{4,3,2,1,0:T(8,128)(2,1)}, u32[]{:S(2)}) copy-start(bf16[4,3,8,24,128]{4,3,2,1,0:T(8,128)(2,1)} %u_ref.11) | copy-start | bytes 1769476
  2.2 5.1 %copy-start.2 = (f32[8,128]{1,0:T(8,128)S(1)}, f32[8,128]{1,0:T(8,128)}, u32[]{:S(2)}) copy-start(f32[8,128]{1,0:T(8,128)} %table_ref.5) | copy-start | bytes 12292
  2.2 5.2 %copy-start.3 = (bf16[128,128]{1,0:T(8,128)(2,1)S(1)}, bf16[128,128]{1,0:T(8,128)(2,1)}, u32[]{:S(2)}) copy-start(bf16[128,128]{1,0:T(8,128)(2,1)} %constant.28.clone.op_ref) | copy-start | bytes 98308
  2.2 10.2 %collective-permute-start.3 = (bf16[4,3,4,24,128]{4,3,2,1,0:T(8,128)(2,1)S(1)}, bf16[4,3,4,24,128]{4,3,2,1,0:T(8,128)(2,1)S(1)}, u32[]{:S(2)}, u32[]{:S(2)}) collective-permute-start(bf16[4,3,4,24,128]{4,3,2,1,0:T(8,128)(2,1)S(1)} %piece.1), channel_id=1, source_target_pairs={{0,2},{1,3},{2,0},{3,1},{4,6},{5,7},{6,4},{7,5},{8,10},{9,11},{10,... | collective-permute-start | bytes 884744 | tf_op jit(solution)/shard_map/ppermute | solution.py:363
  5.6 6.9 %collective-permute-start.1 = (bf16[37,8,128]{2,1,0:T(8,128)(2,1)S(1)}, bf16[37,8,128]{2,1,0:T(8,128)(2,1)S(1)}, u32[]{:S(2)}, u32[]{:S(2)}) collective-permute-start(bf16[37,8,128]{2,1,0:T(8,128)(2,1)S(1)} %get-tuple-element.18), channel_id=1, source_target_pairs={{0,4},{1,5},{2,6},{3,7},{4,0},{5,1},{6,2},{7,3},{8,12},{9,13},{10,... | collective-permute-start | bytes 227336 | tf_op jit(solution)/shard_map/ppermute | solution.py:381
  7.3 5.2 %collective-permute-start.2 = (bf16[37,8,128]{2,1,0:T(8,128)(2,1)S(1)}, bf16[37,8,128]{2,1,0:T(8,128)(2,1)S(1)}, u32[]{:S(2)}, u32[]{:S(2)}) collective-permute-start(bf16[37,8,128]{2,1,0:T(8,128)(2,1)S(1)} %get-tuple-element.19), channel_id=1, source_target_pairs={{0,1},{1,0},{2,3},{3,2},{4,8},{5,9},{6,10},{7,11},{8,4},{9,5},{10,... | collective-permute-start | bytes 227336 | tf_op jit(solution)/shard_map/ppermute | solution.py:381
  13.2 3.6 %collective-permute-start.4 = (f32[8,128]{1,0:T(8,128)S(1)}, f32[8,128]{1,0:T(8,128)S(1)}, u32[]{:S(2)}, u32[]{:S(2)}) collective-permute-start(f32[8,128]{1,0:T(8,128)S(1)} %get-tuple-element.30), channel_id=1, source_target_pairs={{0,2},{1,3},{2,0},{3,1},{4,6},{5,7},{6,4},{7,5},{8,10},{9,11},{10,... | collective-permute-start | bytes 12296 | tf_op jit(solution)/shard_map/ppermute | solution.py:412
  15.0 1.9 %collective-permute-start.5 = (f32[8,128]{1,0:T(8,128)S(1)}, f32[8,128]{1,0:T(8,128)S(1)}, u32[]{:S(2)}, u32[]{:S(2)}) collective-permute-start(f32[8,128]{1,0:T(8,128)S(1)} %get-tuple-element.31), channel_id=1, source_target_pairs={{0,1},{1,0},{2,3},{3,2},{4,5},{5,4},{6,7},{7,6},{8,9},{9,8},{10,11... | collective-permute-start | bytes 12296 | tf_op jit(solution)/shard_map/ppermute | solution.py:357
  16.8 3.7 %collective-permute-start.6 = (f32[8,128]{1,0:T(8,128)S(1)}, f32[8,128]{1,0:T(8,128)S(1)}, u32[]{:S(2)}, u32[]{:S(2)}) collective-permute-start(f32[8,128]{1,0:T(8,128)S(1)} %add_add_fusion), channel_id=1, source_target_pairs={{0,4},{4,0},{8,12},{12,8},{1,5},{5,1},{9,13},{13,9},{2,6},{6,2},{1... | collective-permute-start | bytes 12296 | tf_op jit(solution)/shard_map/ppermute | solution.py:420
  20.5 4.5 %collective-permute-start.7 = (f32[8,128]{1,0:T(8,128)S(1)}, f32[8,128]{1,0:T(8,128)S(1)}, u32[]{:S(2)}, u32[]{:S(2)}) collective-permute-start(f32[8,128]{1,0:T(8,128)S(1)} %add.29), channel_id=1, source_target_pairs={{0,8},{4,12},{8,0},{12,4},{1,9},{5,13},{9,1},{13,5},{2,10},{6,14},... | collective-permute-start | bytes 12296 | tf_op jit(solution)/shard_map/ppermute | solution.py:420

commit v5 on v4

v5 whole, which is shorter than its diff:
```python
import functools

import jax
import jax.numpy as jnp
from jax import lax
from jax.experimental import pallas as pl
from jax.experimental.pallas import tpu as pltpu
from jax.sharding import PartitionSpec as P

F32 = jnp.float32
BF16 = jnp.bfloat16
ROWS = 8
VMEM = pl.BlockSpec(memory_space=pltpu.VMEM)


def call(kernel, name, out_shape, scratch_shapes=()):
    single = not isinstance(out_shape, list)

    def run(*args):
        return pl.pallas_call(
            kernel,
            name=name,
            out_shape=out_shape,
            in_specs=[VMEM] * len(args),
            out_specs=VMEM if single else [VMEM] * len(out_shape),
            scratch_shapes=list(scratch_shapes),
            compiler_params=pltpu.CompilerParams(vmem_limit_bytes=16 * 2**20),
            cost_estimate=pl.CostEstimate(flops=0, bytes_accessed=0, transcendentals=0),
        )(*args)

    return run


def sublane(shape):
    return lax.broadcasted_iota(jnp.int32, shape, len(shape) - 2)


def lanes(shape):
    return lax.broadcasted_iota(jnp.int32, shape, len(shape) - 1)


class Components:
    def __init__(self, refs):
        self.refs = refs

    def __getitem__(self, at):
        return self.refs[at[1]][(at[0],) + at[2:]]


def span_operator(cells):
    i, j = sublane((cells, cells)), lanes((cells, cells))
    low, high = jnp.maximum(i - 1, 0), jnp.minimum(i + 1, cells - 1)
    scale = jnp.where(high - low == 2, 0.25, 0.5)
    diff = jnp.where(j == high, scale, jnp.where(j == low, -scale, 0.0)).astype(BF16)
    return lax.dot_general(diff, diff, (((0,), (0,)), ((), ())), preferred_element_type=F32).astype(BF16)


def stretch_of(row_ids, rows):
    z, spaces = lax.axis_index("space"), lax.axis_size("space")
    return 0.25 + 2.25 * (row_ids + z * rows).astype(F32) / (rows * spaces - 1)


def half_here(k, planes):
    chips = lax.axis_size("snap") // 2
    chip = lax.axis_index("snap") // 2
    return jnp.where(chip < (chip + chips - k) % chips, 0, planes // 2)


def piece_kernel(u_ref, edge_ref, *refs):
    snaps, comps, planes, rows, span = u_ref.shape
    half = planes // 2
    pieces, components = refs[:-comps], refs[-comps:]
    chips = len(pieces) + 1
    chip = lax.axis_index("snap") // 2
    for k, piece in enumerate(pieces):
        start = jnp.where((chip + k + 1) % chips < chip, 0, half)
        for a in range(snaps):
            for c in range(comps):
                for i in range(half):
                    piece[a, c, i] = u_ref[a, c, start + i]
    for c in range(comps):
        components[c][...] = u_ref[:, c]
    row8 = sublane((ROWS, span))
    for t in range(comps * planes, edge_ref.shape[1]):
        edge_ref[0, t] = edge_ref[1, t] = jnp.zeros((ROWS, span), BF16)
    for c in range(comps):
        for p in range(planes):
            up = jnp.zeros((ROWS, span), F32)
            down = jnp.zeros((ROWS, span), F32)
            for a in range(snaps):
                mine = row8 // 2 == a
                first = u_ref[a, c, p, 0:ROWS, :].astype(F32)
                last = u_ref[a, c, p, rows - ROWS : rows, :].astype(F32)
                up = jnp.where(mine, pltpu.roll(last, (2 * a + 2) % ROWS, 0), up)
                down = jnp.where(mine, pltpu.roll(first, (2 * a) % ROWS, 0), down)
            edge_ref[0, c * planes + p] = up.astype(BF16)
            edge_ref[1, c * planes + p] = down.astype(BF16)


def pack_kernel(comps, planes, rows, table_ref, own_ref, mate_ref, first_ref, second_ref):
    count = comps * planes
    mate_planes = (first_ref.shape[0] - 1 - count) // comps
    span = first_ref.shape[2]
    row8, lane = sublane((ROWS, span)), lanes((1, table_ref.shape[1]))
    odd = lax.axis_index("space") % 2
    entries = []
    for j in (rows - 1, 0):
        level = jnp.sum(jnp.where(lane == j, table_ref[planes : planes + 1, :], 0.0), axis=1, keepdims=True)
        level = jnp.broadcast_to(level, (ROWS, span))
        high = jnp.floor(level * (1.0 / 128.0))
        entries.append(jnp.where(row8 == 0, high, jnp.where(row8 == 1, level - 128.0 * high, 1.0)))
    first_ref[first_ref.shape[0] - 1] = jnp.where(odd == 1, entries[1], entries[0]).astype(BF16)
    second_ref[first_ref.shape[0] - 1] = jnp.where(odd == 1, entries[0], entries[1]).astype(BF16)
    for ref, way in ((first_ref, odd), (second_ref, 1 - odd)):
        ref[0:count] = own_ref[way, 0:count]
        for c in range(comps):
            start = c * planes + (0 if mate_planes == planes else half_here(1, planes))
            at = count + c * mate_planes
            ref[at : at + mate_planes] = mate_ref[way, pl.ds(start, mate_planes)]


def metric_kernel(table_ref, metric_ref, volume_ref, operator_ref):
    planes, rows, span = metric_ref.shape
    levels = table_ref.shape[1]
    level = jnp.broadcast_to(table_ref[planes : planes + 1, 0:rows], (rows, rows))
    level = jnp.where(sublane((rows, rows)) == lanes((rows, rows)), level, 0.0)
    level = jnp.sum(level, axis=1, keepdims=True).astype(jnp.int32)
    chosen = jnp.broadcast_to(level, (rows, levels)) == lanes((rows, levels))
    stretch = stretch_of(sublane((rows, span)), rows)
    for p in range(planes):
        picked = jnp.sum(jnp.where(chosen, table_ref[p : p + 1, :], 0.0), axis=1, keepdims=True)
        picked = jnp.broadcast_to(picked, (rows, span))
        metric_ref[p] = picked / stretch
        volume_ref[p] = stretch / picked
    operator_ref[...] = span_operator(span)


def inner_kernel(comps, other, cores, *refs):
    sources = [Components(refs[i * comps : (i + 1) * comps]) for i in range(cores)]
    metric_ref, volume_ref, operator_ref, *parts, energy_ref, f_ref, e_ref = refs[cores * comps :]
    snaps, _, half, rows, span = parts[0].shape
    planes = 2 * half
    first, end = ROWS, ROWS + rows
    row = sublane((rows, span))
    within = (row > 0) & (row < rows - 1)
    for i in range(half):
        for ref in (f_ref, e_ref):
            ref[i, 0:first, :] = jnp.zeros((ROWS, span), F32)
            ref[i, end : end + ROWS, :] = jnp.zeros((ROWS, span), F32)

    def work(start, source, part_ref, own):
        def field(a, carry):
            total = jnp.zeros((rows, span), F32)
            for c in range(comps):
                raw = source[a, c][start : start + half]
                spanned = jnp.dot(raw.reshape(half * rows, span), operator_ref[...], preferred_element_type=F32)
                spanned = spanned.reshape(half, rows, span)
                u = {
                    p: source[a, c, p].astype(F32)
                    for p in range(max(start - 2, 0), min(start + half + 2, planes))
                }
                stream = {}
                for i in range(max(start - 1, 0), min(start + half + 1, planes)):
                    lo, hi = max(i - 1, 0), min(i + 1, planes - 1)
                    edge = (volume_ref[i] * (0.25 / (hi - lo) ** 2)) * (u[hi] - u[lo])
                    stream[hi] = stream[hi] + edge if hi in stream else edge
                    stream[lo] = stream[lo] - edge if lo in stream else -edge
                for i in range(half):
                    p = start + i
                    f_ref[i, first:end, :] = u[p]
                    jump = f_ref[i, first + 1 : end + 1, :] - f_ref[i, first - 1 : end - 1, :]
                    edge = jnp.where(within, (metric_ref[p] * 0.0625) * jump, 0.0)
                    e_ref[i, first:end, :] = edge
                    partial = volume_ref[p] * (u[p] + spanned[i]) + stream[p]
                    if own:
                        total = total + (u[p] * partial + edge * jump)
                    normal = e_ref[i, first - 1 : end - 1, :] - e_ref[i, first + 1 : end + 1, :]
                    part_ref[a, c, i] = partial + normal
            if own:
                energy_ref[a] = total
            return carry

        lax.fori_loop(0, snaps, field, 0)

    def both(start):
        for i in range(cores):
            work(start, sources[i], parts[i], i == 0)

    at_first = (half_here(1, planes) == 0) != other
    pl.when(at_first)(lambda: both(0))
    pl.when(jnp.logical_not(at_first))(lambda: both(half))


def edge_scales(table_ref, metric_ref, low_ref, high_ref):
    planes, rows, span = metric_ref.shape
    levels = table_ref.shape[1]
    row8 = sublane((ROWS, span))
    factors = []
    for ref, offset in ((low_ref, -1), (high_ref, rows)):
        sent = ref[ref.shape[0] - 1].astype(F32)
        level = (128.0 * sent[0:1, :] + sent[1:2, :]).astype(jnp.int32)
        chosen = lanes((planes, levels)) == jnp.broadcast_to(level[:, 0:1], (planes, levels))
        picked = jnp.sum(jnp.where(chosen, table_ref[0:planes, :], 0.0), axis=1, keepdims=True)
        stretch = stretch_of(jnp.full((1, span), offset, jnp.int32), rows)
        exists = sent[2:3, :] > 0.0
        factors.append(jnp.where(exists, jnp.broadcast_to(picked, (planes, span)) / stretch * 0.0625, 0.0))
    below, above = factors
    scales = []
    for p in range(planes):
        metric_low = metric_ref[p, 0:ROWS, :] * 0.0625
        metric_high = metric_ref[p, rows - ROWS : rows, :] * 0.0625
        scale_low = jnp.where(row8 == 0, jnp.broadcast_to(below[p : p + 1, :], (ROWS, span)), 0.0)
        scale_low = jnp.where(row8 == 1, pltpu.roll(metric_low, 1, 0), scale_low)
        scale_high = jnp.where(row8 == ROWS - 1, jnp.broadcast_to(above[p : p + 1, :], (ROWS, span)), 0.0)
        scale_high = jnp.where(row8 == ROWS - 2, pltpu.roll(metric_high, ROWS - 1, 0), scale_high)
        scales.append((scale_low, scale_high))
    return scales


def edges_at(scale, u, low, high, a):
    jump_low = u[0:ROWS] - pltpu.roll(low, (-2 * a) % ROWS, 0)
    jump_high = u[-ROWS:] - pltpu.roll(high, (ROWS - 2 - 2 * a) % ROWS, 0)
    edge_low, edge_high = scale[0] * jump_low, scale[1] * jump_high
    return edge_low, edge_high, edge_low * jump_low, edge_high * jump_high


def edge_kernel(table_ref, part_ref, other_ref, metric_ref, low_ref, high_ref, *refs):
    u_ref, (w_ref, gain_ref, scale_ref) = Components(refs[:-3]), refs[-3:]
    snaps, comps, planes, rows, span = w_ref.shape
    half = planes // 2
    for p, (low, high) in enumerate(edge_scales(table_ref, metric_ref, low_ref, high_ref)):
        scale_ref[p, 0] = low
        scale_ref[p, 1] = high
    start = half_here(1, planes)
    zero = jnp.zeros((ROWS, span), F32)
    sums = [[zero, zero] for _ in range(snaps)]
    for c in range(comps):
        for ref, begin in ((part_ref, start), (other_ref, half - start)):
            for i in range(half):
                p = begin + i
                scale = scale_ref[p, 0], scale_ref[p, 1]
                low, high = low_ref[c * planes + p].astype(F32), high_ref[c * planes + p].astype(F32)
                for a in range(snaps):
                    edges = edges_at(scale, u_ref[a, c, p].astype(F32), low, high, a)
                    sums[a] = [x + y for x, y in zip(sums[a], edges[2:])]
                    part = ref[a, c, i]
                    w_ref[a, c, p] = jnp.concatenate(
                        [part[0:ROWS] + edges[0], part[ROWS : rows - ROWS], part[rows - ROWS :] + edges[1]], axis=0
                    ).astype(BF16)
    for a in range(snaps):
        gain_ref[a, 0] = sums[a][0]
        gain_ref[a, 1] = sums[a][1]


def profile_kernel(planes, energy_ref, other_ref, gain_ref, profile_ref):
    snaps, rows, span = energy_ref.shape
    row8 = sublane((ROWS, span))
    ones = jnp.ones((ROWS, span), F32)
    for a in range(snaps):
        first = jnp.where(row8 == 0, pltpu.roll(gain_ref[a, 0], ROWS - 1, 0), 0.0)
        last = jnp.where(row8 == ROWS - 1, pltpu.roll(gain_ref[a, 1], 1, 0), 0.0)
        energy = energy_ref[a] + other_ref[a]
        energy = jnp.concatenate(
            [
                energy[0:ROWS] + first,
                energy[ROWS : rows - ROWS],
                energy[rows - ROWS :] + last,
            ],
            axis=0,
        )
        line = lax.dot_general(
            ones, energy, (((1,), (1,)), ((), ())), precision=lax.Precision.HIGHEST, preferred_element_type=F32
        )
        profile_ref[a : a + 1, :] = line[0:1, :] * (1.0 / (planes * span))


def pair_sums(sums, pairs, lefts, rights):
    lefts = [x.astype(F32) for x in lefts]
    rights = [x.astype(F32) for x in rights]
    out = list(sums)
    for t in range(0, lefts[0].shape[0], ROWS):
        for k, (a, b) in enumerate(pairs):
            out[k] = out[k] + lefts[a][t : t + ROWS] * rights[b][t : t + ROWS]
    return out


def totals(sums):
    tiles = []
    for start in range(0, len(sums), ROWS):
        tile = jnp.concatenate([jnp.sum(s, axis=0, keepdims=True) for s in sums[start : start + ROWS]], axis=0)
        tiles.append(jnp.broadcast_to(jnp.sum(tile, axis=1, keepdims=True), tile.shape))
    return tiles


def square_kernel(by_mate, *refs):
    w_ref, block_ref = refs[-2:]
    u_ref = Components(refs[:-2])
    snaps, comps, planes, rows, span = w_ref.shape
    row, lane = sublane((ROWS, span)), lanes((ROWS, span))
    pairs = [(b, a) for b in range(snaps) for a in range(snaps) if by_mate or a <= b]
    sums = [jnp.zeros((ROWS, span), F32) for _ in pairs]
    for c in range(comps):
        for p in range(planes):
            sums = pair_sums(
                sums, pairs, [u_ref[b, c, p] for b in range(snaps)], [w_ref[a, c, p] for a in range(snaps)]
            )
    core = lax.axis_index("snap")
    column = snaps * (core + 1 - 2 * (core % 2) if by_mate else core)
    block = jnp.zeros((ROWS, span), F32)
    stacked = []
    for b in range(snaps):
        stacked += [sums[pairs.index((b, a) if (b, a) in pairs else (a, b))] for a in range(snaps)]
        stacked += [sums[0]] * (ROWS - snaps)
    for b, tile in enumerate(totals(stacked)):
        block = jnp.where((lane == column + b) & (row < snaps), tile, block)
    block_ref[...] = block


def cross_kernel(
    k, table_ref, part_ref, mate_part_ref, metric_ref, low_ref, high_ref, got_ref, *refs
):
    own_ref, for_mate_ref, back_ref, scale_ref = refs[-4:]
    comps = part_ref.shape[1]
    u_ref, mate_ref = Components(refs[:comps]), Components(refs[comps:-4])
    snaps, comps, half, rows, span = got_ref.shape
    planes = 2 * half
    count = comps * planes
    group = ROWS // snaps
    mate_planes = (low_ref.shape[0] - 1 - count) // comps
    start = half_here(k, planes)
    for p, (low, high) in enumerate(edge_scales(table_ref, metric_ref, low_ref, high_ref)):
        scale_ref[p, 0] = low
        scale_ref[p, 1] = high
    lane, row = lanes((ROWS, span)), sublane((ROWS, span))
    pairs = [(i, j) for i in range(2 * snaps) for j in range(snaps)]
    sums = [jnp.zeros((ROWS, span), F32) for _ in pairs]
    for c in range(comps):
        for i in range(half):
            p = start + i
            scale = scale_ref[p, 0], scale_ref[p, 1]
            at_mate = count + c * mate_planes + (p if mate_planes == planes else i)
            left = []
            for u, part, at in ((u_ref, part_ref, c * planes + p), (mate_ref, mate_part_ref, at_mate)):
                low, high = low_ref[at].astype(F32), high_ref[at].astype(F32)
                for a in range(snaps):
                    edges = edges_at(scale, u[a, c, p].astype(F32), low, high, a)
                    w = part[a, c, i]
                    left.append(
                        jnp.concatenate(
                            [w[0:ROWS] + edges[0], w[ROWS : rows - ROWS], w[rows - ROWS :] + edges[1]], axis=0
                        )
                    )
            sums = pair_sums(sums, pairs, left, [got_ref[a, c, i] for a in range(snaps)])
    cores = lax.axis_size("snap")
    core = lax.axis_index("snap")
    own, mate = core * snaps, (core + 1 - 2 * (core % 2)) * snaps
    source = (core + cores - 2 * k) % cores * snaps
    ahead = jnp.zeros((ROWS, span), F32)
    flipped = [sums[i * snaps + j] for j in range(snaps) for i in range(2 * snaps)]
    for t, tile in enumerate(totals(flipped)):
        ahead = ahead + jnp.where(lane == source + t, tile, 0.0)
    own_ref[...] = jnp.where(row < snaps, ahead, 0.0)
    for_mate_ref[...] = jnp.where(row < snaps, pltpu.roll(ahead, ROWS - snaps, 0), 0.0)
    back = jnp.zeros((ROWS, span), F32)
    for t, tile in enumerate(totals(sums)):
        i = t * group + row // snaps
        back = back + jnp.where(lane == jnp.where(i < snaps, own + i, mate + i - snaps), tile, 0.0)
    fold = back
    for i in range(1, group):
        fold = fold + pltpu.roll(back, i * snaps, 0)
    back_ref[...] = fold


def local(velocity, row_level, metric_table):
    snaps, comps, planes, rows, span = velocity.shape
    spaces, cores = lax.axis_size("space"), lax.axis_size("snap")
    chips = cores // 2
    z = lax.axis_index("space")
    half = planes // 2
    shifts = range(1, chips)

    def shape(*dims, dtype=BF16):
        return jax.ShapeDtypeStruct(dims, dtype)

    def to_mate(array):
        return lax.ppermute(array, "snap", [(i, i ^ 1) for i in range(cores)])

    piece = shape(snaps, comps, half, rows, span)
    component = shape(snaps, planes, rows, span)
    tiles = max(comps * planes, snaps * planes * rows // ROWS // 2 + 1)
    edge_rows, *pieces = call(
        piece_kernel, "piece", [shape(2, tiles, ROWS, span)] + [piece] * (chips - 1) + [component] * comps
    )(velocity)
    u = pieces[chips - 1 :]
    edge_rows_mate = to_mate(edge_rows)
    u_mate = [to_mate(x) for x in u]
    got = [
        lax.ppermute(piece, "snap", [(i, (i + 2 * k) % cores) for i in range(cores)])
        for k, piece in zip(shifts, pieces[: chips - 1])
    ]

    odd = z % 2 == 1
    levels = max(metric_table.shape[1], rows)
    entries = jnp.pad(row_level[None, :], ((planes, ROWS - 1), (0, levels - rows))).astype(F32)
    table = jnp.pad(metric_table, ((0, ROWS), (0, levels - metric_table.shape[1]))) + entries
    factor = shape(planes, rows, span, dtype=F32)
    metric, volume, operator = call(metric_kernel, "metric", [factor, factor, shape(span, span)])(table)
    scratch = [pltpu.VMEM((half, rows + 2 * ROWS, span), F32)] * 2

    def inner(other, *velocities):
        parts = [shape(snaps, comps, half, rows, span, dtype=F32)] * len(velocities)
        return call(
            functools.partial(inner_kernel, comps, other, len(velocities)),
            "inner",
            parts + [shape(snaps, rows, span, dtype=F32)],
            scratch,
        )(*[x for velocity in velocities for x in velocity], metric, volume, operator)

    part, part_mate, energy = inner(False, u, u_mate)
    mate_planes = half if chips == 2 else planes
    packed = shape(comps * (planes + mate_planes) + 1, ROWS, span)
    first, second = call(functools.partial(pack_kernel, comps, planes, rows), "pack", [packed, packed])(
        table, edge_rows, edge_rows_mate
    )

    def swap(array, first):
        pairs = []
        for i in range(spaces):
            j = ((i - first) ^ 1) + first
            alone = not 0 <= j < spaces
            pairs += [(i * cores + t, i * cores + (t ^ 1) if alone else j * cores + t) for t in range(cores)]
        return lax.ppermute(array, ("space", "snap"), pairs)

    first, second = swap(first, 0), swap(second, 1)
    first, second, part, part_mate, *got = lax.optimization_barrier((first, second, part, part_mate, *got))
    low = jnp.where(z > 0, jnp.where(odd, first, second), 0)
    high = jnp.where(z < spaces - 1, jnp.where(odd, second, first), 0)

    tile = shape(ROWS, span, dtype=F32)
    total, for_mate, back = 0, 0, []
    chip = lax.axis_index("snap") // 2
    *others, energy_other = inner(True, *([u] if chips == 2 else [u, u_mate]))
    for k in shifts:
        parts = part, part_mate
        if k > 1:
            same = (chip < (chip + chips - k) % chips) == (chip < (chip + chips - 1) % chips)
            parts = [jnp.where(same, x, y) for x, y in zip(parts, others)]
        answer = call(
            functools.partial(cross_kernel, k), "cross", [tile] * 3, [pltpu.VMEM((planes, 2, ROWS, span), F32)]
        )(table, *parts, metric, low, high, got[k - 1], *u, *u_mate)
        total = total + answer[0]
        for_mate = for_mate + answer[1]
        back.append(answer[2])
    part_other = others[0]
    w, gain = call(
        edge_kernel,
        "edges",
        [shape(*velocity.shape), shape(snaps, 2, ROWS, span, dtype=F32)],
        [pltpu.VMEM((planes, 2, ROWS, span), F32)],
    )(table, part, part_other, metric, low, high, *u)
    total = total + call(functools.partial(square_kernel, False), "square", tile)(*u, w)
    total = total + call(functools.partial(square_kernel, True), "mates", tile)(*u_mate, w)
    profile = call(functools.partial(profile_kernel, planes), "profile", shape(snaps, rows, dtype=F32))(energy, energy_other, gain)
    for k in shifts:
        total = total + lax.ppermute(back[k - 1], "snap", [(i, (i - 2 * k) % cores) for i in range(cores)])
    total = total + to_mate(for_mate)
    if spaces & (spaces - 1):
        gram = lax.psum(total, "space")
    else:
        gram = total
        step = 1
        while step < spaces:
            gram = gram + lax.ppermute(gram, "space", [(i, i ^ step) for i in range(spaces)])
            step *= 2
    gram = gram[:snaps, : snaps * cores] * (1.0 / (planes * rows * spaces * span))
    return gram, profile


def solution(mesh):
    in_specs = (P(("grp", "snap"), None, None, "space", None), P("space"), P())
    out_specs = (P(("grp", "snap"), None), P(("grp", "snap"), "space"))
    return jax.shard_map(local, mesh=mesh, in_specs=in_specs, out_specs=out_specs, check_vma=False)
```

time: 25.8 us -> 25.3 us (0.981)
  waiting for transfers between devices: 6.1 us -> 5.18 us
  starting transfers between devices: 11.2 us -> 12.1 us
  local copies, waits for them, and re-layouts: 1.73 us -> 1.21 us
    ppermute x1, waiting for transfers between devices: 2.75 us -> 0.97 us  [local(): lax.ppermute(piece, 'snap', [(i, (i + 2 * k) % cores) for i in range(core...]
    ppermute x2, waiting for transfers between devices: 0.01 us -> 1.12 us  [swap(): return lax.ppermute(array, ('space', 'snap'), pairs)]
    pad x1 -> x0, local copies, waits for them, and re-layouts: 0.66 us -> none  [local(): jnp.pad(row_level, (0, span - rows))]
    ppermute x1, waiting for transfers between devices: 0.66 us -> 0.01 us  [local(): lax.ppermute(back[k - 1], 'snap', [(i, (i - 2 * k) % cores) for i in rang...]
    ppermute x2 -> x5, starting transfers between devices: 0.52 us -> 1.04 us  [to_mate(): return lax.ppermute(array, 'snap', [(i, i ^ 1) for i in range(cores)])]
    ppermute x1, starting transfers between devices: 2.56 us -> 3 us  [local(): lax.ppermute(piece, 'snap', [(i, (i + 2 * k) % cores) for i in range(core...]
    ppermute x2 -> x5, waiting for transfers between devices: 0.01 us -> 0.28 us  [to_mate(): return lax.ppermute(array, 'snap', [(i, i ^ 1) for i in range(cores)])]
    unnamed x8 -> x6, local copies, waits for them, and re-layouts: 1.07 us -> 1.21 us
  transfers between devices with their start and end apart: 8 -> 11, of which waited for: 4 -> 5; matrix products, arithmetic and copies ran while one was open for 3% -> 0% of each run, Pallas kernels for 18% -> 18%
where the time goes in v5:
time: 25.3 us; the launch traced here: 25.2 us
  starting transfers between devices  12.1 us (48%)
  Pallas kernels  5.34 us (21%)
  waiting for transfers between devices  5.18 us (20%)
  local copies, waits for them, and re-layouts  1.21 us (5%)
  between operations  0.73 us (3%)
  other arithmetic  0.65 us (3%)
    pallas_call x10, Pallas kernels, run(): pl.pallas_call(kernel, name=name, out_shape=out_shape, in_specs=[VMEM] *...  5.34 us
    ppermute x2, starting transfers between devices, local(): lax.ppermute(gram, 'space', [(i, i ^ step) for i in range(spaces)])  4.6 us
    ppermute x1, starting transfers between devices, local(): lax.ppermute(piece, 'snap', [(i, (i + 2 * k) % cores) for i in range(core...  3 us
    ppermute x2, waiting for transfers between devices, local(): lax.ppermute(gram, 'space', [(i, i ^ step) for i in range(spaces)])  2.8 us
    ppermute x1, starting transfers between devices, local(): lax.ppermute(back[k - 1], 'snap', [(i, (i - 2 * k) % cores) for i in rang...  1.82 us
    ppermute x2, starting transfers between devices, swap(): return lax.ppermute(array, ('space', 'snap'), pairs)  1.6 us
    unnamed x6, local copies, waits for them, and re-layouts  1.21 us
    ppermute x2, waiting for transfers between devices, swap(): return lax.ppermute(array, ('space', 'snap'), pairs)  1.12 us
  transfers between devices with their start and end apart: 11, of which 5 were waited for; matrix products, arithmetic and copies ran while one was open for 0% of the time, Pallas kernels for 18%

profile of v5, /device:TPU:0, one launch (start us, length us, event | category | flops | bytes accessed | tf_op | source)
XLA Modules:
  0.0 25.2 jit_solution(16258023739931308150)
XLA Ops:
  0.6 0.0 copy-start
  0.6 1.1 %copy-done = bf16[4,3,8,24,128]{4,3,2,1,0:T(8,128)(2,1)S(1)} copy-done((bf16[4,3,8,24,128]{4,3,2,1,0:T(8,128)(2,1)S(1)}, bf16[4,3,8,24,128]{4,3,2,1,0:T(8,128)(2,1)}, u32[]{:S(2)}) %copy-start) | copy-done | bytes 589848
  1.7 0.1 piece.1
  1.8 3.0 %collective-permute-start.6 = (bf16[4,3,4,24,128]{4,3,2,1,0:T(8,128)(2,1)S(1)}, bf16[4,3,4,24,128]{4,3,2,1,0:T(8,128)(2,1)S(1)}, u32[]{:S(2)}, u32[]{:S(2)}) collective-permute-start(bf16[4,3,4,24,128]{4,3,2,1,0:T(8,128)(2,1)S(1)} %get-tuple-element.38), channel_id=1, source_target_pairs={{0,2},{1,3},{2,0},{3,1},{4,6},{5,7},{6,4},{7,5},{8,10},{9,11},{10,... | collective-permute-start | bytes 884744 | tf_op jit(solution)/shard_map/ppermute | solution.py:398
  4.8 0.0 copy-start.1
  4.8 0.0 collective-permute-start
  4.9 0.5 %collective-permute-start.3 = (bf16[4,8,24,128]{3,2,1,0:T(8,128)(2,1)S(1)}, bf16[4,8,24,128]{3,2,1,0:T(8,128)(2,1)S(1)}, u32[]{:S(2)}, u32[]{:S(2)}) collective-permute-start(bf16[4,8,24,128]{3,2,1,0:T(8,128)(2,1)S(1)} %get-tuple-element.30.refs_0_), channel_id=1, source_target_pairs={{0,1},{1,0},{2,3},{3,2},{4,5},{5,4},{6,7},{7,6},{8,9},{9,8},{10,11... | collective-permute-start | bytes 589832 | tf_op jit(solution)/shard_map/ppermute | solution.py:386
  5.4 0.0 collective-permute-start.4
  5.4 0.0 copy-start.2
  5.4 0.5 %collective-permute-start.5 = (bf16[4,8,24,128]{3,2,1,0:T(8,128)(2,1)S(1)}, bf16[4,8,24,128]{3,2,1,0:T(8,128)(2,1)S(1)}, u32[]{:S(2)}, u32[]{:S(2)}) collective-permute-start(bf16[4,8,24,128]{3,2,1,0:T(8,128)(2,1)S(1)} %get-tuple-element.32.refs_2_), channel_id=1, source_target_pairs={{0,1},{1,0},{2,3},{3,2},{4,5},{5,4},{6,7},{7,6},{8,9},{9,8},{10,11... | collective-permute-start | bytes 589832 | tf_op jit(solution)/shard_map/ppermute | solution.py:386
  5.9 0.0 copy-done.1
  5.9 0.1 copy-done.2
  6.0 0.3 %collective-permute-done.mate_ref = bf16[2,49,8,128]{3,2,1,0:T(8,128)(2,1)S(1)} collective-permute-done((bf16[2,49,8,128]{3,2,1,0:T(8,128)(2,1)S(1)}, bf16[2,49,8,128]{3,2,1,0:T(8,128)(2,1)S(1)}, u32[]{:S(2)}, u32[]{:S(2)}) %collective-permute-start) | collective-permute-done | bytes 200736 | tf_op jit(solution)/shard_map/ppermute | solution.py:386
  6.3 0.1 pack.1
  6.4 1.6 %collective-permute-start.1 = (bf16[37,8,128]{2,1,0:T(8,128)(2,1)S(1)}, bf16[37,8,128]{2,1,0:T(8,128)(2,1)S(1)}, u32[]{:S(2)}, u32[]{:S(2)}) collective-permute-start(bf16[37,8,128]{2,1,0:T(8,128)(2,1)S(1)} %get-tuple-element.28), channel_id=1, source_target_pairs={{0,4},{1,5},{2,6},{3,7},{4,0},{5,1},{6,2},{7,3},{8,12},{9,13},{10,... | collective-permute-start | bytes 227336 | tf_op jit(solution)/shard_map/ppermute | solution.py:432
  8.0 0.0 collective-permute-done.3.refs_3_.refs_0_
  8.0 0.0 collective-permute-start.2
  8.0 0.2 metric.1
  8.2 0.0 collective-permute-done.4.refs_4_.refs_1_
  8.2 0.0 collective-permute-done.5.refs_5_.refs_2_
  8.2 1.5 %inner.2 = (f32[4,3,4,24,128]{4,3,2,1,0:T(8,128)S(1)}, f32[4,3,4,24,128]{4,3,2,1,0:T(8,128)S(1)}, f32[4,24,128]{2,1,0:T(8,128)S(1)}) custom-call(bf16[4,8,24,128]{3,2,1,0:T(8,128)(2,1)S(1)} %get-tuple-element.30.refs_0_, bf16[4,8,24,128]{3,2,1,0:T(8,128)(2,1)S(1)} %get-tuple-element.31.refs_1_, bf16[4,8,24,128]{3,2,1,0:T(8,128)(2,1)S(1)} %get-tuple-element.32.refs_2_, ...), custom_call_target="tpu_custom_call" | custom-call | tf_op jit(solution)/shard_map/inner/pallas_call | solution.py:20
  9.8 1.1 %collective-permute-done.1 = bf16[37,8,128]{2,1,0:T(8,128)(2,1)S(1)} collective-permute-done((bf16[37,8,128]{2,1,0:T(8,128)(2,1)S(1)}, bf16[37,8,128]{2,1,0:T(8,128)(2,1)S(1)}, u32[]{:S(2)}, u32[]{:S(2)}) %collective-permute-start.1) | collective-permute-done | bytes 75808 | tf_op jit(solution)/shard_map/ppermute | solution.py:432
  10.9 0.0 collective-permute-done.2
  10.9 1.0 %collective-permute-done.6.got_ref = bf16[4,3,4,24,128]{4,3,2,1,0:T(8,128)(2,1)S(1)} collective-permute-done((bf16[4,3,4,24,128]{4,3,2,1,0:T(8,128)(2,1)S(1)}, bf16[4,3,4,24,128]{4,3,2,1,0:T(8,128)(2,1)S(1)}, u32[]{:S(2)}, u32[]{:S(2)}) %collective-permute-start.6) | collective-permute-done | bytes 294944 | tf_op jit(solution)/shard_map/ppermute | solution.py:398
  11.9 0.7 %cross.1 = (f32[8,128]{1,0:T(8,128)S(1)}, f32[8,128]{1,0:T(8,128)S(1)}, f32[8,128]{1,0:T(8,128)S(1)}) custom-call(f32[16,128]{1,0:T(8,128)S(1)} %convert_add_fusion.table_ref, f32[4,3,4,24,128]{4,3,2,1,0:T(8,128)S(1)} %get-tuple-element.39.part_ref, f32[4,3,4,24,128]{4,3,2,1,0:T(8,128)S(1)} %get-tuple-element.40.mate_part_ref, ...), custom_call_target="tpu_custom_call" | custom-call | tf_op jit(solution)/shard_map/cross/pallas_call | solution.py:20
  12.6 0.0 collective-permute-start.8
  12.6 1.8 %collective-permute-start.7 = (f32[8,128]{1,0:T(8,128)S(1)}, f32[8,128]{1,0:T(8,128)S(1)}, u32[]{:S(2)}, u32[]{:S(2)}) collective-permute-start(f32[8,128]{1,0:T(8,128)S(1)} %get-tuple-element.47), channel_id=1, source_target_pairs={{0,2},{1,3},{2,0},{3,1},{4,6},{5,7},{6,4},{7,5},{8,10},{9,11},{10,... | collective-permute-start | bytes 12296 | tf_op jit(solution)/shard_map/ppermute | solution.py:465
  14.4 0.8 %inner.3 = (f32[4,3,4,24,128]{4,3,2,1,0:T(8,128)S(1)}, f32[4,24,128]{2,1,0:T(8,128)S(1)}) custom-call(bf16[4,8,24,128]{3,2,1,0:T(8,128)(2,1)S(1)} %get-tuple-element.30.refs_0_, bf16[4,8,24,128]{3,2,1,0:T(8,128)(2,1)S(1)} %get-tuple-element.31.refs_1_, bf16[4,8,24,128]{3,2,1,0:T(8,128)(2,1)S(1)} %get-tuple-element.32.refs_2_, ...), custom_call_target="tpu_custom_call" | custom-call | tf_op jit(solution)/shard_map/inner/pallas_call | solution.py:20
  15.2 0.3 %edges.1 = (bf16[4,3,8,24,128]{4,3,2,1,0:T(8,128)(2,1)S(1)}, f32[4,2,8,128]{3,2,1,0:T(8,128)S(1)}) custom-call(f32[16,128]{1,0:T(8,128)S(1)} %convert_add_fusion.table_ref, f32[4,3,4,24,128]{4,3,2,1,0:T(8,128)S(1)} %get-tuple-element.39.part_ref, f32[4,3,4,24,128]{4,3,2,1,0:T(8,128)S(1)} %get-tuple-element.45.other_ref, ...), custom_call_target="tpu_custom_call" | custom-call | tf_op jit(solution)/shard_map/edges/pallas_call | solution.py:20
  15.5 0.4 %square.1 = f32[8,128]{1,0:T(8,128)S(1)} custom-call(bf16[4,8,24,128]{3,2,1,0:T(8,128)(2,1)S(1)} %get-tuple-element.30.refs_0_, bf16[4,8,24,128]{3,2,1,0:T(8,128)(2,1)S(1)} %get-tuple-element.31.refs_1_, bf16[4,8,24,128]{3,2,1,0:T(8,128)(2,1)S(1)} %get-tuple-element.32.refs_2_, bf16[4,3,8,24,128]{4,3,2,1,0:T(8,128)(2,1)S(1)} %get-tuple-element.46.refs_3_), custom_call_target="tpu_custom_call" | custom-call | tf_op jit(solution)/shard_map/square/pallas_call | solution.py:20
  15.9 0.5 %mates.1 = f32[8,128]{1,0:T(8,128)S(1)} custom-call(bf16[4,8,24,128]{3,2,1,0:T(8,128)(2,1)S(1)} %collective-permute-done.3.refs_3_.refs_0_, bf16[4,8,24,128]{3,2,1,0:T(8,128)(2,1)S(1)} %collective-permute-done.4.refs_4_.refs_1_, bf16[4,8,24,128]{3,2,1,0:T(8,128)(2,1)S(1)} %collective-permute-done.5.refs_5_.refs_2_, ...), custom_call_target="tpu_custom_call" | custom-call | tf_op jit(solution)/shard_map/mates/pallas_call | solution.py:20
  16.4 0.0 collective-permute-done.8
  16.4 0.0 collective-permute-done.7
  16.4 1.7 %collective-permute-start.9 = (f32[8,128]{1,0:T(8,128)S(1)}, f32[8,128]{1,0:T(8,128)S(1)}, u32[]{:S(2)}, u32[]{:S(2)}) collective-permute-start(f32[8,128]{1,0:T(8,128)S(1)} %add_add_fusion), channel_id=1, source_target_pairs={{0,4},{4,0},{8,12},{12,8},{1,5},{5,1},{9,13},{13,9},{2,6},{6,2},{1... | collective-permute-start | bytes 12296 | tf_op jit(solution)/shard_map/ppermute | solution.py:473
  18.1 2.0 %collective-permute-done.9 = f32[8,128]{1,0:T(8,128)S(1)} collective-permute-done((f32[8,128]{1,0:T(8,128)S(1)}, f32[8,128]{1,0:T(8,128)S(1)}, u32[]{:S(2)}, u32[]{:S(2)}) %collective-permute-start.9) | collective-permute-done | bytes 4128 | tf_op jit(solution)/shard_map/ppermute | solution.py:473
  20.1 2.9 %collective-permute-start.10 = (f32[8,128]{1,0:T(8,128)S(1)}, f32[8,128]{1,0:T(8,128)S(1)}, u32[]{:S(2)}, u32[]{:S(2)}) collective-permute-start(f32[8,128]{1,0:T(8,128)S(1)} %add.35), channel_id=1, source_target_pairs={{0,8},{4,12},{8,0},{12,4},{1,9},{5,13},{9,1},{13,5},{2,10},{6,14},... | collective-permute-start | bytes 12296 | tf_op jit(solution)/shard_map/ppermute | solution.py:473
  23.0 0.8 %profile.1 = f32[4,24]{1,0:T(4,128)} custom-call(f32[4,24,128]{2,1,0:T(8,128)S(1)} %get-tuple-element.49.energy_ref, f32[4,24,128]{2,1,0:T(8,128)S(1)} %get-tuple-element.50.other_ref, f32[4,2,8,128]{3,2,1,0:T(8,128)S(1)} %get-tuple-element.51.gain_ref), custom_call_target="tpu_custom_call" | custom-call | tf_op jit(solution)/shard_map/profile/pallas_call | solution.py:20
  23.8 0.8 %collective-permute-done.10 = f32[8,128]{1,0:T(8,128)S(1)} collective-permute-done((f32[8,128]{1,0:T(8,128)S(1)}, f32[8,128]{1,0:T(8,128)S(1)}, u32[]{:S(2)}, u32[]{:S(2)}) %collective-permute-start.10) | collective-permute-done | bytes 4128 | tf_op jit(solution)/shard_map/ppermute | solution.py:473
  24.6 0.6 %slice_multiply_fusion = f32[4,16]{1,0:T(4,128)} fusion(f32[8,128]{1,0:T(8,128)S(1)} %add.36), kind=kLoop, calls=%fused_computation.4 | loop fusion | flops 64 | bytes 512 | tf_op jit(solution)/shard_map/mul | solution.py:475
  (5 shorter events, 0.1 us)
Async XLA Ops:
  0.6 1.1 %copy-start = (bf16[4,3,8,24,128]{4,3,2,1,0:T(8,128)(2,1)S(1)}, bf16[4,3,8,24,128]{4,3,2,1,0:T(8,128)(2,1)}, u32[]{:S(2)}) copy-start(bf16[4,3,8,24,128]{4,3,2,1,0:T(8,128)(2,1)} %u_ref.1) | copy-start | bytes 1769476
  1.8 10.0 %collective-permute-start.6 = (bf16[4,3,4,24,128]{4,3,2,1,0:T(8,128)(2,1)S(1)}, bf16[4,3,4,24,128]{4,3,2,1,0:T(8,128)(2,1)S(1)}, u32[]{:S(2)}, u32[]{:S(2)}) collective-permute-start(bf16[4,3,4,24,128]{4,3,2,1,0:T(8,128)(2,1)S(1)} %get-tuple-element.38), channel_id=1, source_target_pairs={{0,2},{1,3},{2,0},{3,1},{4,6},{5,7},{6,4},{7,5},{8,10},{9,11},{10,... | collective-permute-start | bytes 884744 | tf_op jit(solution)/shard_map/ppermute | solution.py:398
  4.8 1.0 %copy-start.1 = (f32[8,128]{1,0:T(8,128)S(1)}, f32[8,128]{1,0:T(8,128)}, u32[]{:S(2)}) copy-start(f32[8,128]{1,0:T(8,128)} %param.5) | copy-start | bytes 12292
  4.8 1.4 %collective-permute-start = (bf16[2,49,8,128]{3,2,1,0:T(8,128)(2,1)S(1)}, bf16[2,49,8,128]{3,2,1,0:T(8,128)(2,1)S(1)}, u32[]{:S(2)}, u32[]{:S(2)}) collective-permute-start(bf16[2,49,8,128]{3,2,1,0:T(8,128)(2,1)S(1)} %get-tuple-element.27.own_ref), channel_id=1, source_target_pairs={{0,1},{1,0},{2,3},{3,2},{4,5},{5,4},{6,7},{7,6},{8,9},{9,8},{10,11... | collective-permute-start | bytes 602120 | tf_op jit(solution)/shard_map/ppermute | solution.py:386
  4.9 3.1 %collective-permute-start.3 = (bf16[4,8,24,128]{3,2,1,0:T(8,128)(2,1)S(1)}, bf16[4,8,24,128]{3,2,1,0:T(8,128)(2,1)S(1)}, u32[]{:S(2)}, u32[]{:S(2)}) collective-permute-start(bf16[4,8,24,128]{3,2,1,0:T(8,128)(2,1)S(1)} %get-tuple-element.30.refs_0_), channel_id=1, source_target_pairs={{0,1},{1,0},{2,3},{3,2},{4,5},{5,4},{6,7},{7,6},{8,9},{9,8},{10,11... | collective-permute-start | bytes 589832 | tf_op jit(solution)/shard_map/ppermute | solution.py:386
  5.4 2.8 %collective-permute-start.4 = (bf16[4,8,24,128]{3,2,1,0:T(8,128)(2,1)S(1)}, bf16[4,8,24,128]{3,2,1,0:T(8,128)(2,1)S(1)}, u32[]{:S(2)}, u32[]{:S(2)}) collective-permute-start(bf16[4,8,24,128]{3,2,1,0:T(8,128)(2,1)S(1)} %get-tuple-element.31.refs_1_), channel_id=1, source_target_pairs={{0,1},{1,0},{2,3},{3,2},{4,5},{5,4},{6,7},{7,6},{8,9},{9,8},{10,11... | collective-permute-start | bytes 589832 | tf_op jit(solution)/shard_map/ppermute | solution.py:386
  5.4 0.7 %copy-start.2 = (s32[24]{0:T(128)S(1)}, s32[24]{0:T(128)}, u32[]{:S(2)}) copy-start(s32[24]{0:T(128)} %param.4) | copy-start | bytes 292
  5.4 2.9 %collective-permute-start.5 = (bf16[4,8,24,128]{3,2,1,0:T(8,128)(2,1)S(1)}, bf16[4,8,24,128]{3,2,1,0:T(8,128)(2,1)S(1)}, u32[]{:S(2)}, u32[]{:S(2)}) collective-permute-start(bf16[4,8,24,128]{3,2,1,0:T(8,128)(2,1)S(1)} %get-tuple-element.32.refs_2_), channel_id=1, source_target_pairs={{0,1},{1,0},{2,3},{3,2},{4,5},{5,4},{6,7},{7,6},{8,9},{9,8},{10,11... | collective-permute-start | bytes 589832 | tf_op jit(solution)/shard_map/ppermute | solution.py:386
  6.4 4.5 %collective-permute-start.1 = (bf16[37,8,128]{2,1,0:T(8,128)(2,1)S(1)}, bf16[37,8,128]{2,1,0:T(8,128)(2,1)S(1)}, u32[]{:S(2)}, u32[]{:S(2)}) collective-permute-start(bf16[37,8,128]{2,1,0:T(8,128)(2,1)S(1)} %get-tuple-element.28), channel_id=1, source_target_pairs={{0,4},{1,5},{2,6},{3,7},{4,0},{5,1},{6,2},{7,3},{8,12},{9,13},{10,... | collective-permute-start | bytes 227336 | tf_op jit(solution)/shard_map/ppermute | solution.py:432
  8.0 2.9 %collective-permute-start.2 = (bf16[37,8,128]{2,1,0:T(8,128)(2,1)S(1)}, bf16[37,8,128]{2,1,0:T(8,128)(2,1)S(1)}, u32[]{:S(2)}, u32[]{:S(2)}) collective-permute-start(bf16[37,8,128]{2,1,0:T(8,128)(2,1)S(1)} %get-tuple-element.29), channel_id=1, source_target_pairs={{0,1},{1,0},{2,3},{3,2},{4,8},{5,9},{6,10},{7,11},{8,4},{9,5},{10,... | collective-permute-start | bytes 227336 | tf_op jit(solution)/shard_map/ppermute | solution.py:432
  12.6 3.8 %collective-permute-start.8 = (f32[8,128]{1,0:T(8,128)S(1)}, f32[8,128]{1,0:T(8,128)S(1)}, u32[]{:S(2)}, u32[]{:S(2)}) collective-permute-start(f32[8,128]{1,0:T(8,128)S(1)} %get-tuple-element.48), channel_id=1, source_target_pairs={{0,1},{1,0},{2,3},{3,2},{4,5},{5,4},{6,7},{7,6},{8,9},{9,8},{10,11... | collective-permute-start | bytes 12296 | tf_op jit(solution)/shard_map/ppermute | solution.py:386
  12.6 3.8 %collective-permute-start.7 = (f32[8,128]{1,0:T(8,128)S(1)}, f32[8,128]{1,0:T(8,128)S(1)}, u32[]{:S(2)}, u32[]{:S(2)}) collective-permute-start(f32[8,128]{1,0:T(8,128)S(1)} %get-tuple-element.47), channel_id=1, source_target_pairs={{0,2},{1,3},{2,0},{3,1},{4,6},{5,7},{6,4},{7,5},{8,10},{9,11},{10,... | collective-permute-start | bytes 12296 | tf_op jit(solution)/shard_map/ppermute | solution.py:465
  16.4 3.7 %collective-permute-start.9 = (f32[8,128]{1,0:T(8,128)S(1)}, f32[8,128]{1,0:T(8,128)S(1)}, u32[]{:S(2)}, u32[]{:S(2)}) collective-permute-start(f32[8,128]{1,0:T(8,128)S(1)} %add_add_fusion), channel_id=1, source_target_pairs={{0,4},{4,0},{8,12},{12,8},{1,5},{5,1},{9,13},{13,9},{2,6},{6,2},{1... | collective-permute-start | bytes 12296 | tf_op jit(solution)/shard_map/ppermute | solution.py:473
  20.1 4.5 %collective-permute-start.10 = (f32[8,128]{1,0:T(8,128)S(1)}, f32[8,128]{1,0:T(8,128)S(1)}, u32[]{:S(2)}, u32[]{:S(2)}) collective-permute-start(f32[8,128]{1,0:T(8,128)S(1)} %add.35), channel_id=1, source_target_pairs={{0,8},{4,12},{8,0},{12,4},{1,9},{5,13},{9,1},{13,5},{2,10},{6,14},... | collective-permute-start | bytes 12296 | tf_op jit(solution)/shard_map/ppermute | solution.py:473

commit v6 on v5

--- a/solution.py
+++ b/solution.py
@@ -468,10 +468,10 @@
         gram = lax.psum(total, "space")
     else:
         gram = total
-        step = 1
-        while step < spaces:
+        step = spaces // 2
+        while step:
             gram = gram + lax.ppermute(gram, "space", [(i, i ^ step) for i in range(spaces)])
-            step *= 2
+            step //= 2
     gram = gram[:snaps, : snaps * cores] * (1.0 / (planes * rows * spaces * span))
     return gram, profile
 

time: 25.3 us -> 25.3 us (level)
  no operation moved by 1% of the time
where the time goes in v6:
time: 25.3 us; the launch traced here: 25.2 us
  starting transfers between devices  12.1 us (48%)
  Pallas kernels  5.34 us (21%)
  waiting for transfers between devices  5.18 us (20%)
  local copies, waits for them, and re-layouts  1.21 us (5%)
  between operations  0.73 us (3%)
  other arithmetic  0.65 us (3%)
    pallas_call x10, Pallas kernels, run(): pl.pallas_call(kernel, name=name, out_shape=out_shape, in_specs=[VMEM] *...  5.34 us
    ppermute x2, starting transfers between devices, local(): lax.ppermute(gram, 'space', [(i, i ^ step) for i in range(spaces)])  4.6 us
    ppermute x1, starting transfers between devices, local(): lax.ppermute(piece, 'snap', [(i, (i + 2 * k) % cores) for i in range(core...  3 us
    ppermute x2, waiting for transfers between devices, local(): lax.ppermute(gram, 'space', [(i, i ^ step) for i in range(spaces)])  2.8 us
    ppermute x1, starting transfers between devices, local(): lax.ppermute(back[k - 1], 'snap', [(i, (i - 2 * k) % cores) for i in rang...  1.82 us
    ppermute x2, starting transfers between devices, swap(): return lax.ppermute(array, ('space', 'snap'), pairs)  1.6 us
    unnamed x6, local copies, waits for them, and re-layouts  1.21 us
    ppermute x2, waiting for transfers between devices, swap(): return lax.ppermute(array, ('space', 'snap'), pairs)  1.12 us
  transfers between devices with their start and end apart: 11, of which 5 were waited for; matrix products, arithmetic and copies ran while one was open for 0% of the time, Pallas kernels for 18%

profile of v6, /device:TPU:0, one launch (start us, length us, event | category | flops | bytes accessed | tf_op | source)
XLA Modules:
  0.0 25.2 jit_solution(3312711210469313829)
XLA Ops:
  0.6 0.0 copy-start
  0.6 1.1 %copy-done = bf16[4,3,8,24,128]{4,3,2,1,0:T(8,128)(2,1)S(1)} copy-done((bf16[4,3,8,24,128]{4,3,2,1,0:T(8,128)(2,1)S(1)}, bf16[4,3,8,24,128]{4,3,2,1,0:T(8,128)(2,1)}, u32[]{:S(2)}) %copy-start) | copy-done | bytes 589848
  1.7 0.1 piece.1
  1.8 3.0 %collective-permute-start.6 = (bf16[4,3,4,24,128]{4,3,2,1,0:T(8,128)(2,1)S(1)}, bf16[4,3,4,24,128]{4,3,2,1,0:T(8,128)(2,1)S(1)}, u32[]{:S(2)}, u32[]{:S(2)}) collective-permute-start(bf16[4,3,4,24,128]{4,3,2,1,0:T(8,128)(2,1)S(1)} %get-tuple-element.38), channel_id=1, source_target_pairs={{0,2},{1,3},{2,0},{3,1},{4,6},{5,7},{6,4},{7,5},{8,10},{9,11},{10,... | collective-permute-start | bytes 884744 | tf_op jit(solution)/shard_map/ppermute | solution.py:398
  4.8 0.0 copy-start.1
  4.8 0.0 collective-permute-start
  4.9 0.5 %collective-permute-start.3 = (bf16[4,8,24,128]{3,2,1,0:T(8,128)(2,1)S(1)}, bf16[4,8,24,128]{3,2,1,0:T(8,128)(2,1)S(1)}, u32[]{:S(2)}, u32[]{:S(2)}) collective-permute-start(bf16[4,8,24,128]{3,2,1,0:T(8,128)(2,1)S(1)} %get-tuple-element.30.refs_0_), channel_id=1, source_target_pairs={{0,1},{1,0},{2,3},{3,2},{4,5},{5,4},{6,7},{7,6},{8,9},{9,8},{10,11... | collective-permute-start | bytes 589832 | tf_op jit(solution)/shard_map/ppermute | solution.py:386
  5.4 0.0 collective-permute-start.4
  5.4 0.0 copy-start.2
  5.4 0.5 %collective-permute-start.5 = (bf16[4,8,24,128]{3,2,1,0:T(8,128)(2,1)S(1)}, bf16[4,8,24,128]{3,2,1,0:T(8,128)(2,1)S(1)}, u32[]{:S(2)}, u32[]{:S(2)}) collective-permute-start(bf16[4,8,24,128]{3,2,1,0:T(8,128)(2,1)S(1)} %get-tuple-element.32.refs_2_), channel_id=1, source_target_pairs={{0,1},{1,0},{2,3},{3,2},{4,5},{5,4},{6,7},{7,6},{8,9},{9,8},{10,11... | collective-permute-start | bytes 589832 | tf_op jit(solution)/shard_map/ppermute | solution.py:386
  5.9 0.0 copy-done.1
  5.9 0.1 copy-done.2
  6.0 0.3 %collective-permute-done.mate_ref = bf16[2,49,8,128]{3,2,1,0:T(8,128)(2,1)S(1)} collective-permute-done((bf16[2,49,8,128]{3,2,1,0:T(8,128)(2,1)S(1)}, bf16[2,49,8,128]{3,2,1,0:T(8,128)(2,1)S(1)}, u32[]{:S(2)}, u32[]{:S(2)}) %collective-permute-start) | collective-permute-done | bytes 200736 | tf_op jit(solution)/shard_map/ppermute | solution.py:386
  6.3 0.1 pack.1
  6.4 1.6 %collective-permute-start.1 = (bf16[37,8,128]{2,1,0:T(8,128)(2,1)S(1)}, bf16[37,8,128]{2,1,0:T(8,128)(2,1)S(1)}, u32[]{:S(2)}, u32[]{:S(2)}) collective-permute-start(bf16[37,8,128]{2,1,0:T(8,128)(2,1)S(1)} %get-tuple-element.28), channel_id=1, source_target_pairs={{0,4},{1,5},{2,6},{3,7},{4,0},{5,1},{6,2},{7,3},{8,12},{9,13},{10,... | collective-permute-start | bytes 227336 | tf_op jit(solution)/shard_map/ppermute | solution.py:432
  8.0 0.0 collective-permute-done.3.refs_3_.refs_0_
  8.0 0.0 collective-permute-start.2
  8.0 0.2 metric.1
  8.2 0.0 collective-permute-done.4.refs_4_.refs_1_
  8.2 0.0 collective-permute-done.5.refs_5_.refs_2_
  8.2 1.5 %inner.2 = (f32[4,3,4,24,128]{4,3,2,1,0:T(8,128)S(1)}, f32[4,3,4,24,128]{4,3,2,1,0:T(8,128)S(1)}, f32[4,24,128]{2,1,0:T(8,128)S(1)}) custom-call(bf16[4,8,24,128]{3,2,1,0:T(8,128)(2,1)S(1)} %get-tuple-element.30.refs_0_, bf16[4,8,24,128]{3,2,1,0:T(8,128)(2,1)S(1)} %get-tuple-element.31.refs_1_, bf16[4,8,24,128]{3,2,1,0:T(8,128)(2,1)S(1)} %get-tuple-element.32.refs_2_, ...), custom_call_target="tpu_custom_call" | custom-call | tf_op jit(solution)/shard_map/inner/pallas_call | solution.py:20
  9.8 1.1 %collective-permute-done.1 = bf16[37,8,128]{2,1,0:T(8,128)(2,1)S(1)} collective-permute-done((bf16[37,8,128]{2,1,0:T(8,128)(2,1)S(1)}, bf16[37,8,128]{2,1,0:T(8,128)(2,1)S(1)}, u32[]{:S(2)}, u32[]{:S(2)}) %collective-permute-start.1) | collective-permute-done | bytes 75808 | tf_op jit(solution)/shard_map/ppermute | solution.py:432
  10.9 0.0 collective-permute-done.2
  10.9 1.0 %collective-permute-done.6.got_ref = bf16[4,3,4,24,128]{4,3,2,1,0:T(8,128)(2,1)S(1)} collective-permute-done((bf16[4,3,4,24,128]{4,3,2,1,0:T(8,128)(2,1)S(1)}, bf16[4,3,4,24,128]{4,3,2,1,0:T(8,128)(2,1)S(1)}, u32[]{:S(2)}, u32[]{:S(2)}) %collective-permute-start.6) | collective-permute-done | bytes 294944 | tf_op jit(solution)/shard_map/ppermute | solution.py:398
  11.9 0.7 %cross.1 = (f32[8,128]{1,0:T(8,128)S(1)}, f32[8,128]{1,0:T(8,128)S(1)}, f32[8,128]{1,0:T(8,128)S(1)}) custom-call(f32[16,128]{1,0:T(8,128)S(1)} %convert_add_fusion.table_ref, f32[4,3,4,24,128]{4,3,2,1,0:T(8,128)S(1)} %get-tuple-element.39.part_ref, f32[4,3,4,24,128]{4,3,2,1,0:T(8,128)S(1)} %get-tuple-element.40.mate_part_ref, ...), custom_call_target="tpu_custom_call" | custom-call | tf_op jit(solution)/shard_map/cross/pallas_call | solution.py:20
  12.6 0.0 collective-permute-start.8
  12.6 1.8 %collective-permute-start.7 = (f32[8,128]{1,0:T(8,128)S(1)}, f32[8,128]{1,0:T(8,128)S(1)}, u32[]{:S(2)}, u32[]{:S(2)}) collective-permute-start(f32[8,128]{1,0:T(8,128)S(1)} %get-tuple-element.47), channel_id=1, source_target_pairs={{0,2},{1,3},{2,0},{3,1},{4,6},{5,7},{6,4},{7,5},{8,10},{9,11},{10,... | collective-permute-start | bytes 12296 | tf_op jit(solution)/shard_map/ppermute | solution.py:465
  14.4 0.8 %inner.3 = (f32[4,3,4,24,128]{4,3,2,1,0:T(8,128)S(1)}, f32[4,24,128]{2,1,0:T(8,128)S(1)}) custom-call(bf16[4,8,24,128]{3,2,1,0:T(8,128)(2,1)S(1)} %get-tuple-element.30.refs_0_, bf16[4,8,24,128]{3,2,1,0:T(8,128)(2,1)S(1)} %get-tuple-element.31.refs_1_, bf16[4,8,24,128]{3,2,1,0:T(8,128)(2,1)S(1)} %get-tuple-element.32.refs_2_, ...), custom_call_target="tpu_custom_call" | custom-call | tf_op jit(solution)/shard_map/inner/pallas_call | solution.py:20
  15.2 0.3 %edges.1 = (bf16[4,3,8,24,128]{4,3,2,1,0:T(8,128)(2,1)S(1)}, f32[4,2,8,128]{3,2,1,0:T(8,128)S(1)}) custom-call(f32[16,128]{1,0:T(8,128)S(1)} %convert_add_fusion.table_ref, f32[4,3,4,24,128]{4,3,2,1,0:T(8,128)S(1)} %get-tuple-element.39.part_ref, f32[4,3,4,24,128]{4,3,2,1,0:T(8,128)S(1)} %get-tuple-element.45.other_ref, ...), custom_call_target="tpu_custom_call" | custom-call | tf_op jit(solution)/shard_map/edges/pallas_call | solution.py:20
  15.5 0.4 %square.1 = f32[8,128]{1,0:T(8,128)S(1)} custom-call(bf16[4,8,24,128]{3,2,1,0:T(8,128)(2,1)S(1)} %get-tuple-element.30.refs_0_, bf16[4,8,24,128]{3,2,1,0:T(8,128)(2,1)S(1)} %get-tuple-element.31.refs_1_, bf16[4,8,24,128]{3,2,1,0:T(8,128)(2,1)S(1)} %get-tuple-element.32.refs_2_, bf16[4,3,8,24,128]{4,3,2,1,0:T(8,128)(2,1)S(1)} %get-tuple-element.46.refs_3_), custom_call_target="tpu_custom_call" | custom-call | tf_op jit(solution)/shard_map/square/pallas_call | solution.py:20
  15.9 0.5 %mates.1 = f32[8,128]{1,0:T(8,128)S(1)} custom-call(bf16[4,8,24,128]{3,2,1,0:T(8,128)(2,1)S(1)} %collective-permute-done.3.refs_3_.refs_0_, bf16[4,8,24,128]{3,2,1,0:T(8,128)(2,1)S(1)} %collective-permute-done.4.refs_4_.refs_1_, bf16[4,8,24,128]{3,2,1,0:T(8,128)(2,1)S(1)} %collective-permute-done.5.refs_5_.refs_2_, ...), custom_call_target="tpu_custom_call" | custom-call | tf_op jit(solution)/shard_map/mates/pallas_call | solution.py:20
  16.4 0.0 collective-permute-done.8
  16.4 0.0 collective-permute-done.7
  16.4 3.0 %collective-permute-start.9 = (f32[8,128]{1,0:T(8,128)S(1)}, f32[8,128]{1,0:T(8,128)S(1)}, u32[]{:S(2)}, u32[]{:S(2)}) collective-permute-start(f32[8,128]{1,0:T(8,128)S(1)} %add_add_fusion), channel_id=1, source_target_pairs={{0,8},{4,12},{8,0},{12,4},{1,9},{5,13},{9,1},{13,5},{2,10},{6,14},... | collective-permute-start | bytes 12296 | tf_op jit(solution)/shard_map/ppermute | solution.py:473
  19.4 1.6 %collective-permute-done.9 = f32[8,128]{1,0:T(8,128)S(1)} collective-permute-done((f32[8,128]{1,0:T(8,128)S(1)}, f32[8,128]{1,0:T(8,128)S(1)}, u32[]{:S(2)}, u32[]{:S(2)}) %collective-permute-start.9) | collective-permute-done | bytes 4128 | tf_op jit(solution)/shard_map/ppermute | solution.py:473
  21.0 1.6 %collective-permute-start.10 = (f32[8,128]{1,0:T(8,128)S(1)}, f32[8,128]{1,0:T(8,128)S(1)}, u32[]{:S(2)}, u32[]{:S(2)}) collective-permute-start(f32[8,128]{1,0:T(8,128)S(1)} %add.35), channel_id=1, source_target_pairs={{0,4},{4,0},{8,12},{12,8},{1,5},{5,1},{9,13},{13,9},{2,6},{6,2},{1... | collective-permute-start | bytes 12296 | tf_op jit(solution)/shard_map/ppermute | solution.py:473
  22.6 0.8 %profile.1 = f32[4,24]{1,0:T(4,128)} custom-call(f32[4,24,128]{2,1,0:T(8,128)S(1)} %get-tuple-element.49.energy_ref, f32[4,24,128]{2,1,0:T(8,128)S(1)} %get-tuple-element.50.other_ref, f32[4,2,8,128]{3,2,1,0:T(8,128)S(1)} %get-tuple-element.51.gain_ref), custom_call_target="tpu_custom_call" | custom-call | tf_op jit(solution)/shard_map/profile/pallas_call | solution.py:20
  23.4 1.2 %collective-permute-done.10 = f32[8,128]{1,0:T(8,128)S(1)} collective-permute-done((f32[8,128]{1,0:T(8,128)S(1)}, f32[8,128]{1,0:T(8,128)S(1)}, u32[]{:S(2)}, u32[]{:S(2)}) %collective-permute-start.10) | collective-permute-done | bytes 4128 | tf_op jit(solution)/shard_map/ppermute | solution.py:473
  24.6 0.6 %slice_multiply_fusion = f32[4,16]{1,0:T(4,128)} fusion(f32[8,128]{1,0:T(8,128)S(1)} %add.36), kind=kLoop, calls=%fused_computation.4 | loop fusion | flops 64 | bytes 512 | tf_op jit(solution)/shard_map/mul | solution.py:475
  (5 shorter events, 0.1 us)
Async XLA Ops:
  0.6 1.1 %copy-start = (bf16[4,3,8,24,128]{4,3,2,1,0:T(8,128)(2,1)S(1)}, bf16[4,3,8,24,128]{4,3,2,1,0:T(8,128)(2,1)}, u32[]{:S(2)}) copy-start(bf16[4,3,8,24,128]{4,3,2,1,0:T(8,128)(2,1)} %u_ref.1) | copy-start | bytes 1769476
  1.8 10.0 %collective-permute-start.6 = (bf16[4,3,4,24,128]{4,3,2,1,0:T(8,128)(2,1)S(1)}, bf16[4,3,4,24,128]{4,3,2,1,0:T(8,128)(2,1)S(1)}, u32[]{:S(2)}, u32[]{:S(2)}) collective-permute-start(bf16[4,3,4,24,128]{4,3,2,1,0:T(8,128)(2,1)S(1)} %get-tuple-element.38), channel_id=1, source_target_pairs={{0,2},{1,3},{2,0},{3,1},{4,6},{5,7},{6,4},{7,5},{8,10},{9,11},{10,... | collective-permute-start | bytes 884744 | tf_op jit(solution)/shard_map/ppermute | solution.py:398
  4.8 1.0 %copy-start.1 = (f32[8,128]{1,0:T(8,128)S(1)}, f32[8,128]{1,0:T(8,128)}, u32[]{:S(2)}) copy-start(f32[8,128]{1,0:T(8,128)} %param.5) | copy-start | bytes 12292
  4.8 1.4 %collective-permute-start = (bf16[2,49,8,128]{3,2,1,0:T(8,128)(2,1)S(1)}, bf16[2,49,8,128]{3,2,1,0:T(8,128)(2,1)S(1)}, u32[]{:S(2)}, u32[]{:S(2)}) collective-permute-start(bf16[2,49,8,128]{3,2,1,0:T(8,128)(2,1)S(1)} %get-tuple-element.27.own_ref), channel_id=1, source_target_pairs={{0,1},{1,0},{2,3},{3,2},{4,5},{5,4},{6,7},{7,6},{8,9},{9,8},{10,11... | collective-permute-start | bytes 602120 | tf_op jit(solution)/shard_map/ppermute | solution.py:386
  4.9 3.1 %collective-permute-start.3 = (bf16[4,8,24,128]{3,2,1,0:T(8,128)(2,1)S(1)}, bf16[4,8,24,128]{3,2,1,0:T(8,128)(2,1)S(1)}, u32[]{:S(2)}, u32[]{:S(2)}) collective-permute-start(bf16[4,8,24,128]{3,2,1,0:T(8,128)(2,1)S(1)} %get-tuple-element.30.refs_0_), channel_id=1, source_target_pairs={{0,1},{1,0},{2,3},{3,2},{4,5},{5,4},{6,7},{7,6},{8,9},{9,8},{10,11... | collective-permute-start | bytes 589832 | tf_op jit(solution)/shard_map/ppermute | solution.py:386
  5.4 2.8 %collective-permute-start.4 = (bf16[4,8,24,128]{3,2,1,0:T(8,128)(2,1)S(1)}, bf16[4,8,24,128]{3,2,1,0:T(8,128)(2,1)S(1)}, u32[]{:S(2)}, u32[]{:S(2)}) collective-permute-start(bf16[4,8,24,128]{3,2,1,0:T(8,128)(2,1)S(1)} %get-tuple-element.31.refs_1_), channel_id=1, source_target_pairs={{0,1},{1,0},{2,3},{3,2},{4,5},{5,4},{6,7},{7,6},{8,9},{9,8},{10,11... | collective-permute-start | bytes 589832 | tf_op jit(solution)/shard_map/ppermute | solution.py:386
  5.4 0.7 %copy-start.2 = (s32[24]{0:T(128)S(1)}, s32[24]{0:T(128)}, u32[]{:S(2)}) copy-start(s32[24]{0:T(128)} %param.4) | copy-start | bytes 292
  5.4 2.9 %collective-permute-start.5 = (bf16[4,8,24,128]{3,2,1,0:T(8,128)(2,1)S(1)}, bf16[4,8,24,128]{3,2,1,0:T(8,128)(2,1)S(1)}, u32[]{:S(2)}, u32[]{:S(2)}) collective-permute-start(bf16[4,8,24,128]{3,2,1,0:T(8,128)(2,1)S(1)} %get-tuple-element.32.refs_2_), channel_id=1, source_target_pairs={{0,1},{1,0},{2,3},{3,2},{4,5},{5,4},{6,7},{7,6},{8,9},{9,8},{10,11... | collective-permute-start | bytes 589832 | tf_op jit(solution)/shard_map/ppermute | solution.py:386
  6.4 4.5 %collective-permute-start.1 = (bf16[37,8,128]{2,1,0:T(8,128)(2,1)S(1)}, bf16[37,8,128]{2,1,0:T(8,128)(2,1)S(1)}, u32[]{:S(2)}, u32[]{:S(2)}) collective-permute-start(bf16[37,8,128]{2,1,0:T(8,128)(2,1)S(1)} %get-tuple-element.28), channel_id=1, source_target_pairs={{0,4},{1,5},{2,6},{3,7},{4,0},{5,1},{6,2},{7,3},{8,12},{9,13},{10,... | collective-permute-start | bytes 227336 | tf_op jit(solution)/shard_map/ppermute | solution.py:432
  8.0 2.9 %collective-permute-start.2 = (bf16[37,8,128]{2,1,0:T(8,128)(2,1)S(1)}, bf16[37,8,128]{2,1,0:T(8,128)(2,1)S(1)}, u32[]{:S(2)}, u32[]{:S(2)}) collective-permute-start(bf16[37,8,128]{2,1,0:T(8,128)(2,1)S(1)} %get-tuple-element.29), channel_id=1, source_target_pairs={{0,1},{1,0},{2,3},{3,2},{4,8},{5,9},{6,10},{7,11},{8,4},{9,5},{10,... | collective-permute-start | bytes 227336 | tf_op jit(solution)/shard_map/ppermute | solution.py:432
  12.6 3.8 %collective-permute-start.8 = (f32[8,128]{1,0:T(8,128)S(1)}, f32[8,128]{1,0:T(8,128)S(1)}, u32[]{:S(2)}, u32[]{:S(2)}) collective-permute-start(f32[8,128]{1,0:T(8,128)S(1)} %get-tuple-element.48), channel_id=1, source_target_pairs={{0,1},{1,0},{2,3},{3,2},{4,5},{5,4},{6,7},{7,6},{8,9},{9,8},{10,11... | collective-permute-start | bytes 12296 | tf_op jit(solution)/shard_map/ppermute | solution.py:386
  12.6 3.8 %collective-permute-start.7 = (f32[8,128]{1,0:T(8,128)S(1)}, f32[8,128]{1,0:T(8,128)S(1)}, u32[]{:S(2)}, u32[]{:S(2)}) collective-permute-start(f32[8,128]{1,0:T(8,128)S(1)} %get-tuple-element.47), channel_id=1, source_target_pairs={{0,2},{1,3},{2,0},{3,1},{4,6},{5,7},{6,4},{7,5},{8,10},{9,11},{10,... | collective-permute-start | bytes 12296 | tf_op jit(solution)/shard_map/ppermute | solution.py:465
  16.4 4.6 %collective-permute-start.9 = (f32[8,128]{1,0:T(8,128)S(1)}, f32[8,128]{1,0:T(8,128)S(1)}, u32[]{:S(2)}, u32[]{:S(2)}) collective-permute-start(f32[8,128]{1,0:T(8,128)S(1)} %add_add_fusion), channel_id=1, source_target_pairs={{0,8},{4,12},{8,0},{12,4},{1,9},{5,13},{9,1},{13,5},{2,10},{6,14},... | collective-permute-start | bytes 12296 | tf_op jit(solution)/shard_map/ppermute | solution.py:473
  21.0 3.6 %collective-permute-start.10 = (f32[8,128]{1,0:T(8,128)S(1)}, f32[8,128]{1,0:T(8,128)S(1)}, u32[]{:S(2)}, u32[]{:S(2)}) collective-permute-start(f32[8,128]{1,0:T(8,128)S(1)} %add.35), channel_id=1, source_target_pairs={{0,4},{4,0},{8,12},{12,8},{1,5},{5,1},{9,13},{13,9},{2,6},{6,2},{1... | collective-permute-start | bytes 12296 | tf_op jit(solution)/shard_map/ppermute | solution.py:473

commit v7 on v6

--- a/solution.py
+++ b/solution.py
@@ -73,10 +73,10 @@
     chips = len(pieces) + 1
     chip = lax.axis_index("snap") // 2
     for k, piece in enumerate(pieces):
-        start = jnp.where((chip + k + 1) % chips < chip, 0, half)
+        start = jnp.where((chip + k + 1) % chips < chip, 0, half - 1)
         for a in range(snaps):
             for c in range(comps):
-                for i in range(half):
+                for i in range(half + 1):
                     piece[a, c, i] = u_ref[a, c, start + i]
     for c in range(comps):
         components[c][...] = u_ref[:, c]
@@ -139,6 +139,7 @@
     sources = [Components(refs[i * comps : (i + 1) * comps]) for i in range(cores)]
     metric_ref, volume_ref, operator_ref, *parts, energy_ref, f_ref, e_ref = refs[cores * comps :]
     snaps, _, half, rows, span = parts[0].shape
+    half -= 1
     planes = 2 * half
     first, end = ROWS, ROWS + rows
     row = sublane((rows, span))
@@ -155,12 +156,10 @@
                 raw = source[a, c][start : start + half]
                 spanned = jnp.dot(raw.reshape(half * rows, span), operator_ref[...], preferred_element_type=F32)
                 spanned = spanned.reshape(half, rows, span)
-                u = {
-                    p: source[a, c, p].astype(F32)
-                    for p in range(max(start - 2, 0), min(start + half + 2, planes))
-                }
+                begin = max(start - 1, 0)
+                u = {p: source[a, c, p].astype(F32) for p in range(begin, begin + half + 1)}
                 stream = {}
-                for i in range(max(start - 1, 0), min(start + half + 1, planes)):
+                for i in range(start, start + half):
                     lo, hi = max(i - 1, 0), min(i + 1, planes - 1)
                     edge = (volume_ref[i] * (0.25 / (hi - lo) ** 2)) * (u[hi] - u[lo])
                     stream[hi] = stream[hi] + edge if hi in stream else edge
@@ -175,7 +174,11 @@
                     if own:
                         total = total + (u[p] * partial + edge * jump)
                     normal = e_ref[i, first - 1 : end - 1, :] - e_ref[i, first + 1 : end + 1, :]
-                    part_ref[a, c, i] = partial + normal
+                    part_ref[a, c, p - begin] = partial + normal
+                (beyond,) = [p for p in u if not start <= p < start + half]
+                part_ref[a, c, beyond - begin] = stream[beyond]
+                if own:
+                    total = total + u[beyond] * stream[beyond]
             if own:
                 energy_ref[a] = total
             return carry
@@ -235,7 +238,8 @@
     zero = jnp.zeros((ROWS, span), F32)
     sums = [[zero, zero] for _ in range(snaps)]
     for c in range(comps):
-        for ref, begin in ((part_ref, start), (other_ref, half - start)):
+        for ref, beside, begin in ((part_ref, other_ref, start), (other_ref, part_ref, half - start)):
+            first = begin == 0
             for i in range(half):
                 p = begin + i
                 scale = scale_ref[p, 0], scale_ref[p, 1]
@@ -243,7 +247,11 @@
                 for a in range(snaps):
                     edges = edges_at(scale, u_ref[a, c, p].astype(F32), low, high, a)
                     sums[a] = [x + y for x, y in zip(sums[a], edges[2:])]
-                    part = ref[a, c, i]
+                    part = ref[a, c, i + jnp.where(first, 0, 1)]
+                    if i == 0:
+                        part = part + jnp.where(first, 0.0, beside[a, c, half])
+                    if i == half - 1:
+                        part = part + jnp.where(first, beside[a, c, 0], 0.0)
                     w_ref[a, c, p] = jnp.concatenate(
                         [part[0:ROWS] + edges[0], part[ROWS : rows - ROWS], part[rows - ROWS :] + edges[1]], axis=0
                     ).astype(BF16)
@@ -323,6 +331,7 @@
     comps = part_ref.shape[1]
     u_ref, mate_ref = Components(refs[:comps]), Components(refs[comps:-4])
     snaps, comps, half, rows, span = got_ref.shape
+    half -= 1
     planes = 2 * half
     count = comps * planes
     group = ROWS // snaps
@@ -335,10 +344,14 @@
     pairs = [(i, j) for i in range(2 * snaps) for j in range(snaps)]
     sums = [jnp.zeros((ROWS, span), F32) for _ in pairs]
     for c in range(comps):
-        for i in range(half):
-            p = start + i
+        for i in range(half + 1):
+            p = jnp.where(start == 0, 0, half - 1) + i
             scale = scale_ref[p, 0], scale_ref[p, 1]
-            at_mate = count + c * mate_planes + (p if mate_planes == planes else i)
+            if i in (0, half):
+                inside = (start == 0) == (i == 0)
+                scale = [jnp.where(inside, x, 0.0) for x in scale]
+            at = p if mate_planes == planes else jnp.clip(p - start, 0, half - 1)
+            at_mate = count + c * mate_planes + at
             left = []
             for u, part, at in ((u_ref, part_ref, c * planes + p), (mate_ref, mate_part_ref, at_mate)):
                 low, high = low_ref[at].astype(F32), high_ref[at].astype(F32)
@@ -385,7 +398,7 @@
     def to_mate(array):
         return lax.ppermute(array, "snap", [(i, i ^ 1) for i in range(cores)])
 
-    piece = shape(snaps, comps, half, rows, span)
+    piece = shape(snaps, comps, half + 1, rows, span)
     component = shape(snaps, planes, rows, span)
     tiles = max(comps * planes, snaps * planes * rows // ROWS // 2 + 1)
     edge_rows, *pieces = call(
@@ -408,7 +421,7 @@
     scratch = [pltpu.VMEM((half, rows + 2 * ROWS, span), F32)] * 2
 
     def inner(other, *velocities):
-        parts = [shape(snaps, comps, half, rows, span, dtype=F32)] * len(velocities)
+        parts = [shape(snaps, comps, half + 1, rows, span, dtype=F32)] * len(velocities)
         return call(
             functools.partial(inner_kernel, comps, other, len(velocities)),
             "inner",

time: 25.3 us -> 27.1 us (1.071)
  waiting for transfers between devices: 5.18 us -> 7.09 us
  starting transfers between devices: 12.1 us -> 11.7 us
    ppermute x1, waiting for transfers between devices: 0.97 us -> 2.55 us  [local(): lax.ppermute(piece, 'snap', [(i, (i + 2 * k) % cores) for i in range(core...]
    ppermute x2, starting transfers between devices: 4.6 us -> 4.27 us  [local(): lax.ppermute(gram, 'space', [(i, i ^ step) for i in range(spaces)])]
    ppermute x2, waiting for transfers between devices: 2.8 us -> 3.13 us  [local(): lax.ppermute(gram, 'space', [(i, i ^ step) for i in range(spaces)])]
  transfers between devices with their start and end apart: 11 -> 11, of which waited for: 5 -> 5; matrix products, arithmetic and copies ran while one was open for 0% -> 0% of each run, Pallas kernels for 18% -> 17%
where the time goes in v7:
time: 27.1 us; the launch traced here: 26.9 us
  starting transfers between devices  11.7 us (43%)
  waiting for transfers between devices  7.09 us (26%)
  Pallas kernels  5.54 us (20%)
  local copies, waits for them, and re-layouts  1.21 us (4%)
  between operations  0.73 us (3%)
  other arithmetic  0.65 us (2%)
    pallas_call x10, Pallas kernels, run(): pl.pallas_call(kernel, name=name, out_shape=out_shape, in_specs=[VMEM] *...  5.54 us
    ppermute x2, starting transfers between devices, local(): lax.ppermute(gram, 'space', [(i, i ^ step) for i in range(spaces)])  4.27 us
    ppermute x2, waiting for transfers between devices, local(): lax.ppermute(gram, 'space', [(i, i ^ step) for i in range(spaces)])  3.13 us
    ppermute x1, starting transfers between devices, local(): lax.ppermute(piece, 'snap', [(i, (i + 2 * k) % cores) for i in range(core...  3 us
    ppermute x1, waiting for transfers between devices, local(): lax.ppermute(piece, 'snap', [(i, (i + 2 * k) % cores) for i in range(core...  2.55 us
    ppermute x1, starting transfers between devices, local(): lax.ppermute(back[k - 1], 'snap', [(i, (i - 2 * k) % cores) for i in rang...  1.81 us
    ppermute x2, starting transfers between devices, swap(): return lax.ppermute(array, ('space', 'snap'), pairs)  1.6 us
    unnamed x6, local copies, waits for them, and re-layouts  1.21 us
  transfers between devices with their start and end apart: 11, of which 5 were waited for; matrix products, arithmetic and copies ran while one was open for 0% of the time, Pallas kernels for 17%

profile of v7, /device:TPU:0, one launch (start us, length us, event | category | flops | bytes accessed | tf_op | source)
XLA Modules:
  0.0 26.9 jit_solution(7512515222091789953)
XLA Ops:
  0.6 0.0 copy-start
  0.6 1.1 %copy-done = bf16[4,3,8,24,128]{4,3,2,1,0:T(8,128)(2,1)S(1)} copy-done((bf16[4,3,8,24,128]{4,3,2,1,0:T(8,128)(2,1)S(1)}, bf16[4,3,8,24,128]{4,3,2,1,0:T(8,128)(2,1)}, u32[]{:S(2)}) %copy-start) | copy-done | bytes 589848
  1.7 0.2 piece.1
  1.8 3.0 %collective-permute-start.6 = (bf16[4,3,5,24,128]{4,3,2,1,0:T(8,128)(2,1)S(1)}, bf16[4,3,5,24,128]{4,3,2,1,0:T(8,128)(2,1)S(1)}, u32[]{:S(2)}, u32[]{:S(2)}) collective-permute-start(bf16[4,3,5,24,128]{4,3,2,1,0:T(8,128)(2,1)S(1)} %get-tuple-element.38), channel_id=1, source_target_pairs={{0,2},{1,3},{2,0},{3,1},{4,6},{5,7},{6,4},{7,5},{8,10},{9,11},{10,... | collective-permute-start | bytes 1105928 | tf_op jit(solution)/shard_map/ppermute | solution.py:411
  4.9 0.0 copy-start.1
  4.9 0.0 collective-permute-start
  4.9 0.5 %collective-permute-start.3 = (bf16[4,8,24,128]{3,2,1,0:T(8,128)(2,1)S(1)}, bf16[4,8,24,128]{3,2,1,0:T(8,128)(2,1)S(1)}, u32[]{:S(2)}, u32[]{:S(2)}) collective-permute-start(bf16[4,8,24,128]{3,2,1,0:T(8,128)(2,1)S(1)} %get-tuple-element.30.refs_0_), channel_id=1, source_target_pairs={{0,1},{1,0},{2,3},{3,2},{4,5},{5,4},{6,7},{7,6},{8,9},{9,8},{10,11... | collective-permute-start | bytes 589832 | tf_op jit(solution)/shard_map/ppermute | solution.py:399
  5.4 0.0 collective-permute-start.4
  5.4 0.0 copy-start.2
  5.4 0.5 %collective-permute-start.5 = (bf16[4,8,24,128]{3,2,1,0:T(8,128)(2,1)S(1)}, bf16[4,8,24,128]{3,2,1,0:T(8,128)(2,1)S(1)}, u32[]{:S(2)}, u32[]{:S(2)}) collective-permute-start(bf16[4,8,24,128]{3,2,1,0:T(8,128)(2,1)S(1)} %get-tuple-element.32.refs_2_), channel_id=1, source_target_pairs={{0,1},{1,0},{2,3},{3,2},{4,5},{5,4},{6,7},{7,6},{8,9},{9,8},{10,11... | collective-permute-start | bytes 589832 | tf_op jit(solution)/shard_map/ppermute | solution.py:399
  5.9 0.0 copy-done.1
  5.9 0.1 copy-done.2
  6.0 0.3 %collective-permute-done.mate_ref = bf16[2,49,8,128]{3,2,1,0:T(8,128)(2,1)S(1)} collective-permute-done((bf16[2,49,8,128]{3,2,1,0:T(8,128)(2,1)S(1)}, bf16[2,49,8,128]{3,2,1,0:T(8,128)(2,1)S(1)}, u32[]{:S(2)}, u32[]{:S(2)}) %collective-permute-start) | collective-permute-done | bytes 200736 | tf_op jit(solution)/shard_map/ppermute | solution.py:399
  6.3 0.1 pack.1
  6.4 1.6 %collective-permute-start.1 = (bf16[37,8,128]{2,1,0:T(8,128)(2,1)S(1)}, bf16[37,8,128]{2,1,0:T(8,128)(2,1)S(1)}, u32[]{:S(2)}, u32[]{:S(2)}) collective-permute-start(bf16[37,8,128]{2,1,0:T(8,128)(2,1)S(1)} %get-tuple-element.28), channel_id=1, source_target_pairs={{0,4},{1,5},{2,6},{3,7},{4,0},{5,1},{6,2},{7,3},{8,12},{9,13},{10,... | collective-permute-start | bytes 227336 | tf_op jit(solution)/shard_map/ppermute | solution.py:445
  8.0 0.0 collective-permute-done.3.refs_3_.refs_0_
  8.0 0.0 collective-permute-start.2
  8.0 0.2 metric.1
  8.2 0.0 collective-permute-done.4.refs_4_.refs_1_
  8.2 0.0 collective-permute-done.5.refs_5_.refs_2_
  8.2 1.5 %inner.2 = (f32[4,3,5,24,128]{4,3,2,1,0:T(8,128)S(1)}, f32[4,3,5,24,128]{4,3,2,1,0:T(8,128)S(1)}, f32[4,24,128]{2,1,0:T(8,128)S(1)}) custom-call(bf16[4,8,24,128]{3,2,1,0:T(8,128)(2,1)S(1)} %get-tuple-element.30.refs_0_, bf16[4,8,24,128]{3,2,1,0:T(8,128)(2,1)S(1)} %get-tuple-element.31.refs_1_, bf16[4,8,24,128]{3,2,1,0:T(8,128)(2,1)S(1)} %get-tuple-element.32.refs_2_, ...), custom_call_target="tpu_custom_call" | custom-call | tf_op jit(solution)/shard_map/inner/pallas_call | solution.py:20
  9.8 1.1 %collective-permute-done.1 = bf16[37,8,128]{2,1,0:T(8,128)(2,1)S(1)} collective-permute-done((bf16[37,8,128]{2,1,0:T(8,128)(2,1)S(1)}, bf16[37,8,128]{2,1,0:T(8,128)(2,1)S(1)}, u32[]{:S(2)}, u32[]{:S(2)}) %collective-permute-start.1) | collective-permute-done | bytes 75808 | tf_op jit(solution)/shard_map/ppermute | solution.py:445
  10.9 0.0 collective-permute-done.2
  10.9 2.6 %collective-permute-done.6.got_ref = bf16[4,3,5,24,128]{4,3,2,1,0:T(8,128)(2,1)S(1)} collective-permute-done((bf16[4,3,5,24,128]{4,3,2,1,0:T(8,128)(2,1)S(1)}, bf16[4,3,5,24,128]{4,3,2,1,0:T(8,128)(2,1)S(1)}, u32[]{:S(2)}, u32[]{:S(2)}) %collective-permute-start.6) | collective-permute-done | bytes 368672 | tf_op jit(solution)/shard_map/ppermute | solution.py:411
  13.5 0.8 %cross.1 = (f32[8,128]{1,0:T(8,128)S(1)}, f32[8,128]{1,0:T(8,128)S(1)}, f32[8,128]{1,0:T(8,128)S(1)}) custom-call(f32[16,128]{1,0:T(8,128)S(1)} %convert_add_fusion.table_ref, f32[4,3,5,24,128]{4,3,2,1,0:T(8,128)S(1)} %get-tuple-element.39.part_ref, f32[4,3,5,24,128]{4,3,2,1,0:T(8,128)S(1)} %get-tuple-element.40.mate_part_ref, ...), custom_call_target="tpu_custom_call" | custom-call | tf_op jit(solution)/shard_map/cross/pallas_call | solution.py:20
  14.3 0.0 collective-permute-start.8
  14.3 1.8 %collective-permute-start.7 = (f32[8,128]{1,0:T(8,128)S(1)}, f32[8,128]{1,0:T(8,128)S(1)}, u32[]{:S(2)}, u32[]{:S(2)}) collective-permute-start(f32[8,128]{1,0:T(8,128)S(1)} %get-tuple-element.47), channel_id=1, source_target_pairs={{0,2},{1,3},{2,0},{3,1},{4,6},{5,7},{6,4},{7,5},{8,10},{9,11},{10,... | collective-permute-start | bytes 12296 | tf_op jit(solution)/shard_map/ppermute | solution.py:478
  16.1 0.8 %inner.3 = (f32[4,3,5,24,128]{4,3,2,1,0:T(8,128)S(1)}, f32[4,24,128]{2,1,0:T(8,128)S(1)}) custom-call(bf16[4,8,24,128]{3,2,1,0:T(8,128)(2,1)S(1)} %get-tuple-element.30.refs_0_, bf16[4,8,24,128]{3,2,1,0:T(8,128)(2,1)S(1)} %get-tuple-element.31.refs_1_, bf16[4,8,24,128]{3,2,1,0:T(8,128)(2,1)S(1)} %get-tuple-element.32.refs_2_, ...), custom_call_target="tpu_custom_call" | custom-call | tf_op jit(solution)/shard_map/inner/pallas_call | solution.py:20
  16.9 0.4 %edges.1 = (bf16[4,3,8,24,128]{4,3,2,1,0:T(8,128)(2,1)S(1)}, f32[4,2,8,128]{3,2,1,0:T(8,128)S(1)}) custom-call(f32[16,128]{1,0:T(8,128)S(1)} %convert_add_fusion.table_ref, f32[4,3,5,24,128]{4,3,2,1,0:T(8,128)S(1)} %get-tuple-element.39.part_ref, f32[4,3,5,24,128]{4,3,2,1,0:T(8,128)S(1)} %get-tuple-element.45.other_ref, ...), custom_call_target="tpu_custom_call" | custom-call | tf_op jit(solution)/shard_map/edges/pallas_call | solution.py:20
  17.3 0.4 %square.1 = f32[8,128]{1,0:T(8,128)S(1)} custom-call(bf16[4,8,24,128]{3,2,1,0:T(8,128)(2,1)S(1)} %get-tuple-element.30.refs_0_, bf16[4,8,24,128]{3,2,1,0:T(8,128)(2,1)S(1)} %get-tuple-element.31.refs_1_, bf16[4,8,24,128]{3,2,1,0:T(8,128)(2,1)S(1)} %get-tuple-element.32.refs_2_, bf16[4,3,8,24,128]{4,3,2,1,0:T(8,128)(2,1)S(1)} %get-tuple-element.46.refs_3_), custom_call_target="tpu_custom_call" | custom-call | tf_op jit(solution)/shard_map/square/pallas_call | solution.py:20
  17.7 0.5 %mates.1 = f32[8,128]{1,0:T(8,128)S(1)} custom-call(bf16[4,8,24,128]{3,2,1,0:T(8,128)(2,1)S(1)} %collective-permute-done.3.refs_3_.refs_0_, bf16[4,8,24,128]{3,2,1,0:T(8,128)(2,1)S(1)} %collective-permute-done.4.refs_4_.refs_1_, bf16[4,8,24,128]{3,2,1,0:T(8,128)(2,1)S(1)} %collective-permute-done.5.refs_5_.refs_2_, ...), custom_call_target="tpu_custom_call" | custom-call | tf_op jit(solution)/shard_map/mates/pallas_call | solution.py:20
  18.1 0.0 collective-permute-done.8
  18.1 0.0 collective-permute-done.7
  18.2 2.7 %collective-permute-start.9 = (f32[8,128]{1,0:T(8,128)S(1)}, f32[8,128]{1,0:T(8,128)S(1)}, u32[]{:S(2)}, u32[]{:S(2)}) collective-permute-start(f32[8,128]{1,0:T(8,128)S(1)} %add_add_fusion), channel_id=1, source_target_pairs={{0,8},{4,12},{8,0},{12,4},{1,9},{5,13},{9,1},{13,5},{2,10},{6,14},... | collective-permute-start | bytes 12296 | tf_op jit(solution)/shard_map/ppermute | solution.py:486
  20.8 1.9 %collective-permute-done.9 = f32[8,128]{1,0:T(8,128)S(1)} collective-permute-done((f32[8,128]{1,0:T(8,128)S(1)}, f32[8,128]{1,0:T(8,128)S(1)}, u32[]{:S(2)}, u32[]{:S(2)}) %collective-permute-start.9) | collective-permute-done | bytes 4128 | tf_op jit(solution)/shard_map/ppermute | solution.py:486
  22.7 1.6 %collective-permute-start.10 = (f32[8,128]{1,0:T(8,128)S(1)}, f32[8,128]{1,0:T(8,128)S(1)}, u32[]{:S(2)}, u32[]{:S(2)}) collective-permute-start(f32[8,128]{1,0:T(8,128)S(1)} %add.35), channel_id=1, source_target_pairs={{0,4},{4,0},{8,12},{12,8},{1,5},{5,1},{9,13},{13,9},{2,6},{6,2},{1... | collective-permute-start | bytes 12296 | tf_op jit(solution)/shard_map/ppermute | solution.py:486
  24.3 0.8 %profile.1 = f32[4,24]{1,0:T(4,128)} custom-call(f32[4,24,128]{2,1,0:T(8,128)S(1)} %get-tuple-element.49.energy_ref, f32[4,24,128]{2,1,0:T(8,128)S(1)} %get-tuple-element.50.other_ref, f32[4,2,8,128]{3,2,1,0:T(8,128)S(1)} %get-tuple-element.51.gain_ref), custom_call_target="tpu_custom_call" | custom-call | tf_op jit(solution)/shard_map/profile/pallas_call | solution.py:20
  25.1 1.2 %collective-permute-done.10 = f32[8,128]{1,0:T(8,128)S(1)} collective-permute-done((f32[8,128]{1,0:T(8,128)S(1)}, f32[8,128]{1,0:T(8,128)S(1)}, u32[]{:S(2)}, u32[]{:S(2)}) %collective-permute-start.10) | collective-permute-done | bytes 4128 | tf_op jit(solution)/shard_map/ppermute | solution.py:486
  26.3 0.6 %slice_multiply_fusion = f32[4,16]{1,0:T(4,128)} fusion(f32[8,128]{1,0:T(8,128)S(1)} %add.36), kind=kLoop, calls=%fused_computation.4 | loop fusion | flops 64 | bytes 512 | tf_op jit(solution)/shard_map/mul | solution.py:488
  (5 shorter events, 0.1 us)
Async XLA Ops:
  0.6 1.1 %copy-start = (bf16[4,3,8,24,128]{4,3,2,1,0:T(8,128)(2,1)S(1)}, bf16[4,3,8,24,128]{4,3,2,1,0:T(8,128)(2,1)}, u32[]{:S(2)}) copy-start(bf16[4,3,8,24,128]{4,3,2,1,0:T(8,128)(2,1)} %u_ref.1) | copy-start | bytes 1769476
  1.8 11.6 %collective-permute-start.6 = (bf16[4,3,5,24,128]{4,3,2,1,0:T(8,128)(2,1)S(1)}, bf16[4,3,5,24,128]{4,3,2,1,0:T(8,128)(2,1)S(1)}, u32[]{:S(2)}, u32[]{:S(2)}) collective-permute-start(bf16[4,3,5,24,128]{4,3,2,1,0:T(8,128)(2,1)S(1)} %get-tuple-element.38), channel_id=1, source_target_pairs={{0,2},{1,3},{2,0},{3,1},{4,6},{5,7},{6,4},{7,5},{8,10},{9,11},{10,... | collective-permute-start | bytes 1105928 | tf_op jit(solution)/shard_map/ppermute | solution.py:411
  4.9 1.0 %copy-start.1 = (f32[8,128]{1,0:T(8,128)S(1)}, f32[8,128]{1,0:T(8,128)}, u32[]{:S(2)}) copy-start(f32[8,128]{1,0:T(8,128)} %param.5) | copy-start | bytes 12292
  4.9 1.4 %collective-permute-start = (bf16[2,49,8,128]{3,2,1,0:T(8,128)(2,1)S(1)}, bf16[2,49,8,128]{3,2,1,0:T(8,128)(2,1)S(1)}, u32[]{:S(2)}, u32[]{:S(2)}) collective-permute-start(bf16[2,49,8,128]{3,2,1,0:T(8,128)(2,1)S(1)} %get-tuple-element.27.own_ref), channel_id=1, source_target_pairs={{0,1},{1,0},{2,3},{3,2},{4,5},{5,4},{6,7},{7,6},{8,9},{9,8},{10,11... | collective-permute-start | bytes 602120 | tf_op jit(solution)/shard_map/ppermute | solution.py:399
  4.9 3.1 %collective-permute-start.3 = (bf16[4,8,24,128]{3,2,1,0:T(8,128)(2,1)S(1)}, bf16[4,8,24,128]{3,2,1,0:T(8,128)(2,1)S(1)}, u32[]{:S(2)}, u32[]{:S(2)}) collective-permute-start(bf16[4,8,24,128]{3,2,1,0:T(8,128)(2,1)S(1)} %get-tuple-element.30.refs_0_), channel_id=1, source_target_pairs={{0,1},{1,0},{2,3},{3,2},{4,5},{5,4},{6,7},{7,6},{8,9},{9,8},{10,11... | collective-permute-start | bytes 589832 | tf_op jit(solution)/shard_map/ppermute | solution.py:399
  5.4 2.9 %collective-permute-start.4 = (bf16[4,8,24,128]{3,2,1,0:T(8,128)(2,1)S(1)}, bf16[4,8,24,128]{3,2,1,0:T(8,128)(2,1)S(1)}, u32[]{:S(2)}, u32[]{:S(2)}) collective-permute-start(bf16[4,8,24,128]{3,2,1,0:T(8,128)(2,1)S(1)} %get-tuple-element.31.refs_1_), channel_id=1, source_target_pairs={{0,1},{1,0},{2,3},{3,2},{4,5},{5,4},{6,7},{7,6},{8,9},{9,8},{10,11... | collective-permute-start | bytes 589832 | tf_op jit(solution)/shard_map/ppermute | solution.py:399
  5.4 0.7 %copy-start.2 = (s32[24]{0:T(128)S(1)}, s32[24]{0:T(128)}, u32[]{:S(2)}) copy-start(s32[24]{0:T(128)} %param.4) | copy-start | bytes 292
  5.4 2.9 %collective-permute-start.5 = (bf16[4,8,24,128]{3,2,1,0:T(8,128)(2,1)S(1)}, bf16[4,8,24,128]{3,2,1,0:T(8,128)(2,1)S(1)}, u32[]{:S(2)}, u32[]{:S(2)}) collective-permute-start(bf16[4,8,24,128]{3,2,1,0:T(8,128)(2,1)S(1)} %get-tuple-element.32.refs_2_), channel_id=1, source_target_pairs={{0,1},{1,0},{2,3},{3,2},{4,5},{5,4},{6,7},{7,6},{8,9},{9,8},{10,11... | collective-permute-start | bytes 589832 | tf_op jit(solution)/shard_map/ppermute | solution.py:399
  6.4 4.5 %collective-permute-start.1 = (bf16[37,8,128]{2,1,0:T(8,128)(2,1)S(1)}, bf16[37,8,128]{2,1,0:T(8,128)(2,1)S(1)}, u32[]{:S(2)}, u32[]{:S(2)}) collective-permute-start(bf16[37,8,128]{2,1,0:T(8,128)(2,1)S(1)} %get-tuple-element.28), channel_id=1, source_target_pairs={{0,4},{1,5},{2,6},{3,7},{4,0},{5,1},{6,2},{7,3},{8,12},{9,13},{10,... | collective-permute-start | bytes 227336 | tf_op jit(solution)/shard_map/ppermute | solution.py:445
  8.0 2.9 %collective-permute-start.2 = (bf16[37,8,128]{2,1,0:T(8,128)(2,1)S(1)}, bf16[37,8,128]{2,1,0:T(8,128)(2,1)S(1)}, u32[]{:S(2)}, u32[]{:S(2)}) collective-permute-start(bf16[37,8,128]{2,1,0:T(8,128)(2,1)S(1)} %get-tuple-element.29), channel_id=1, source_target_pairs={{0,1},{1,0},{2,3},{3,2},{4,8},{5,9},{6,10},{7,11},{8,4},{9,5},{10,... | collective-permute-start | bytes 227336 | tf_op jit(solution)/shard_map/ppermute | solution.py:445
  14.3 3.8 %collective-permute-start.8 = (f32[8,128]{1,0:T(8,128)S(1)}, f32[8,128]{1,0:T(8,128)S(1)}, u32[]{:S(2)}, u32[]{:S(2)}) collective-permute-start(f32[8,128]{1,0:T(8,128)S(1)} %get-tuple-element.48), channel_id=1, source_target_pairs={{0,1},{1,0},{2,3},{3,2},{4,5},{5,4},{6,7},{7,6},{8,9},{9,8},{10,11... | collective-permute-start | bytes 12296 | tf_op jit(solution)/shard_map/ppermute | solution.py:399
  14.3 3.8 %collective-permute-start.7 = (f32[8,128]{1,0:T(8,128)S(1)}, f32[8,128]{1,0:T(8,128)S(1)}, u32[]{:S(2)}, u32[]{:S(2)}) collective-permute-start(f32[8,128]{1,0:T(8,128)S(1)} %get-tuple-element.47), channel_id=1, source_target_pairs={{0,2},{1,3},{2,0},{3,1},{4,6},{5,7},{6,4},{7,5},{8,10},{9,11},{10,... | collective-permute-start | bytes 12296 | tf_op jit(solution)/shard_map/ppermute | solution.py:478
  18.2 4.6 %collective-permute-start.9 = (f32[8,128]{1,0:T(8,128)S(1)}, f32[8,128]{1,0:T(8,128)S(1)}, u32[]{:S(2)}, u32[]{:S(2)}) collective-permute-start(f32[8,128]{1,0:T(8,128)S(1)} %add_add_fusion), channel_id=1, source_target_pairs={{0,8},{4,12},{8,0},{12,4},{1,9},{5,13},{9,1},{13,5},{2,10},{6,14},... | collective-permute-start | bytes 12296 | tf_op jit(solution)/shard_map/ppermute | solution.py:486
  22.7 3.6 %collective-permute-start.10 = (f32[8,128]{1,0:T(8,128)S(1)}, f32[8,128]{1,0:T(8,128)S(1)}, u32[]{:S(2)}, u32[]{:S(2)}) collective-permute-start(f32[8,128]{1,0:T(8,128)S(1)} %add.35), channel_id=1, source_target_pairs={{0,4},{4,0},{8,12},{12,8},{1,5},{5,1},{9,13},{13,9},{2,6},{6,2},{1... | collective-permute-start | bytes 12296 | tf_op jit(solution)/shard_map/ppermute | solution.py:486
